TPU v7x, 256 devices: a whole 4x4x8 slice. The times are simulated.
256 devices in a mesh: dp: 16 (over x, z_lo), mp: 16 (over z_hi, y, core).
Axes of the slice: x: 4, y: 4, z: 8 (z_hi: 2, z_lo: 4; z = z_hi * 4 + z_lo), core: 2. Of those that a mesh axis runs over, the one named last changes fastest.
Arguments:
- acts: bfloat16 [2, 16384, 8192], P(None, 'dp', 'mp'), may hold values from -6 to 6
- out_grads: bfloat16 [2, 16384, 28672], P(None, 'dp', 'mp'), may hold values from -6 to 6
- token_ids: int32 [64, 256], P('dp'), may hold values from 0 to 128255
- lengths: int32 [64], P('dp'), may hold values from 64 to 256, as said below
- token_weight: float32 [128256], replicated, may hold values from 0.25 to 4
- proj_in: bfloat16 [2, 8192, 64], P(None, 'mp'), may hold values from -0.0625 to 0.0625
- proj_out: bfloat16 [2, 28672, 64], P(None, 'mp'), may hold values from -0.03125 to 0.03125
- hess_inv: float32 [2, 4096, 4096], P(None, 'mp', 'dp'), as said below
- queries: bfloat16 [2, 4096, 4096], P(None, 'dp', 'mp'), may hold values from -0.0078125 to 0.0078125
Outputs:
- scores: float32 [64, 4096], P('dp', 'mp')
Inputs may be any that keep to these rules, and one draw needn't show every extreme that they name: `lengths`: some example uses all 256 slots. `hess_inv`: each layer's matrix is symmetric.
All inputs are finite; a program needn't handle non-finite values.
Results may differ from a plain program's by a relative error of at most 0.0003.
Values may be sent and summed in bfloat16 or wider, within the bound.
No kernel may reach another device: no remote copies, remote signals or barrier semaphores. Data moves between devices by JAX's collectives and lax.ppermute only.
A program may use at most 128 MiB of HBM per device.

v0:
```python
import jax
import jax.numpy as jnp
from jax import lax
from jax.sharding import PartitionSpec as P


def per_device(
    acts, out_grads, token_ids, lengths, token_weight, proj_in, proj_out, hess_inv, queries
):
    layers = acts.shape[0]
    tokens_here = acts.shape[1]
    rank_dim = proj_in.shape[2]
    groups = lax.axis_size("mp")
    narrow = rank_dim // groups
    examples = token_ids.shape[0]
    seq_len = token_ids.shape[1]
    highest = lax.Precision.HIGHEST
    x_proj = jnp.einsum("ltd,ldk->tlk", acts, proj_in, preferred_element_type=jnp.float32).reshape(
        tokens_here, layers * rank_dim
    )
    g_proj = jnp.einsum(
        "ltd,ldk->tlk", out_grads, proj_out, preferred_element_type=jnp.float32
    ).reshape(tokens_here, layers * rank_dim)
    x_all, g_all = lax.psum((x_proj, g_proj), "mp")
    x_block = lax.dynamic_slice_in_dim(
        x_all.reshape(tokens_here, layers, rank_dim), lax.axis_index("mp") * narrow, narrow, 2
    )
    positions = lax.broadcasted_iota(jnp.int32, (examples, seq_len), 1)
    weights = token_weight[token_ids] * (positions < lengths[:, None]).astype(jnp.float32)
    weighted = x_block.reshape(examples, seq_len, layers, narrow) * weights[:, :, None, None]
    grams = jnp.einsum(
        "eslk,eslj->lekj",
        weighted,
        g_all.reshape(examples, seq_len, layers, rank_dim),
        precision=highest,
    )
    grams = grams.reshape(layers, examples, narrow * rank_dim)
    image_part = jnp.einsum(
        "ler,lrf->lef", grams, lax.all_gather(hess_inv, "dp", axis=2, tiled=True), precision=highest
    )
    image = lax.psum_scatter(image_part, "mp", scatter_dimension=2, tiled=True)
    partial_scores = jnp.einsum(
        "lef,ljf->ej",
        image,
        lax.all_gather(queries, "dp", axis=1, tiled=True).astype(jnp.float32),
        precision=highest,
    )
    return lax.psum_scatter(partial_scores, "mp", scatter_dimension=1, tiled=True)


def solution(mesh):
    in_specs = (
        P(None, "dp", "mp"),
        P(None, "dp", "mp"),
        P("dp", None),
        P("dp"),
        P(),
        P(None, "mp", None),
        P(None, "mp", None),
        P(None, "mp", "dp"),
        P(None, "dp", "mp"),
    )
    out_specs = P("dp", "mp")
    return jax.shard_map(
        per_device, mesh=mesh, in_specs=in_specs, out_specs=out_specs, check_vma=False
    )
```

profile of v0, /device:TPU:1, one launch (start us, length us, event | category | flops | bytes accessed | tf_op | source)
XLA Modules:
  0.0 550.4 jit_solution(18163970646675823506)
XLA Ops:
  7.4 0.0 all-reduce.3.cloned.1.call-start
  7.4 5.7 %fusion.6 = f32[2,64,1024]{2,1,0:T(8,128)S(1)} fusion(bf16[2,1792,64]{1,2,0:T(8,128)(2,1)} %param.15, bf16[2,1024,1792]{2,1,0:T(8,128)(2,1)} %param.10), kind=kOutput, calls=%fused_computation.14 | convolution fusion | flops 469762048 | bytes 8323072 | tf_op jit(solution)/shard_map/ltd,ldk->tlk/dot_general | solution.py:21
  13.1 0.0 copy-start.3
  13.1 0.0 copy-start.1
  13.1 0.9 copy.22
  13.9 1.6 convolution_bitcast_fusion.1
  15.5 0.0 all-reduce.3.cloned.1.call-update
  15.5 0.0 all-gather.3.cloned.1.call-start
  15.6 0.5 all-gather.3.cloned.1.call-update
  16.1 0.0 reduce-scatter.7.cloned.1.call-start
  16.2 0.0 copy-done.1
  16.2 6.2 %gather_fusion = f32[1024]{0:T(1024)S(1)} fusion(f32[128256]{0:T(1024)S(1)} %copy-done.1, s32[1024]{0:T(1024)S(1)} %broadcast_clamp_fusion), kind=kCustom, calls=%fused_computation | custom fusion | bytes 12288 | tf_op jit(solution)/shard_map/gather | solution.py:29
  22.4 0.0 copy-done.4
  22.4 0.1 fusion.5
  22.5 289.9 %all-reduce.3.cloned.1.call-done = (f32[4,256,2,64]{1,3,0,2:T(8,128)}, f32[1024,2,64]{0,2,1:T(8,128)}) async-done(((f32[4,256,2,64]{1,3,0,2:T(8,128)}, f32[1024,2,64]{0,2,1:T(8,128)}), (f32[4,256,2,64]{1,3,0,2:T(8,128)}, f32[1024,2,64]{0,2,1:T(8,128)})) %all-reduce.3.cloned.1.call-update) | async-done | bytes 1048592 | tf_op jit(solution)/shard_map/psum | solution.py:24
  312.3 0.8 constant_dynamic-slice_fusion
  313.2 1.6 fusion.1
  314.7 0.1 reshape.45
  314.8 7.4 %fusion.7 = f32[2,4,4096]{2,1,0:T(4,128)S(1)} fusion(f32[2,4,256]{2,1,0:T(4,128)S(1)} %reshape.45, f32[2,256,4096]{2,1,0:T(8,128)} %all-gather.3.cloned.1.call-done), kind=kOutput, calls=%fused_computation.15 | convolution fusion | flops 100663296 | bytes 8527872 | tf_op jit(solution)/shard_map/ler,lrf->lef/dot_general | solution.py:38
  322.2 4.3 copy.13
  326.6 5.4 reshape.59
  332.0 0.0 reduce-scatter.7.cloned.1.call-update
  332.0 0.0 all-gather.5.cloned.1.call-start
  332.0 0.5 all-gather.5.cloned.1.call-update
  332.6 0.2 reduce-scatter.9.cloned.1.call-start
  332.8 92.4 %reduce-scatter.7.cloned.1.call-done = f32[256,8]{1,0:T(8,128)} async-done(((f32[4096,8]{1,0:T(8,128)}), f32[256,8]{1,0:T(8,128)}) %reduce-scatter.7.cloned.1.call-update) | async-done | bytes 8208
  425.2 1.1 reshape.60
  426.3 24.6 %all-gather.5.cloned.1.call-done = bf16[2,4096,256]{2,1,0:T(8,128)(2,1)} async-done(((bf16[2,256,256]{2,1,0:T(8,128)(2,1)}), bf16[2,4096,256]{2,1,0:T(8,128)(2,1)}) %all-gather.5.cloned.1.call-update) | async-done | bytes 4194320 | tf_op jit(solution)/shard_map/all_gather | solution.py:45
  450.9 7.0 %convolution_bitcast_fusion = f32[4096,4]{1,0:T(8,128)} fusion(bf16[2,4096,256]{2,1,0:T(8,128)(2,1)} %all-gather.5.cloned.1.call-done, f32[2,4,256]{1,0,2:T(2,128)S(1)} %bitcast.30), kind=kOutput, calls=%fused_computation.1 | convolution fusion | flops 100663296 | bytes 4268032 | tf_op jit(solution)/shard_map/lef,ljf->ej/dot_general | solution.py:42
  457.9 0.0 reduce-scatter.9.cloned.1.call-update
  457.9 83.8 %reduce-scatter.9.cloned.1.call-done = f32[256,4]{1,0:T(8,128)} async-done(((f32[4096,4]{1,0:T(8,128)}), f32[256,4]{1,0:T(8,128)}) %reduce-scatter.9.cloned.1.call-update) | async-done | bytes 4112
  541.7 1.6 copy.16
  (11 shorter events, 0.0 us)
Async XLA Ops:
  7.4 6.6 %copy-start = (bf16[2,1024,512]{2,1,0:T(8,128)(2,1)S(1)}, bf16[2,1024,512]{2,1,0:T(8,128)(2,1)}, u32[]{:S(2)}) copy-start(bf16[2,1024,512]{2,1,0:T(8,128)(2,1)} %param.9) | copy-start | bytes 6291460
  7.4 304.9 %all-reduce.3.cloned.1.call-start = ((), (), s32[]{:S(2)}) async-start(), calls=%async_computation.6 | async-start | bytes 2097152 | tf_op jit(solution)/shard_map/psum | solution.py:24
  7.4 6.6 %copy-start.2 = (bf16[2,512,64]{1,2,0:T(8,128)(2,1)S(1)}, bf16[2,512,64]{1,2,0:T(8,128)(2,1)}, u32[]{:S(2)}) copy-start(bf16[2,512,64]{1,2,0:T(8,128)(2,1)} %param.14) | copy-start | bytes 393220
  13.1 3.1 copy-start.3
  13.1 3.1 copy-start.1
  13.9 8.4 %copy-start.4 = (s32[4]{0:T(128)S(1)}, s32[4]{0:T(128)}, u32[]{:S(2)}) copy-start(s32[4]{0:T(128)} %param.12) | copy-start | bytes 52
  15.5 299.3 %all-gather.3.cloned.1.call-start = ((), (), s32[]{:S(2)}) async-start(), calls=%async_computation.2 | async-start | bytes 8912896 | tf_op jit(solution)/shard_map/all_gather | solution.py:39
  16.1 409.1 %reduce-scatter.7.cloned.1.call-start = ((), (), s32[]{:S(2)}) async-start(), calls=%async_computation.4 | async-start | bytes 2228224
  332.0 118.9 %all-gather.5.cloned.1.call-start = ((), (), s32[]{:S(2)}) async-start(), calls=%async_computation.3 | async-start | bytes 4456448 | tf_op jit(solution)/shard_map/all_gather | solution.py:45
  332.6 209.2 %reduce-scatter.9.cloned.1.call-start = ((), (), s32[]{:S(2)}) async-start(), calls=%async_computation.5 | async-start | bytes 2228224
Sparse Core Ops, SparseCore 0:
  15.6 296.6 all-reduce.2
  332.1 93.0 reduce-scatter.6
  458.0 83.6 reduce-scatter.8
Sparse Core Ops, SparseCore 1:
  17.9 193.7 all-gather.2
  334.4 116.5 all-gather.4
where the time goes:
time: 551 us; the launch traced here: 550 us
  waiting for transfers between devices  492 us (89%)
  matrix products  23.2 us (4%)
  local copies, waits for them, and re-layouts  20.4 us (4%)
  between operations  14.7 us (3%)
    psum x1, waiting for transfers between devices, per_device(): x_all, g_all = lax.psum((x_proj, g_proj), 'mp')  290 us
    unnamed x7, waiting for transfers between devices  177 us
    all_gather x1, waiting for transfers between devices, per_device(): lax.all_gather(queries, 'dp', axis=1, tiled=True).astype(jnp.float32)  24.6 us
    unnamed x15, local copies, waits for them, and re-layouts  12.4 us
  transfers between devices with their start and end apart: 5, of which 4 were waited for; matrix products, arithmetic and copies ran while one was open for 2% of the time, Pallas kernels for 0%

commit v1 on v0

v1 whole, which is shorter than its diff:
```python
import functools
import jax
import jax.numpy as jnp
from jax import lax
from jax.experimental import pallas as pl
from jax.experimental.pallas import tpu as pltpu
from jax.sharding import PartitionSpec as P

AXES = ("dp", "mp")
VMEM = pl.BlockSpec(memory_space=pltpu.VMEM)
SMEM = pl.BlockSpec(memory_space=pltpu.SMEM)


def send(value, target):
    pairs = []
    for d in range(16):
        for m in range(16):
            td, tm = target(d, m)
            pairs.append((d * 16 + m, td * 16 + tm))
    return lax.ppermute(value, AXES, pairs)


def to_core(value):
    return send(value, lambda d, m: (d, m ^ 1))


def to_y(value, k):
    return send(value, lambda d, m: (d, m ^ (2 * k)))


def to_z(value):
    return send(value, lambda d, m: (d, m ^ 8))


def to_zl(value, k):
    return send(value, lambda d, m: (d ^ k, m))


def to_x(value, k):
    return send(value, lambda d, m: (d ^ (4 * k), m))


def project_kernel(layer_ref, acts_ref, grads_ref, in_ref, out_ref, res_ref):
    x = jnp.dot(acts_ref[0], in_ref[0], preferred_element_type=jnp.float32)
    g = jnp.dot(grads_ref[0], out_ref[0], preferred_element_type=jnp.float32)
    res_ref[...] = jnp.concatenate([x, g], axis=1)


def project(layer, acts, out_grads, proj_in, proj_out):
    tokens, width = acts.shape[1:]
    hidden = out_grads.shape[2]
    rank = proj_in.shape[2]
    block = 256
    return pl.pallas_call(
        project_kernel,
        grid_spec=pltpu.PrefetchScalarGridSpec(
            num_scalar_prefetch=1,
            grid=(tokens // block,),
            in_specs=[
                pl.BlockSpec((1, block, width), lambda t, l: (l[0], t, 0)),
                pl.BlockSpec((1, block, hidden), lambda t, l: (l[0], t, 0)),
                pl.BlockSpec((1, width, rank), lambda t, l: (l[0], 0, 0)),
                pl.BlockSpec((1, hidden, rank), lambda t, l: (l[0], 0, 0)),
            ],
            out_specs=pl.BlockSpec((block, 2 * rank), lambda t, l: (t, 0)),
        ),
        out_shape=jax.ShapeDtypeStruct((tokens, 2 * rank), jnp.float32),
        compiler_params=pltpu.CompilerParams(vmem_limit_bytes=32 * 2**20),
        cost_estimate=pl.CostEstimate(
            flops=2 * tokens * (width + hidden) * 256,
            bytes_accessed=tokens * (width + hidden) * 2,
            transcendentals=0,
        ),
    )(layer, acts, out_grads, proj_in, proj_out)


def call(kernel, out, *args, smem=1):
    return pl.pallas_call(
        kernel,
        in_specs=[SMEM] * smem + [VMEM] * (len(args) - smem),
        out_specs=[VMEM] * len(out),
        out_shape=[jax.ShapeDtypeStruct(s, jnp.float32) for s in out],
        compiler_params=pltpu.CompilerParams(vmem_limit_bytes=32 * 2**20),
    )(*args)


def split_kernel(place_ref, a_ref, b_ref, *outs):
    y = place_ref[1]
    rows = outs[0].shape[0]
    for k, out in enumerate(outs):
        at = pl.ds(pl.multiple_of((y ^ k) * rows, rows), rows)
        out[...] = a_ref[at] + b_ref[at]


def sum_kernel(place_ref, *refs):
    *ins, out = refs
    total = ins[0][...]
    for ref in ins[1:]:
        total = total + ref[...]
    out[...] = total


def gram_kernel(place_ref, a_ref, b_ref, w_ref, *refs):
    *outs, held = refs
    z, y = place_ref[0], place_ref[1]
    total = a_ref[...] + b_ref[...]
    x = total[:, :64] * w_ref[...]
    held[...] = lax.dot_general(
        x,
        total[:, 64:],
        (((0,), (0,)), ((), ())),
        precision=lax.Precision.HIGHEST,
        preferred_element_type=jnp.float32,
    )
    for k, out in enumerate(outs):
        out[...] = held[pl.ds(pl.multiple_of(z * 32 + (y ^ k) * 8, 8), 8)]


def image_kernel(place_ref, *refs):
    grams, hess = refs[:4], refs[4:8]
    out, held = refs[8:]
    y, c = place_ref[1], place_ref[2]
    for kz in range(4):
        for ky in range(4):
            held[:, pl.ds(4 * kz + (y ^ ky), 1), :] = grams[kz][ky][:, None, :]
    for block in range(2):
        at = (c ^ block) * 4
        rows = jnp.concatenate([held[at + i] for i in range(4)], axis=1)
        for k in range(4):
            part = jnp.dot(
                rows,
                hess[k][block],
                precision=lax.Precision.HIGHEST,
                preferred_element_type=jnp.float32,
            )
            cols = pl.ds(256 * k, 256)
            if block:
                out[:, cols] += part
            else:
                out[:, cols] = part


def score_kernel(place_ref, a_ref, b_ref, *refs):
    queries, outs = refs[:4], refs[4:]
    image = a_ref[...] + b_ref[...]
    high = image.astype(jnp.bfloat16)
    rest = image - high.astype(jnp.float32)
    mid = rest.astype(jnp.bfloat16)
    low = (rest - mid.astype(jnp.float32)).astype(jnp.bfloat16)
    rows = jnp.concatenate([high, mid, low], axis=0)
    count = image.shape[0]
    for block, out in enumerate(outs):
        total = 0.0
        for k in range(4):
            part = lax.dot_general(
                rows[:, 256 * k : 256 * (k + 1)],
                queries[k][block],
                (((1,), (1,)), ((), ())),
                preferred_element_type=jnp.float32,
            )
            total = total + (part[:count] + part[count : 2 * count] + part[2 * count :])
        out[...] = total


def per_device(
    acts, out_grads, token_ids, lengths, token_weight, proj_in, proj_out, hess_inv, queries
):
    m = lax.axis_index("mp")
    z, y, c = m >> 3, (m >> 1) & 3, m & 1
    place = jnp.stack([z, y, c]).astype(jnp.int32)
    f32 = jnp.float32

    other = project((1 - c)[None], acts, out_grads, proj_in, proj_out)
    theirs = to_core(other)
    mine = project(c[None], acts, out_grads, proj_in, proj_out)

    blocks = call(split_kernel, [(256, 128)] * 4, place, mine, theirs)
    got = [to_y(blocks[k], k) for k in (1, 2, 3)]

    hess_mine = lax.dynamic_index_in_dim(hess_inv, c, 0, keepdims=False)
    hess_theirs = to_core(lax.dynamic_index_in_dim(hess_inv, 1 - c, 0, keepdims=False))
    hess = jnp.stack([hess_mine, hess_theirs])
    hess = [hess] + [to_x(hess, k) for k in (1, 2, 3)]

    turned = send(queries, lambda d, m: (m, d))
    query_mine = lax.dynamic_index_in_dim(turned, c, 0, keepdims=False)
    query_theirs = to_core(lax.dynamic_index_in_dim(turned, 1 - c, 0, keepdims=False))
    query = jnp.stack([query_mine, query_theirs])
    query = [query] + [to_x(query, k) for k in (1, 2, 3)]

    ids = lax.dynamic_index_in_dim(token_ids, y, 0, keepdims=False)
    length = lax.dynamic_index_in_dim(lengths, y, 0, keepdims=False)
    live = (lax.iota(jnp.int32, ids.shape[0]) < length).astype(f32)
    weights = (token_weight[ids] * live)[:, None]

    (half,) = call(sum_kernel, [(256, 128)], place, blocks[0], *got)
    half_theirs = to_z(half)
    grams = pl.pallas_call(
        gram_kernel,
        in_specs=[SMEM] + [VMEM] * 3,
        out_specs=[VMEM] * 4,
        out_shape=[jax.ShapeDtypeStruct((8, 64), f32)] * 4,
        scratch_shapes=[pltpu.VMEM((64, 64), f32)],
    )(place, half, half_theirs, weights)
    rows = jnp.stack([grams[0]] + [to_y(grams[k], k) for k in (1, 2, 3)])
    rows = [rows] + [to_zl(rows, k) for k in (1, 2, 3)]

    image = pl.pallas_call(
        image_kernel,
        in_specs=[SMEM] + [VMEM] * 8,
        out_specs=VMEM,
        out_shape=jax.ShapeDtypeStruct((16, 1024), f32),
        scratch_shapes=[pltpu.VMEM((8, 16, 64), f32)],
        compiler_params=pltpu.CompilerParams(vmem_limit_bytes=32 * 2**20),
    )(place, *rows, *hess)
    got = [to_y(image, k) for k in (1, 2, 3)]
    (image,) = call(sum_kernel, [(16, 1024)], place, image, *got)
    image_theirs = to_z(image)
    keep, give = call(
        score_kernel, [(16, 256)] * 2, place, image, image_theirs, *query
    )
    scores = keep + to_core(give)
    result = scores[:4]
    for k in (1, 2, 3):
        result = result + to_zl(scores[4 * k : 4 * k + 4], k)
    return result


def solution(mesh):
    in_specs = (
        P(None, "dp", "mp"),
        P(None, "dp", "mp"),
        P("dp", None),
        P("dp"),
        P(),
        P(None, "mp", None),
        P(None, "mp", None),
        P(None, "mp", "dp"),
        P(None, "dp", "mp"),
    )
    out_specs = P("dp", "mp")
    return jax.shard_map(
        per_device, mesh=mesh, in_specs=in_specs, out_specs=out_specs, check_vma=False
    )
```

time: 551 us -> 118 us (0.21)
  waiting for transfers between devices: 492 us -> 22.1 us
  starting transfers between devices: 0.35 us -> 57.5 us
  matrix products: 23.2 us -> 0 us
  between operations: 14.7 us -> 0.16 us
  Pallas kernels: 0 us -> 11.8 us
    psum x1 -> x0, waiting for transfers between devices: 290 us -> none  [per_device(): x_all, g_all = lax.psum((x_proj, g_proj), 'mp')]
    unnamed x7 -> x0, waiting for transfers between devices: 177 us -> none
    ppermute x0 -> x28, starting transfers between devices: none -> 57.5 us  [send(): return lax.ppermute(value, AXES, pairs)]
    all_gather x2 -> x0, waiting for transfers between devices: 24.6 us -> none  [the longest x1 24.6 us: per_device(): lax.all_gather(queries, 'dp', axis=1, tiled=True).astype(jnp.float32)]
    dot_general x5 -> x0, matrix products: 23.2 us -> none  [the longest x1 7.42 us: per_device(): jnp.einsum('ler,lrf->lef', grams, lax.all_gather(hess_inv, 'dp', axis=2,...]
    ppermute x0 -> x28, waiting for transfers between devices: none -> 22.1 us  [send(): return lax.ppermute(value, AXES, pairs)]
    pallas_call x0 -> x8, Pallas kernels: none -> 11.8 us  [the longest x2 5.05 us: project(): pl.pallas_call(project_kernel, grid_spec=pltpu.PrefetchScalarGridSpec(num...]
    unnamed x15 -> x28, local copies, waits for them, and re-layouts: 12.4 us -> 14.2 us
  transfers between devices with their start and end apart: 5 -> 28, of which waited for: 4 -> 13; matrix products, arithmetic and copies ran while one was open for 2% -> 10% of each run, Pallas kernels for 0% -> 7%
where the time goes in v1:
time: 118 us
  starting transfers between devices  57.5 us (49%)
  waiting for transfers between devices  22.1 us (19%)
  local copies, waits for them, and re-layouts  20.8 us (18%)
  Pallas kernels  11.8 us (10%)
  other arithmetic  5.3 us (4%)
    ppermute x28, starting transfers between devices, send(): return lax.ppermute(value, AXES, pairs)  57.5 us
    ppermute x28, waiting for transfers between devices, send(): return lax.ppermute(value, AXES, pairs)  22.1 us
    unnamed x28, local copies, waits for them, and re-layouts  14.2 us
    pallas_call x2, Pallas kernels, project(): pl.pallas_call(project_kernel, grid_spec=pltpu.PrefetchScalarGridSpec(num...  5.05 us
    pallas_call x4, Pallas kernels, call(): pl.pallas_call(kernel, in_specs=[SMEM] * smem + [VMEM] * (len(args) - sme...  3.17 us
    gather x2, local copies, waits for them, and re-layouts, per_device(): weights = (token_weight[ids] * live)[:, None]  2.52 us
  transfers between devices with their start and end apart: 28, of which 13 were waited for; matrix products, arithmetic and copies ran while one was open for 10% of the time, Pallas kernels for 7%

profile of v1, /device:TPU:1, one launch (start us, length us, event | category | flops | bytes accessed | tf_op | source)
XLA Modules:
  0.0 117.7 jit_solution(8745471535554413767)
XLA Ops:
  0.0 1.8 %copy.14.in_ref = bf16[2,512,64]{2,1,0:T(8,128)(2,1)} copy(bf16[2,512,64]{1,2,0:T(8,128)(2,1)} %param.14) | data formatting | bytes 262144 | tf_op args[5]
  1.8 1.4 %copy.15.out_ref = bf16[2,1792,64]{2,1,0:T(8,128)(2,1)S(1)} copy(bf16[2,1792,64]{1,2,0:T(8,128)(2,1)} %param.15) | data formatting | bytes 917504 | tf_op args[6]
  3.3 3.1 %copy-done.1 = bf16[2,1024,1792]{2,1,0:T(8,128)(2,1)S(1)} copy-done((bf16[2,1024,1792]{2,1,0:T(8,128)(2,1)S(1)}, bf16[2,1024,1792]{2,1,0:T(8,128)(2,1)}, u32[]{:S(2)}) %copy-start.1) | copy-done | bytes 7340056
  6.4 1.6 %copy-done.3 = bf16[2,1024,512]{2,1,0:T(8,128)(2,1)S(1)} copy-done((bf16[2,1024,512]{2,1,0:T(8,128)(2,1)S(1)}, bf16[2,1024,512]{2,1,0:T(8,128)(2,1)}, u32[]{:S(2)}) %copy-start.3) | copy-done | bytes 2097176
  8.9 2.9 %shard_map.92 = f32[1024,128]{1,0:T(8,128)} custom-call(s32[1]{0:T(128)} %bitcast.3.layer_ref, bf16[2,1024,512]{2,1,0:T(8,128)(2,1)S(1)} %copy-done.3, bf16[2,1024,1792]{2,1,0:T(8,128)(2,1)S(1)} %copy-done.1, bf16[2,512,64]{2,1,0:T(8,128)(2,1)S(1)} %copy-done.5, bf16[2,1792,64]{2,1,0:T(8,128)(2,1)S(1)} %copy.15.out_ref), custom_call_target="tpu_custom_call" | custom-call | flops 1207959552 | bytes 4718592 | tf_op jit(solution)/shard_map/pallas_call | solution.py:54
  11.8 3.2 %collective-permute-start = (f32[1024,128]{1,0:T(8,128)}, f32[1024,128]{1,0:T(8,128)}, u32[]{:S(2)}, u32[]{:S(2)}) collective-permute-start(f32[1024,128]{1,0:T(8,128)} %shard_map.92), channel_id=1, source_target_pairs={{0,1},{1,0},{2,3},{3,2},{4,5},{5,4},{6,7},{7,6},{8,9},{9,8},{10,11... | collective-permute-start | bytes 1572872 | tf_op jit(solution)/shard_map/ppermute | solution.py:20
  15.1 1.9 %constant_dynamic-slice_fusion.1 = (f32[1,256,256]{2,1,0:T(8,128)}, f32[256,256]{1,0:T(8,128)}) fusion(f32[2,256,256]{2,1,0:T(8,128)} %param.16, s32[]{:T(128)S(6)} %select_n.28, s32[]{:T(128)S(6)} %select_n.29), kind=kLoop, calls=%fused_computation.14 | loop fusion | bytes 1048584 | tf_op jit(solution)/shard_map/jit(dynamic_index_in_dim)/dynamic_slice | solution.py:180
  16.9 2.2 %collective-permute-start.19 = (bf16[2,256,256]{2,1,0:T(8,128)(2,1)}, bf16[2,256,256]{2,1,0:T(8,128)(2,1)}, u32[]{:S(2)}, u32[]{:S(2)}) collective-permute-start(bf16[2,256,256]{2,1,0:T(8,128)(2,1)} %param.17), channel_id=1, source_target_pairs={{0,0},{1,16},{2,32},{3,48},{4,64},{5,80},{6,96},{7,112},{8,128},{9... | collective-permute-start | bytes 786440 | tf_op jit(solution)/shard_map/ppermute | solution.py:20
  19.2 3.1 %copy-done.2 = bf16[2,1024,1792]{2,1,0:T(8,128)(2,1)S(1)} copy-done((bf16[2,1024,1792]{2,1,0:T(8,128)(2,1)S(1)}, bf16[2,1024,1792]{2,1,0:T(8,128)(2,1)}, u32[]{:S(2)}) %copy-start.2) | copy-done | bytes 7340056
  23.3 2.1 %shard_map.91.a_ref = f32[1024,128]{1,0:T(8,128)S(1)} custom-call(s32[1]{0:T(128)} %bitcast.2.layer_ref, bf16[2,1024,512]{2,1,0:T(8,128)(2,1)S(1)} %copy-done.4, bf16[2,1024,1792]{2,1,0:T(8,128)(2,1)S(1)} %copy-done.2, bf16[2,512,64]{2,1,0:T(8,128)(2,1)S(1)} %copy-done.6, bf16[2,1792,64]{2,1,0:T(8,128)(2,1)S(1)} %copy.15.out_ref), custom_call_target="tpu_custom_call" | custom-call | flops 1207959552 | bytes 4718592 | tf_op jit(solution)/shard_map/pallas_call | solution.py:54
  26.4 3.9 %collective-permute-start.12 = (f32[2,256,256]{2,1,0:T(8,128)S(1)}, f32[2,256,256]{2,1,0:T(8,128)S(1)}, u32[]{:S(2)}, u32[]{:S(2)}) collective-permute-start(f32[2,256,256]{2,1,0:T(8,128)S(1)} %pad_maximum_fusion.refs_4_), channel_id=1, source_target_pairs={{0,64},{1,65},{2,66},{3,67},{4,68},{5,69},{6,70},{7,71},{8,72},{9,... | collective-permute-start | bytes 1572872 | tf_op jit(solution)/shard_map/ppermute | solution.py:20
  31.4 2.5 %collective-permute-start.1 = (f32[256,128]{1,0:T(8,128)S(1)}, f32[256,128]{1,0:T(8,128)S(1)}, u32[]{:S(2)}, u32[]{:S(2)}) collective-permute-start(f32[256,128]{1,0:T(8,128)S(1)} %get-tuple-element.16), channel_id=1, source_target_pairs={{0,2},{1,3},{2,0},{3,1},{4,6},{5,7},{6,4},{7,5},{8,10},{9,11},{10,... | collective-permute-start | bytes 393224 | tf_op jit(solution)/shard_map/ppermute | solution.py:20
  34.6 1.8 %collective-permute-start.2 = (f32[256,128]{1,0:T(8,128)S(1)}, f32[256,128]{1,0:T(8,128)S(1)}, u32[]{:S(2)}, u32[]{:S(2)}) collective-permute-start(f32[256,128]{1,0:T(8,128)S(1)} %get-tuple-element.17), channel_id=1, source_target_pairs={{0,4},{1,5},{2,6},{3,7},{4,0},{5,1},{6,2},{7,3},{8,12},{9,13},{10,... | collective-permute-start | bytes 393224 | tf_op jit(solution)/shard_map/ppermute | solution.py:20
  37.0 1.7 %gather_fusion = f32[256]{0:T(256)S(1)} fusion(f32[128256]{0:T(1024)S(1)} %copy-done, s32[1024]{0:T(1024)S(1)} %pad_clamp_fusion), kind=kCustom, calls=%fused_computation | custom fusion | bytes 3072 | tf_op jit(solution)/shard_map/gather | solution.py:194
  40.1 6.3 %collective-permute-start.13 = (f32[2,256,256]{2,1,0:T(8,128)S(1)}, f32[2,256,256]{2,1,0:T(8,128)S(1)}, u32[]{:S(2)}, u32[]{:S(2)}) collective-permute-start(f32[2,256,256]{2,1,0:T(8,128)S(1)} %pad_maximum_fusion.refs_4_), channel_id=1, source_target_pairs={{0,128},{1,129},{2,130},{3,131},{4,132},{5,133},{6,134},{7,135},{8... | collective-permute-start | bytes 1572872 | tf_op jit(solution)/shard_map/ppermute | solution.py:20
  46.4 1.6 %constant_dynamic-slice_fusion = (bf16[1,256,256]{2,1,0:T(8,128)(2,1)S(1)}, bf16[256,256]{1,0:T(8,128)(2,1)}) fusion(bf16[2,256,256]{2,1,0:T(8,128)(2,1)} %collective-permute-done.19, s32[]{:T(128)S(6)} %select_n.28, s32[]{:T(128)S(6)} %select_n.29), kind=kLoop, calls=%fused_computation.13 | loop fusion | bytes 524296 | tf_op jit(solution)/shard_map/jit(dynamic_index_in_dim)/dynamic_slice | solution.py:186
  48.1 2.2 %collective-permute-start.20 = (bf16[256,256]{1,0:T(8,128)(2,1)}, bf16[256,256]{1,0:T(8,128)(2,1)S(1)}, u32[]{:S(2)}, u32[]{:S(2)}) collective-permute-start(bf16[256,256]{1,0:T(8,128)(2,1)} %get-tuple-element.28), channel_id=1, source_target_pairs={{0,1},{1,0},{2,3},{3,2},{4,5},{5,4},{6,7},{7,6},{8,9},{9,8},{10,11... | collective-permute-start | bytes 393224 | tf_op jit(solution)/shard_map/ppermute | solution.py:20
  51.6 2.2 %fusion.w_ref = f32[256,1]{1,0:T(8,128)} fusion(f32[256,1]{1,0:T(8,128)} %copy.18, s32[]{:T(128)} %bitcast.4), kind=kLoop, calls=%fused_computation.6 | loop fusion | flops 512 | bytes 2052 | tf_op jit(solution)/shard_map/mul | solution.py:194
  53.8 6.2 %collective-permute-done.4.b_ref = f32[256,128]{1,0:T(8,128)S(1)} collective-permute-done((f32[256,128]{1,0:T(8,128)S(1)}, f32[256,128]{1,0:T(8,128)S(1)}, u32[]{:S(2)}, u32[]{:S(2)}) %collective-permute-start.4) | collective-permute-done | bytes 131104 | tf_op jit(solution)/shard_map/ppermute | solution.py:20
  60.7 2.0 %shard_map.95 = (f32[8,64]{1,0:T(8,128)}, f32[8,64]{1,0:T(8,128)}, f32[8,64]{1,0:T(8,128)}, f32[8,64]{1,0:T(8,128)}) custom-call(s32[3]{0:T(128)} %copy-done.8, f32[256,128]{1,0:T(8,128)} %copy-done.7, f32[256,128]{1,0:T(8,128)} %copy-done.11, f32[256,1]{1,0:T(8,128)} %fusion.w_ref), custom_call_target="tpu_custom_call" | custom-call | tf_op jit(solution)/shard_map/pallas_call | solution.py:198
  62.6 8.4 %collective-permute-start.7 = (f32[8,64]{1,0:T(8,128)}, f32[8,64]{1,0:T(8,128)S(1)}, u32[]{:S(2)}, u32[]{:S(2)}) collective-permute-start(f32[8,64]{1,0:T(8,128)} %get-tuple-element.22), channel_id=1, source_target_pairs={{0,6},{1,7},{2,4},{3,5},{4,2},{5,3},{6,0},{7,1},{8,14},{9,15},{10,... | collective-permute-start | bytes 6152 | tf_op jit(solution)/shard_map/ppermute | solution.py:20
  72.3 3.0 %collective-permute-done.6 = f32[8,64]{1,0:T(8,128)S(1)} collective-permute-done((f32[8,64]{1,0:T(8,128)}, f32[8,64]{1,0:T(8,128)S(1)}, u32[]{:S(2)}, u32[]{:S(2)}) %collective-permute-start.6) | collective-permute-done | bytes 2080 | tf_op jit(solution)/shard_map/ppermute | solution.py:20
  82.0 2.8 %collective-permute-done.10.refs_3_ = f32[4,8,64]{2,1,0:T(8,128)S(1)} collective-permute-done((f32[4,8,64]{2,1,0:T(8,128)S(1)}, f32[4,8,64]{2,1,0:T(8,128)S(1)}, u32[]{:S(2)}, u32[]{:S(2)}) %collective-permute-start.10) | collective-permute-done | bytes 8224 | tf_op jit(solution)/shard_map/ppermute | solution.py:20
  85.3 1.6 %shard_map.96.refs_0_ = f32[16,1024]{1,0:T(8,128)S(1)} custom-call(s32[3]{0:T(128)S(1)} %copy-done.9, f32[4,8,64]{2,1,0:T(8,128)S(1)} %pad_maximum_fusion.2.refs_0_, f32[4,8,64]{2,1,0:T(8,128)S(1)} %collective-permute-done.8.refs_1_, f32[4,8,64]{2,1,0:T(8,128)S(1)} %collective-permute-done.9.refs_2_, f32[4,8,64]{2,1,0:T(8,128)S(1)} %collective-permute-done.10.refs_3_, ...), custom_call_target="tpu_custom_call" | custom-call | tf_op jit(solution)/shard_map/pallas_call | solution.py:208
  87.6 2.6 %collective-permute-start.16 = (f32[16,1024]{1,0:T(8,128)S(1)}, f32[16,1024]{1,0:T(8,128)S(1)}, u32[]{:S(2)}, u32[]{:S(2)}) collective-permute-start(f32[16,1024]{1,0:T(8,128)S(1)} %shard_map.96.refs_0_), channel_id=1, source_target_pairs={{0,4},{1,5},{2,6},{3,7},{4,0},{5,1},{6,2},{7,3},{8,12},{9,13},{10,... | collective-permute-start | bytes 196616 | tf_op jit(solution)/shard_map/ppermute | solution.py:20
  90.4 1.8 %collective-permute-start.17 = (f32[16,1024]{1,0:T(8,128)S(1)}, f32[16,1024]{1,0:T(8,128)S(1)}, u32[]{:S(2)}, u32[]{:S(2)}) collective-permute-start(f32[16,1024]{1,0:T(8,128)S(1)} %shard_map.96.refs_0_), channel_id=1, source_target_pairs={{0,6},{1,7},{2,4},{3,5},{4,2},{5,3},{6,0},{7,1},{8,14},{9,15},{10,... | collective-permute-start | bytes 196616 | tf_op jit(solution)/shard_map/ppermute | solution.py:20
  92.6 2.1 %collective-permute-done.17.refs_3_ = f32[16,1024]{1,0:T(8,128)S(1)} collective-permute-done((f32[16,1024]{1,0:T(8,128)S(1)}, f32[16,1024]{1,0:T(8,128)S(1)}, u32[]{:S(2)}, u32[]{:S(2)}) %collective-permute-start.17) | collective-permute-done | bytes 65568 | tf_op jit(solution)/shard_map/ppermute | solution.py:20
  95.2 4.8 %collective-permute-start.18 = (f32[16,1024]{1,0:T(8,128)S(1)}, f32[16,1024]{1,0:T(8,128)S(1)}, u32[]{:S(2)}, u32[]{:S(2)}) collective-permute-start(f32[16,1024]{1,0:T(8,128)S(1)} %shard_map.97.a_ref), channel_id=1, source_target_pairs={{0,8},{1,9},{2,10},{3,11},{4,12},{5,13},{6,14},{7,15},{8,0},{9,1},... | collective-permute-start | bytes 196616 | tf_op jit(solution)/shard_map/ppermute | solution.py:20
  100.0 2.3 %collective-permute-done.18.b_ref = f32[16,1024]{1,0:T(8,128)S(1)} collective-permute-done((f32[16,1024]{1,0:T(8,128)S(1)}, f32[16,1024]{1,0:T(8,128)S(1)}, u32[]{:S(2)}, u32[]{:S(2)}) %collective-permute-start.18) | collective-permute-done | bytes 65568 | tf_op jit(solution)/shard_map/ppermute | solution.py:20
  103.3 7.5 %collective-permute-start.24 = (f32[16,256]{1,0:T(8,128)S(1)}, f32[16,256]{1,0:T(8,128)S(1)}, u32[]{:S(2)}, u32[]{:S(2)}) collective-permute-start(f32[16,256]{1,0:T(8,128)S(1)} %get-tuple-element.24), channel_id=1, source_target_pairs={{0,1},{1,0},{2,3},{3,2},{4,5},{5,4},{6,7},{7,6},{8,9},{9,8},{10,11... | collective-permute-start | bytes 49160 | tf_op jit(solution)/shard_map/ppermute | solution.py:20
  111.6 1.8 %collective-permute-start.27 = (f32[4,256]{1,0:T(4,128)S(1)}, f32[4,256]{1,0:T(4,128)S(1)}, u32[]{:S(2)}, u32[]{:S(2)}) collective-permute-start(f32[4,256]{1,0:T(4,128)S(1)} %get-tuple-element.30), channel_id=1, source_target_pairs={{0,48},{1,49},{2,50},{3,51},{4,52},{5,53},{6,54},{7,55},{8,56},{9,... | collective-permute-start | bytes 12296 | tf_op jit(solution)/shard_map/ppermute | solution.py:20
  113.4 1.8 %collective-permute-start.25 = (f32[4,256]{1,0:T(4,128)S(1)}, f32[4,256]{1,0:T(4,128)S(1)}, u32[]{:S(2)}, u32[]{:S(2)}) collective-permute-start(f32[4,256]{1,0:T(4,128)S(1)} %get-tuple-element.29), channel_id=1, source_target_pairs={{0,16},{1,17},{2,18},{3,19},{4,20},{5,21},{6,22},{7,23},{8,24},{9,... | collective-permute-start | bytes 12296 | tf_op jit(solution)/shard_map/ppermute | solution.py:20
  (75 shorter events, 23.3 us)
Async XLA Ops:
  0.0 37.0 %copy-start = (f32[128256]{0:T(1024)S(1)}, f32[128256]{0:T(1024)}, u32[]{:S(2)}) copy-start(f32[128256]{0:T(1024)} %param.13) | copy-start | bytes 1539076
  8.9 10.3 %copy-start.4 = (bf16[2,1024,512]{2,1,0:T(8,128)(2,1)S(1)}, bf16[2,1024,512]{2,1,0:T(8,128)(2,1)}, u32[]{:S(2)}) copy-start(bf16[2,1024,512]{2,1,0:T(8,128)(2,1)} %acts_ref.3) | copy-start | bytes 6291460
  11.8 18.5 %collective-permute-start = (f32[1024,128]{1,0:T(8,128)}, f32[1024,128]{1,0:T(8,128)}, u32[]{:S(2)}, u32[]{:S(2)}) collective-permute-start(f32[1024,128]{1,0:T(8,128)} %shard_map.92), channel_id=1, source_target_pairs={{0,1},{1,0},{2,3},{3,2},{4,5},{5,4},{6,7},{7,6},{8,9},{9,8},{10,11... | collective-permute-start | bytes 1572872 | tf_op jit(solution)/shard_map/ppermute | solution.py:20
  16.9 22.6 %copy-start.12 = (s32[4]{0:T(128)S(1)}, s32[4]{0:T(128)}, u32[]{:S(2)}) copy-start(s32[4]{0:T(128)} %param.12) | copy-start | bytes 52
  16.9 8.5 %collective-permute-start.11 = (f32[256,256]{1,0:T(8,128)}, f32[256,256]{1,0:T(8,128)}, u32[]{:S(2)}, u32[]{:S(2)}) collective-permute-start(f32[256,256]{1,0:T(8,128)} %get-tuple-element.26), channel_id=1, source_target_pairs={{0,1},{1,0},{2,3},{3,2},{4,5},{5,4},{6,7},{7,6},{8,9},{9,8},{10,11... | collective-permute-start | bytes 786440 | tf_op jit(solution)/shard_map/ppermute | solution.py:20
  16.9 23.2 %collective-permute-start.19 = (bf16[2,256,256]{2,1,0:T(8,128)(2,1)}, bf16[2,256,256]{2,1,0:T(8,128)(2,1)}, u32[]{:S(2)}, u32[]{:S(2)}) collective-permute-start(bf16[2,256,256]{2,1,0:T(8,128)(2,1)} %param.17), channel_id=1, source_target_pairs={{0,0},{1,16},{2,32},{3,48},{4,64},{5,80},{6,96},{7,112},{8,128},{9... | collective-permute-start | bytes 786440 | tf_op jit(solution)/shard_map/ppermute | solution.py:20
  23.2 27.1 %copy-start.8 = (s32[3]{0:T(128)}, s32[3]{0:T(128)S(1)}, u32[]{:S(2)}) copy-start(s32[3]{0:T(128)S(1)} %pad_add_fusion.place_ref) | copy-start | bytes 40
  26.4 44.6 %collective-permute-start.12 = (f32[2,256,256]{2,1,0:T(8,128)S(1)}, f32[2,256,256]{2,1,0:T(8,128)S(1)}, u32[]{:S(2)}, u32[]{:S(2)}) collective-permute-start(f32[2,256,256]{2,1,0:T(8,128)S(1)} %pad_maximum_fusion.refs_4_), channel_id=1, source_target_pairs={{0,64},{1,65},{2,66},{3,67},{4,68},{5,69},{6,70},{7,71},{8,72},{9,... | collective-permute-start | bytes 1572872 | tf_op jit(solution)/shard_map/ppermute | solution.py:20
  31.4 15.0 %collective-permute-start.1 = (f32[256,128]{1,0:T(8,128)S(1)}, f32[256,128]{1,0:T(8,128)S(1)}, u32[]{:S(2)}, u32[]{:S(2)}) collective-permute-start(f32[256,128]{1,0:T(8,128)S(1)} %get-tuple-element.16), channel_id=1, source_target_pairs={{0,2},{1,3},{2,0},{3,1},{4,6},{5,7},{6,4},{7,5},{8,10},{9,11},{10,... | collective-permute-start | bytes 393224 | tf_op jit(solution)/shard_map/ppermute | solution.py:20
  34.6 13.5 %collective-permute-start.2 = (f32[256,128]{1,0:T(8,128)S(1)}, f32[256,128]{1,0:T(8,128)S(1)}, u32[]{:S(2)}, u32[]{:S(2)}) collective-permute-start(f32[256,128]{1,0:T(8,128)S(1)} %get-tuple-element.17), channel_id=1, source_target_pairs={{0,4},{1,5},{2,6},{3,7},{4,0},{5,1},{6,2},{7,3},{8,12},{9,13},{10,... | collective-permute-start | bytes 393224 | tf_op jit(solution)/shard_map/ppermute | solution.py:20
  36.4 13.9 %collective-permute-start.3 = (f32[256,128]{1,0:T(8,128)S(1)}, f32[256,128]{1,0:T(8,128)S(1)}, u32[]{:S(2)}, u32[]{:S(2)}) collective-permute-start(f32[256,128]{1,0:T(8,128)S(1)} %get-tuple-element.18), channel_id=1, source_target_pairs={{0,6},{1,7},{2,4},{3,5},{4,2},{5,3},{6,0},{7,1},{8,14},{9,15},{10,... | collective-permute-start | bytes 393224 | tf_op jit(solution)/shard_map/ppermute | solution.py:20
  40.1 37.0 %collective-permute-start.13 = (f32[2,256,256]{2,1,0:T(8,128)S(1)}, f32[2,256,256]{2,1,0:T(8,128)S(1)}, u32[]{:S(2)}, u32[]{:S(2)}) collective-permute-start(f32[2,256,256]{2,1,0:T(8,128)S(1)} %pad_maximum_fusion.refs_4_), channel_id=1, source_target_pairs={{0,128},{1,129},{2,130},{3,131},{4,132},{5,133},{6,134},{7,135},{8... | collective-permute-start | bytes 1572872 | tf_op jit(solution)/shard_map/ppermute | solution.py:20
  46.4 31.7 %collective-permute-start.14 = (f32[2,256,256]{2,1,0:T(8,128)S(1)}, f32[2,256,256]{2,1,0:T(8,128)S(1)}, u32[]{:S(2)}, u32[]{:S(2)}) collective-permute-start(f32[2,256,256]{2,1,0:T(8,128)S(1)} %pad_maximum_fusion.refs_4_), channel_id=1, source_target_pairs={{0,192},{1,193},{2,194},{3,195},{4,196},{5,197},{6,198},{7,199},{8... | collective-permute-start | bytes 1572872 | tf_op jit(solution)/shard_map/ppermute | solution.py:20
  48.1 23.0 %collective-permute-start.20 = (bf16[256,256]{1,0:T(8,128)(2,1)}, bf16[256,256]{1,0:T(8,128)(2,1)S(1)}, u32[]{:S(2)}, u32[]{:S(2)}) collective-permute-start(bf16[256,256]{1,0:T(8,128)(2,1)} %get-tuple-element.28), channel_id=1, source_target_pairs={{0,1},{1,0},{2,3},{3,2},{4,5},{5,4},{6,7},{7,6},{8,9},{9,8},{10,11... | collective-permute-start | bytes 393224 | tf_op jit(solution)/shard_map/ppermute | solution.py:20
  50.9 9.1 %collective-permute-start.4 = (f32[256,128]{1,0:T(8,128)S(1)}, f32[256,128]{1,0:T(8,128)S(1)}, u32[]{:S(2)}, u32[]{:S(2)}) collective-permute-start(f32[256,128]{1,0:T(8,128)S(1)} %shard_map.94.a_ref), channel_id=1, source_target_pairs={{0,8},{1,9},{2,10},{3,11},{4,12},{5,13},{6,14},{7,15},{8,0},{9,1},... | collective-permute-start | bytes 393224 | tf_op jit(solution)/shard_map/ppermute | solution.py:20
  62.6 9.6 %collective-permute-start.7 = (f32[8,64]{1,0:T(8,128)}, f32[8,64]{1,0:T(8,128)S(1)}, u32[]{:S(2)}, u32[]{:S(2)}) collective-permute-start(f32[8,64]{1,0:T(8,128)} %get-tuple-element.22), channel_id=1, source_target_pairs={{0,6},{1,7},{2,4},{3,5},{4,2},{5,3},{6,0},{7,1},{8,14},{9,15},{10,... | collective-permute-start | bytes 6152 | tf_op jit(solution)/shard_map/ppermute | solution.py:20
  71.0 4.2 %collective-permute-start.6 = (f32[8,64]{1,0:T(8,128)}, f32[8,64]{1,0:T(8,128)S(1)}, u32[]{:S(2)}, u32[]{:S(2)}) collective-permute-start(f32[8,64]{1,0:T(8,128)} %get-tuple-element.21), channel_id=1, source_target_pairs={{0,4},{1,5},{2,6},{3,7},{4,0},{5,1},{6,2},{7,3},{8,12},{9,13},{10,... | collective-permute-start | bytes 6152 | tf_op jit(solution)/shard_map/ppermute | solution.py:20
  71.1 4.2 %collective-permute-start.5 = (f32[8,64]{1,0:T(8,128)}, f32[8,64]{1,0:T(8,128)S(1)}, u32[]{:S(2)}, u32[]{:S(2)}) collective-permute-start(f32[8,64]{1,0:T(8,128)} %get-tuple-element.20), channel_id=1, source_target_pairs={{0,2},{1,3},{2,0},{3,1},{4,6},{5,7},{6,4},{7,5},{8,10},{9,11},{10,... | collective-permute-start | bytes 6152 | tf_op jit(solution)/shard_map/ppermute | solution.py:20
  72.2 27.8 %collective-permute-start.21 = (bf16[2,256,256]{2,1,0:T(8,128)(2,1)S(1)}, bf16[2,256,256]{2,1,0:T(8,128)(2,1)S(1)}, u32[]{:S(2)}, u32[]{:S(2)}) collective-permute-start(bf16[2,256,256]{2,1,0:T(8,128)(2,1)S(1)} %pad_maximum_fusion.1.refs_0_), channel_id=1, source_target_pairs={{0,64},{1,65},{2,66},{3,67},{4,68},{5,69},{6,70},{7,71},{8,72},{9,... | collective-permute-start | bytes 786440 | tf_op jit(solution)/shard_map/ppermute | solution.py:20
  75.2 24.8 %collective-permute-start.22 = (bf16[2,256,256]{2,1,0:T(8,128)(2,1)S(1)}, bf16[2,256,256]{2,1,0:T(8,128)(2,1)S(1)}, u32[]{:S(2)}, u32[]{:S(2)}) collective-permute-start(bf16[2,256,256]{2,1,0:T(8,128)(2,1)S(1)} %pad_maximum_fusion.1.refs_0_), channel_id=1, source_target_pairs={{0,128},{1,129},{2,130},{3,131},{4,132},{5,133},{6,134},{7,135},{8... | collective-permute-start | bytes 786440 | tf_op jit(solution)/shard_map/ppermute | solution.py:20
  75.2 24.8 %collective-permute-start.23 = (bf16[2,256,256]{2,1,0:T(8,128)(2,1)S(1)}, bf16[2,256,256]{2,1,0:T(8,128)(2,1)S(1)}, u32[]{:S(2)}, u32[]{:S(2)}) collective-permute-start(bf16[2,256,256]{2,1,0:T(8,128)(2,1)S(1)} %pad_maximum_fusion.1.refs_0_), channel_id=1, source_target_pairs={{0,192},{1,193},{2,194},{3,195},{4,196},{5,197},{6,198},{7,199},{8... | collective-permute-start | bytes 786440 | tf_op jit(solution)/shard_map/ppermute | solution.py:20
  77.1 2.9 %collective-permute-start.8 = (f32[4,8,64]{2,1,0:T(8,128)S(1)}, f32[4,8,64]{2,1,0:T(8,128)S(1)}, u32[]{:S(2)}, u32[]{:S(2)}) collective-permute-start(f32[4,8,64]{2,1,0:T(8,128)S(1)} %pad_maximum_fusion.2.refs_0_), channel_id=1, source_target_pairs={{0,16},{1,17},{2,18},{3,19},{4,20},{5,21},{6,22},{7,23},{8,24},{9,... | collective-permute-start | bytes 24584 | tf_op jit(solution)/shard_map/ppermute | solution.py:20
  78.2 3.8 %collective-permute-start.9 = (f32[4,8,64]{2,1,0:T(8,128)S(1)}, f32[4,8,64]{2,1,0:T(8,128)S(1)}, u32[]{:S(2)}, u32[]{:S(2)}) collective-permute-start(f32[4,8,64]{2,1,0:T(8,128)S(1)} %pad_maximum_fusion.2.refs_0_), channel_id=1, source_target_pairs={{0,32},{1,33},{2,34},{3,35},{4,36},{5,37},{6,38},{7,39},{8,40},{9,... | collective-permute-start | bytes 24584 | tf_op jit(solution)/shard_map/ppermute | solution.py:20
  80.0 4.7 %collective-permute-start.10 = (f32[4,8,64]{2,1,0:T(8,128)S(1)}, f32[4,8,64]{2,1,0:T(8,128)S(1)}, u32[]{:S(2)}, u32[]{:S(2)}) collective-permute-start(f32[4,8,64]{2,1,0:T(8,128)S(1)} %pad_maximum_fusion.2.refs_0_), channel_id=1, source_target_pairs={{0,48},{1,49},{2,50},{3,51},{4,52},{5,53},{6,54},{7,55},{8,56},{9,... | collective-permute-start | bytes 24584 | tf_op jit(solution)/shard_map/ppermute | solution.py:20
  86.9 3.4 %collective-permute-start.15 = (f32[16,1024]{1,0:T(8,128)S(1)}, f32[16,1024]{1,0:T(8,128)S(1)}, u32[]{:S(2)}, u32[]{:S(2)}) collective-permute-start(f32[16,1024]{1,0:T(8,128)S(1)} %shard_map.96.refs_0_), channel_id=1, source_target_pairs={{0,2},{1,3},{2,0},{3,1},{4,6},{5,7},{6,4},{7,5},{8,10},{9,11},{10,... | collective-permute-start | bytes 196616 | tf_op jit(solution)/shard_map/ppermute | solution.py:20
  87.6 4.9 %collective-permute-start.16 = (f32[16,1024]{1,0:T(8,128)S(1)}, f32[16,1024]{1,0:T(8,128)S(1)}, u32[]{:S(2)}, u32[]{:S(2)}) collective-permute-start(f32[16,1024]{1,0:T(8,128)S(1)} %shard_map.96.refs_0_), channel_id=1, source_target_pairs={{0,4},{1,5},{2,6},{3,7},{4,0},{5,1},{6,2},{7,3},{8,12},{9,13},{10,... | collective-permute-start | bytes 196616 | tf_op jit(solution)/shard_map/ppermute | solution.py:20
  90.4 4.3 %collective-permute-start.17 = (f32[16,1024]{1,0:T(8,128)S(1)}, f32[16,1024]{1,0:T(8,128)S(1)}, u32[]{:S(2)}, u32[]{:S(2)}) collective-permute-start(f32[16,1024]{1,0:T(8,128)S(1)} %shard_map.96.refs_0_), channel_id=1, source_target_pairs={{0,6},{1,7},{2,4},{3,5},{4,2},{5,3},{6,0},{7,1},{8,14},{9,15},{10,... | collective-permute-start | bytes 196616 | tf_op jit(solution)/shard_map/ppermute | solution.py:20
  95.2 7.1 %collective-permute-start.18 = (f32[16,1024]{1,0:T(8,128)S(1)}, f32[16,1024]{1,0:T(8,128)S(1)}, u32[]{:S(2)}, u32[]{:S(2)}) collective-permute-start(f32[16,1024]{1,0:T(8,128)S(1)} %shard_map.97.a_ref), channel_id=1, source_target_pairs={{0,8},{1,9},{2,10},{3,11},{4,12},{5,13},{6,14},{7,15},{8,0},{9,1},... | collective-permute-start | bytes 196616 | tf_op jit(solution)/shard_map/ppermute | solution.py:20
  103.3 8.3 %collective-permute-start.24 = (f32[16,256]{1,0:T(8,128)S(1)}, f32[16,256]{1,0:T(8,128)S(1)}, u32[]{:S(2)}, u32[]{:S(2)}) collective-permute-start(f32[16,256]{1,0:T(8,128)S(1)} %get-tuple-element.24), channel_id=1, source_target_pairs={{0,1},{1,0},{2,3},{3,2},{4,5},{5,4},{6,7},{7,6},{8,9},{9,8},{10,11... | collective-permute-start | bytes 49160 | tf_op jit(solution)/shard_map/ppermute | solution.py:20
  111.6 4.3 %collective-permute-start.27 = (f32[4,256]{1,0:T(4,128)S(1)}, f32[4,256]{1,0:T(4,128)S(1)}, u32[]{:S(2)}, u32[]{:S(2)}) collective-permute-start(f32[4,256]{1,0:T(4,128)S(1)} %get-tuple-element.30), channel_id=1, source_target_pairs={{0,48},{1,49},{2,50},{3,51},{4,52},{5,53},{6,54},{7,55},{8,56},{9,... | collective-permute-start | bytes 12296 | tf_op jit(solution)/shard_map/ppermute | solution.py:20
  113.4 3.6 %collective-permute-start.26 = (f32[4,256]{1,0:T(4,128)S(1)}, f32[4,256]{1,0:T(4,128)S(1)}, u32[]{:S(2)}, u32[]{:S(2)}) collective-permute-start(f32[4,256]{1,0:T(4,128)S(1)} %get-tuple-element.31), channel_id=1, source_target_pairs={{0,32},{1,33},{2,34},{3,35},{4,36},{5,37},{6,38},{7,39},{8,40},{9,... | collective-permute-start | bytes 12296 | tf_op jit(solution)/shard_map/ppermute | solution.py:20
  113.4 3.6 %collective-permute-start.25 = (f32[4,256]{1,0:T(4,128)S(1)}, f32[4,256]{1,0:T(4,128)S(1)}, u32[]{:S(2)}, u32[]{:S(2)}) collective-permute-start(f32[4,256]{1,0:T(4,128)S(1)} %get-tuple-element.29), channel_id=1, source_target_pairs={{0,16},{1,17},{2,18},{3,19},{4,20},{5,21},{6,22},{7,23},{8,24},{9,... | collective-permute-start | bytes 12296 | tf_op jit(solution)/shard_map/ppermute | solution.py:20
  (9 other events, 22.2 us)

commit v2 on v0

v2 whole, which is shorter than its diff:
```python
import functools
import jax
import jax.numpy as jnp
from jax import lax
from jax.experimental import pallas as pl
from jax.experimental.pallas import tpu as pltpu
from jax.sharding import PartitionSpec as P

AXES = ("x", "zl", "z", "y", "c")
DP = ("x", "zl")
MP = ("z", "y", "c")
VMEM = pl.BlockSpec(memory_space=pltpu.VMEM)
SMEM = pl.BlockSpec(memory_space=pltpu.SMEM)
ANY = pl.BlockSpec(memory_space=pl.ANY)


def send(value, target):
    pairs = []
    for d in range(16):
        for m in range(16):
            td, tm = target(d, m)
            pairs.append((d * 16 + m, td * 16 + tm))
    return lax.ppermute(value, AXES, pairs)


def to_core(value):
    return send(value, lambda d, m: (d, m ^ 1))


def to_z(value):
    return send(value, lambda d, m: (d, m ^ 8))


def to_zl(value, k):
    return send(value, lambda d, m: (d ^ k, m))


def to_x(value, k):
    return send(value, lambda d, m: (d ^ (4 * k), m))


def where():
    return lax.axis_index("z"), lax.axis_index("y"), lax.axis_index("c")


def project_kernel(layer_ref, acts_ref, grads_ref, in_ref, out_ref, res_ref):
    def times(rows, weights):
        return lax.dot_general(
            rows, weights, (((1,), (1,)), ((), ())), preferred_element_type=jnp.float32
        )

    x = times(acts_ref[0], in_ref[0])
    g = times(grads_ref[0], out_ref[0])
    res_ref[...] = jnp.concatenate([x, g], axis=1)


def project(layer, acts, out_grads, proj_in, proj_out):
    tokens, width = acts.shape[1:]
    hidden = out_grads.shape[2]
    rank = proj_in.shape[1]
    block = 512
    return pl.pallas_call(
        project_kernel,
        grid_spec=pltpu.PrefetchScalarGridSpec(
            num_scalar_prefetch=1,
            grid=(tokens // block,),
            in_specs=[
                pl.BlockSpec((1, block, width), lambda t, l: (l[0], t, 0)),
                pl.BlockSpec((1, block, hidden), lambda t, l: (l[0], t, 0)),
                pl.BlockSpec((1, rank, width), lambda t, l: (l[0], 0, 0)),
                pl.BlockSpec((1, rank, hidden), lambda t, l: (l[0], 0, 0)),
            ],
            out_specs=pl.BlockSpec((block, 2 * rank), lambda t, l: (t, 0)),
        ),
        out_shape=jax.ShapeDtypeStruct((tokens, 2 * rank), jnp.float32),
        compiler_params=pltpu.CompilerParams(vmem_limit_bytes=56 * 2**20),
        cost_estimate=pl.CostEstimate(
            flops=2 * tokens * (width + hidden) * 256,
            bytes_accessed=tokens * (width + hidden) * 2,
            transcendentals=0,
        ),
    )(layer, acts, out_grads, proj_in, proj_out)


def cost(us):
    return pl.CostEstimate(flops=0, bytes_accessed=int(us * 3.69e6), transcendentals=0)


def call(kernel, out, *args, scratch=(), specs=None, us=1.0):
    return pl.pallas_call(
        kernel,
        in_specs=specs or [VMEM] * len(args),
        out_specs=[VMEM] * len(out),
        out_shape=[jax.ShapeDtypeStruct(s, jnp.float32) for s in out],
        scratch_shapes=[pltpu.VMEM(s, jnp.float32) for s in scratch],
        cost_estimate=cost(us),
        compiler_params=pltpu.CompilerParams(vmem_limit_bytes=32 * 2**20),
    )(*args)


def split_kernel(a_ref, b_ref, out):
    rows = out.shape[1]
    for block in range(out.shape[0]):
        at = slice(rows * block, rows * (block + 1))
        out[block] = a_ref[at] + b_ref[at]


def total_kernel(parts_ref, out):
    out[...] = jnp.sum(parts_ref[...], axis=0)


def gram_kernel(length_ref, a_ref, b_ref, w_ref, out, held):
    x, y = lax.axis_index("x"), lax.axis_index("y")
    total = a_ref[...] + b_ref[...]
    slots = lax.broadcasted_iota(jnp.int32, w_ref.shape, 1)
    weights = jnp.where(slots < length_ref[y], w_ref[...], 0.0)
    held[...] = jnp.dot(
        total[:, :64].T * weights,
        total[:, 64:],
        precision=lax.Precision.HIGHEST,
        preferred_element_type=jnp.float32,
    )
    for zl in range(4):
        piece = []
        for k in range(4):
            at = (x ^ k) * 16 + zl * 4
            even = held[pl.ds(at, 2, stride=2)]
            odd = held[pl.ds(at + 1, 2, stride=2)]
            piece.append(jnp.concatenate([even, odd], axis=1))
        piece = jnp.concatenate(piece, axis=0)
        for core in range(2):
            for y in range(4):
                out[16 * core + 4 * zl + y] = piece


def image_kernel(rows_ref, *refs):
    hess, out = refs[:4], refs[4]
    for layer in range(2):
        at = slice(16 * layer, 16 * (layer + 1))
        total = 0.0
        for k in range(4):
            rows = [rows_ref[at, 2 * k + half, :] for half in range(2)]
            total = total + lax.dot_general(
                jnp.concatenate(rows, axis=1),
                hess[k][layer],
                (((1,), (1,)), ((), ())),
                precision=lax.Precision.HIGHEST,
                preferred_element_type=jnp.float32,
            )
        out[at] = total


def score_kernel(*refs):
    images, queries, out = refs[:4], refs[4:8], refs[8]
    x = lax.axis_index("x")
    image = images[0][...] + images[1][...] + images[2][...] + images[3][...]
    high = image.astype(jnp.bfloat16)
    rest = image - high.astype(jnp.float32)
    mid = rest.astype(jnp.bfloat16)
    low = (rest - mid.astype(jnp.float32)).astype(jnp.bfloat16)
    for k in range(4):
        part = 0.0
        for layer in range(2):
            at = slice(16 * layer, 16 * (layer + 1))
            part = part + lax.dot_general(
                jnp.concatenate([high[at], mid[at], low[at]], axis=0),
                queries[k][layer],
                (((1,), (1,)), ((), ())),
                preferred_element_type=jnp.float32,
            )
        part = part[:16] + part[16:32] + part[32:]
        for zl in range(4):
            out[4 * (x ^ k) + zl] = part[4 * zl : 4 * zl + 4]


def per_device(
    acts, out_grads, token_ids, lengths, token_weight, proj_in, proj_out, hess_inv, queries
):
    z, y, c = where()
    proj_in = jnp.swapaxes(proj_in, 1, 2)
    proj_out = jnp.swapaxes(proj_out, 1, 2)
    others = (1, 2, 3)

    other = project((1 - c)[None], acts, out_grads, proj_in, proj_out)
    theirs = to_core(other)
    hess = [hess_inv] + [to_x(hess_inv, k) for k in others]
    query = [queries] + [to_x(queries, k) for k in others]
    mine = project(c[None], acts, out_grads, proj_in, proj_out)

    (blocks,) = call(split_kernel, [(4, 256, 128)], mine, theirs)
    blocks = lax.all_to_all(blocks, "y", 0, 0, tiled=True)

    ids = lax.dynamic_index_in_dim(token_ids, y, 0, keepdims=False)
    weights = token_weight.at[ids].get(mode="promise_in_bounds")[None]

    (half,) = call(total_kernel, [(256, 128)], blocks)
    (grams,) = call(
        gram_kernel,
        [(32, 8, 128)],
        lengths,
        half,
        to_z(half),
        weights,
        scratch=[(64, 64)],
        specs=[SMEM] + [VMEM] * 3,
    )
    grams = lax.all_to_all(grams, ("c", "zl", "y"), 0, 0, tiled=True)
    (image,) = call(image_kernel, [(32, 256)], grams, *hess)
    images = [image] + [to_zl(image, k) for k in others]
    (parts,) = call(score_kernel, [(16, 4, 256)], *images, *query)
    parts = lax.all_to_all(parts, MP, 0, 0, tiled=True)
    (scores,) = call(total_kernel, [(4, 256)], parts)
    return send(scores, lambda d, m: (d // 4 * 4 + m % 4, m // 4 * 4 + d % 4))


def solution(mesh):
    mesh = jax.sharding.Mesh(mesh.devices.reshape(4, 4, 2, 4, 2), AXES)
    in_specs = (
        P(None, DP, MP),
        P(None, DP, MP),
        P(DP, None),
        P(DP),
        P(),
        P(None, MP, None),
        P(None, MP, None),
        P(None, MP, DP),
        P(None, DP, MP),
    )
    return jax.shard_map(
        per_device, mesh=mesh, in_specs=in_specs, out_specs=P(DP, MP), check_vma=False
    )
```

time: 551 us -> 88.3 us (0.16)
  waiting for transfers between devices: 492 us -> 12.9 us
  starting transfers between devices: 0.35 us -> 37.4 us
  matrix products: 23.2 us -> 0 us
  blocking collectives: 0 us -> 18.7 us
  local copies, waits for them, and re-layouts: 20.4 us -> 3.37 us
  between operations: 14.7 us -> 0.08 us
  Pallas kernels: 0 us -> 13.9 us
    psum x1 -> x0, waiting for transfers between devices: 290 us -> none  [per_device(): x_all, g_all = lax.psum((x_proj, g_proj), 'mp')]
    unnamed x7 -> x0, waiting for transfers between devices: 177 us -> none
    ppermute x0 -> x12, starting transfers between devices: none -> 25.1 us  [send(): return lax.ppermute(value, AXES, pairs)]
    all_gather x2 -> x0, waiting for transfers between devices: 24.6 us -> none  [the longest x1 24.6 us: per_device(): lax.all_gather(queries, 'dp', axis=1, tiled=True).astype(jnp.float32)]
    dot_general x5 -> x0, matrix products: 23.2 us -> none  [the longest x1 7.42 us: per_device(): jnp.einsum('ler,lrf->lef', grams, lax.all_gather(hess_inv, 'dp', axis=2,...]
    all_to_all x0 -> x1, blocking collectives: none -> 18.7 us  [per_device(): parts = lax.all_to_all(parts, MP, 0, 0, tiled=True)]
    pallas_call x0 -> x8, Pallas kernels: none -> 13.9 us  [the longest x2 8.22 us: project(): pl.pallas_call(project_kernel, grid_spec=pltpu.PrefetchScalarGridSpec(num...]
    all_to_all x0 -> x2, starting transfers between devices: none -> 12.3 us  [the longest x1 8.84 us: per_device(): grams = lax.all_to_all(grams, ('c', 'zl', 'y'), 0, 0, tiled=True)]
  transfers between devices with their start and end apart: 5 -> 14, of which waited for: 4 -> 5; matrix products, arithmetic and copies ran while one was open for 2% -> 3% of each run, Pallas kernels for 0% -> 9%
where the time goes in v2:
time: 88.3 us; the launch traced here: 87 us
  starting transfers between devices  37.4 us (42%)
  blocking collectives  18.7 us (21%)
  Pallas kernels  13.9 us (16%)
  waiting for transfers between devices  12.9 us (15%)
  local copies, waits for them, and re-layouts  3.37 us (4%)
    ppermute x12, starting transfers between devices, send(): return lax.ppermute(value, AXES, pairs)  25.1 us
    all_to_all x1, blocking collectives, per_device(): parts = lax.all_to_all(parts, MP, 0, 0, tiled=True)  18.7 us
    all_to_all x1, starting transfers between devices, per_device(): grams = lax.all_to_all(grams, ('c', 'zl', 'y'), 0, 0, tiled=True)  8.84 us
    pallas_call x2, Pallas kernels, project(): pl.pallas_call(project_kernel, grid_spec=pltpu.PrefetchScalarGridSpec(num...  8.22 us
    pallas_call x6, Pallas kernels, call(): pl.pallas_call(kernel, in_specs=specs or [VMEM] * len(args), out_specs=[V...  5.68 us
    all_to_all x1, waiting for transfers between devices, per_device(): grams = lax.all_to_all(grams, ('c', 'zl', 'y'), 0, 0, tiled=True)  4.57 us
    ppermute x12, waiting for transfers between devices, send(): return lax.ppermute(value, AXES, pairs)  4.19 us
    all_to_all x1, waiting for transfers between devices, per_device(): blocks = lax.all_to_all(blocks, 'y', 0, 0, tiled=True)  4.11 us
  transfers between devices with their start and end apart: 14, of which 5 were waited for; matrix products, arithmetic and copies ran while one was open for 3% of the time, Pallas kernels for 9%

profile of v2, /device:TPU:1, one launch (start us, length us, event | category | flops | bytes accessed | tf_op | source)
XLA Modules:
  0.0 87.0 jit_solution(13522083434133630012)
XLA Ops:
  0.0 4.1 %shard_map.92 = f32[1024,128]{1,0:T(8,128)} custom-call(s32[1]{0:T(128)} %bitcast.3.layer_ref, bf16[2,1024,512]{2,1,0:T(8,128)(2,1)} %acts_ref.3, bf16[2,1024,1792]{2,1,0:T(8,128)(2,1)} %grads_ref.3, bf16[2,64,512]{2,1,0:T(8,128)(2,1)} %bitcast.11, bf16[2,64,1792]{2,1,0:T(8,128)(2,1)} %bitcast.9), custom_call_target="tpu_custom_call" | custom-call | flops 1207959552 | bytes 4718592 | tf_op jit(solution)/shard_map/pallas_call | solution.py:62
  4.1 3.3 %collective-permute-start = (f32[1024,128]{1,0:T(8,128)}, f32[1024,128]{1,0:T(8,128)S(1)}, u32[]{:S(2)}, u32[]{:S(2)}) collective-permute-start(f32[1024,128]{1,0:T(8,128)} %shard_map.92), channel_id=1, source_target_pairs={{0,1},{1,0},{2,3},{3,2},{4,5},{5,4},{6,7},{7,6},{8,9},{9,8},{10,11... | collective-permute-start | bytes 1572872 | tf_op jit(solution)/shard_map/ppermute | solution.py:23
  7.4 4.1 %shard_map.91.a_ref = f32[1024,128]{1,0:T(8,128)} custom-call(s32[1]{0:T(128)} %bitcast.layer_ref, bf16[2,1024,512]{2,1,0:T(8,128)(2,1)} %acts_ref.3, bf16[2,1024,1792]{2,1,0:T(8,128)(2,1)} %grads_ref.3, bf16[2,64,512]{2,1,0:T(8,128)(2,1)} %bitcast.12, bf16[2,64,1792]{2,1,0:T(8,128)(2,1)} %bitcast.10), custom_call_target="tpu_custom_call" | custom-call | flops 1207959552 | bytes 4718592 | tf_op jit(solution)/shard_map/pallas_call | solution.py:62
  11.5 0.0 collective-permute-done.b_ref
  11.5 1.0 %copy-done.1 = f32[1024,128]{1,0:T(8,128)S(1)} copy-done((f32[1024,128]{1,0:T(8,128)S(1)}, f32[1024,128]{1,0:T(8,128)}, u32[]{:S(2)}) %copy-start.1) | copy-done | bytes 524312
  12.6 0.8 shard_map.93
  13.4 3.5 %all-to-all-start = ((f32[4,256,128]{2,1,0:T(8,128)}), f32[4,256,128]{2,1,0:T(8,128)S(1)}, u32[]{:S(2)}, u32[]{:S(2)}) async-start(f32[4,256,128]{2,1,0:T(8,128)} %shard_map.93), calls=%async_computation | async-start | bytes 1048576 | tf_op jit(solution)/shard_map/all_to_all | solution.py:191
  16.9 0.2 collective-permute-start.2
  17.1 2.5 %collective-permute-start.3 = (f32[2,256,256]{2,1,0:T(8,128)S(1)}, f32[2,256,256]{2,1,0:T(8,128)S(1)}, u32[]{:S(2)}, u32[]{:S(2)}) collective-permute-start(f32[2,256,256]{2,1,0:T(8,128)S(1)} %copy-done.2), channel_id=1, source_target_pairs={{0,128},{1,129},{2,130},{3,131},{4,132},{5,133},{6,134},{7,135},{8... | collective-permute-start | bytes 1572872 | tf_op jit(solution)/shard_map/ppermute | solution.py:23
  19.6 1.3 %collective-permute-start.4 = (f32[2,256,256]{2,1,0:T(8,128)S(1)}, f32[2,256,256]{2,1,0:T(8,128)S(1)}, u32[]{:S(2)}, u32[]{:S(2)}) collective-permute-start(f32[2,256,256]{2,1,0:T(8,128)S(1)} %copy-done.2), channel_id=1, source_target_pairs={{0,192},{1,193},{2,194},{3,195},{4,196},{5,197},{6,198},{7,199},{8... | collective-permute-start | bytes 1572872 | tf_op jit(solution)/shard_map/ppermute | solution.py:23
  20.9 1.4 %collective-permute-start.10 = (bf16[2,256,256]{2,1,0:T(8,128)(2,1)S(1)}, bf16[2,256,256]{2,1,0:T(8,128)(2,1)}, u32[]{:S(2)}, u32[]{:S(2)}) collective-permute-start(bf16[2,256,256]{2,1,0:T(8,128)(2,1)S(1)} %copy-done.3), channel_id=1, source_target_pairs={{0,192},{1,193},{2,194},{3,195},{4,196},{5,197},{6,198},{7,199},{8... | collective-permute-start | bytes 786440 | tf_op jit(solution)/shard_map/ppermute | solution.py:23
  22.2 4.1 %all-to-all-done.parts_ref = f32[4,256,128]{2,1,0:T(8,128)S(1)} async-done(((f32[4,256,128]{2,1,0:T(8,128)}), f32[4,256,128]{2,1,0:T(8,128)S(1)}, u32[]{:S(2)}, u32[]{:S(2)}) %all-to-all-start) | async-done | bytes 524320 | tf_op jit(solution)/shard_map/all_to_all | solution.py:191
  26.4 5.7 %collective-permute-start.1 = (f32[256,128]{1,0:T(8,128)S(1)}, f32[256,128]{1,0:T(8,128)S(1)}, u32[]{:S(2)}, u32[]{:S(2)}) collective-permute-start(f32[256,128]{1,0:T(8,128)S(1)} %shard_map.94.a_ref), channel_id=1, source_target_pairs={{0,8},{1,9},{2,10},{3,11},{4,12},{5,13},{6,14},{7,15},{8,0},{9,1},... | collective-permute-start | bytes 393224 | tf_op jit(solution)/shard_map/ppermute | solution.py:23
  32.1 0.7 compare_select_fusion
  32.8 1.7 %gather_fusion = f32[256]{0:T(256)S(1)} fusion(f32[128256]{0:T(1024)S(1)} %copy-done, s32[1024]{0:T(1024)S(1)} %pad_clamp_fusion), kind=kCustom, calls=%fused_computation | custom fusion | bytes 3072 | tf_op jit(solution)/shard_map/gather | solution.py:194
  34.5 0.0 collective-permute-done.1.b_ref
  34.5 1.6 %shard_map.95 = f32[32,8,128]{2,1,0:T(8,128)} custom-call(s32[4]{0:T(128)S(1)} %copy-done.4, f32[256,128]{1,0:T(8,128)S(1)} %shard_map.94.a_ref, f32[256,128]{1,0:T(8,128)S(1)} %collective-permute-done.1.b_ref, f32[1,256]{1,0:T(1,128)S(1)} %bitcast.8), custom_call_target="tpu_custom_call" | custom-call | bytes 3690000 | tf_op jit(solution)/shard_map/pallas_call | solution.py:90
  36.1 8.8 %all-to-all-start.1 = ((f32[32,8,128]{2,1,0:T(8,128)}), f32[32,8,128]{2,1,0:T(8,128)S(1)}, u32[]{:S(2)}, u32[]{:S(2)}) async-start(f32[32,8,128]{2,1,0:T(8,128)} %shard_map.95), calls=%async_computation.1 | async-start | bytes 262144 | tf_op jit(solution)/shard_map/all_to_all | solution.py:207
  45.0 1.3 %collective-permute-start.8 = (bf16[2,256,256]{2,1,0:T(8,128)(2,1)S(1)}, bf16[2,256,256]{2,1,0:T(8,128)(2,1)S(1)}, u32[]{:S(2)}, u32[]{:S(2)}) collective-permute-start(bf16[2,256,256]{2,1,0:T(8,128)(2,1)S(1)} %copy-done.3), channel_id=1, source_target_pairs={{0,64},{1,65},{2,66},{3,67},{4,68},{5,69},{6,70},{7,71},{8,72},{9,... | collective-permute-start | bytes 786440 | tf_op jit(solution)/shard_map/ppermute | solution.py:23
  46.3 2.5 %collective-permute-start.9 = (bf16[2,256,256]{2,1,0:T(8,128)(2,1)S(1)}, bf16[2,256,256]{2,1,0:T(8,128)(2,1)}, u32[]{:S(2)}, u32[]{:S(2)}) collective-permute-start(bf16[2,256,256]{2,1,0:T(8,128)(2,1)S(1)} %copy-done.3), channel_id=1, source_target_pairs={{0,128},{1,129},{2,130},{3,131},{4,132},{5,133},{6,134},{7,135},{8... | collective-permute-start | bytes 786440 | tf_op jit(solution)/shard_map/ppermute | solution.py:23
  48.7 4.6 %all-to-all-done.1.rows_ref = f32[32,8,128]{2,1,0:T(8,128)S(1)} async-done(((f32[32,8,128]{2,1,0:T(8,128)}), f32[32,8,128]{2,1,0:T(8,128)S(1)}, u32[]{:S(2)}, u32[]{:S(2)}) %all-to-all-start.1) | async-done | bytes 131104 | tf_op jit(solution)/shard_map/all_to_all | solution.py:207
  53.3 1.8 %shard_map.96.refs_0_ = f32[32,256]{1,0:T(8,128)S(1)} custom-call(f32[32,8,128]{2,1,0:T(8,128)S(1)} %all-to-all-done.1.rows_ref, f32[2,256,256]{2,1,0:T(8,128)S(1)} %copy-done.2, f32[2,256,256]{2,1,0:T(8,128)S(1)} %collective-permute-done.2.refs_1_, f32[2,256,256]{2,1,0:T(8,128)S(1)} %collective-permute-done.3.refs_2_, ...), custom_call_target="tpu_custom_call" | custom-call | bytes 3690000 | tf_op jit(solution)/shard_map/pallas_call | solution.py:90
  55.1 0.2 collective-permute-start.5
  55.3 1.3 %collective-permute-start.6 = (f32[32,256]{1,0:T(8,128)S(1)}, f32[32,256]{1,0:T(8,128)S(1)}, u32[]{:S(2)}, u32[]{:S(2)}) collective-permute-start(f32[32,256]{1,0:T(8,128)S(1)} %shard_map.96.refs_0_), channel_id=1, source_target_pairs={{0,32},{1,33},{2,34},{3,35},{4,36},{5,37},{6,38},{7,39},{8,40},{9,... | collective-permute-start | bytes 98312 | tf_op jit(solution)/shard_map/ppermute | solution.py:23
  56.6 2.1 %collective-permute-start.7 = (f32[32,256]{1,0:T(8,128)S(1)}, f32[32,256]{1,0:T(8,128)S(1)}, u32[]{:S(2)}, u32[]{:S(2)}) collective-permute-start(f32[32,256]{1,0:T(8,128)S(1)} %shard_map.96.refs_0_), channel_id=1, source_target_pairs={{0,48},{1,49},{2,50},{3,51},{4,52},{5,53},{6,54},{7,55},{8,56},{9,... | collective-permute-start | bytes 98312 | tf_op jit(solution)/shard_map/ppermute | solution.py:23
  58.7 2.0 %collective-permute-done.9.refs_6_ = bf16[2,256,256]{2,1,0:T(8,128)(2,1)} collective-permute-done((bf16[2,256,256]{2,1,0:T(8,128)(2,1)S(1)}, bf16[2,256,256]{2,1,0:T(8,128)(2,1)}, u32[]{:S(2)}, u32[]{:S(2)}) %collective-permute-start.9) | collective-permute-done | bytes 262176 | tf_op jit(solution)/shard_map/ppermute | solution.py:23
  60.7 0.6 collective-permute-done.7.refs_3_
  61.3 1.4 %shard_map.97 = f32[16,4,256]{2,1,0:T(4,128)S(1)} custom-call(f32[32,256]{1,0:T(8,128)S(1)} %shard_map.96.refs_0_, f32[32,256]{1,0:T(8,128)S(1)} %collective-permute-done.5.refs_1_, f32[32,256]{1,0:T(8,128)S(1)} %collective-permute-done.6.refs_2_, f32[32,256]{1,0:T(8,128)S(1)} %collective-permute-done.7.refs_3_, bf16[2,256,256]{2,1,0:T(8,128)(2,1)S(1)} %copy-done.3, ...), custom_call_target="tpu_custom_call" | custom-call | bytes 3690000 | tf_op jit(solution)/shard_map/pallas_call | solution.py:90
  62.7 18.7 %all_to_all.15.parts_ref = f32[16,4,256]{2,1,0:T(4,128)S(1)} all-to-all(f32[16,4,256]{2,1,0:T(4,128)S(1)} %shard_map.97), channel_id=1, replica_groups=mesh['x'=4,'zl'=4,'z'=2,'y'=4,'c'=2] {'z','y','c'}, dimensions={0} | all-to-all | bytes 131072 | tf_op jit(solution)/shard_map/all_to_all | solution.py:211
  81.5 3.4 %collective-permute-start.11 = (f32[4,256]{1,0:T(4,128)S(1)}, f32[4,256]{1,0:T(4,128)S(1)}, u32[]{:S(2)}, u32[]{:S(2)}) collective-permute-start(f32[4,256]{1,0:T(4,128)S(1)} %shard_map.98), channel_id=1, source_target_pairs={{0,0},{1,16},{2,32},{3,48},{4,4},{5,20},{6,36},{7,52},{8,8},{9,24}... | collective-permute-start | bytes 12296 | tf_op jit(solution)/shard_map/ppermute | solution.py:23
  84.9 1.5 %collective-permute-done.11 = f32[4,256]{1,0:T(4,128)S(1)} collective-permute-done((f32[4,256]{1,0:T(4,128)S(1)}, f32[4,256]{1,0:T(4,128)S(1)}, u32[]{:S(2)}, u32[]{:S(2)}) %collective-permute-start.11) | collective-permute-done | bytes 4128 | tf_op jit(solution)/shard_map/ppermute | solution.py:23
  86.4 0.6 copy.11
  (19 shorter events, 0.1 us)
Async XLA Ops:
  0.0 32.8 %copy-start = (f32[128256]{0:T(1024)S(1)}, f32[128256]{0:T(1024)}, u32[]{:S(2)}) copy-start(f32[128256]{0:T(1024)} %param.13) | copy-start | bytes 1539076
  4.1 12.8 %copy-start.2 = (f32[2,256,256]{2,1,0:T(8,128)S(1)}, f32[2,256,256]{2,1,0:T(8,128)}, u32[]{:S(2)}) copy-start(f32[2,256,256]{2,1,0:T(8,128)} %refs_0_.1) | copy-start | bytes 1572868
  4.1 16.7 %copy-start.3 = (bf16[2,256,256]{2,1,0:T(8,128)(2,1)S(1)}, bf16[2,256,256]{2,1,0:T(8,128)(2,1)}, u32[]{:S(2)}) copy-start(bf16[2,256,256]{2,1,0:T(8,128)(2,1)} %refs_4_.1) | copy-start | bytes 786436
  4.1 7.4 %collective-permute-start = (f32[1024,128]{1,0:T(8,128)}, f32[1024,128]{1,0:T(8,128)S(1)}, u32[]{:S(2)}, u32[]{:S(2)}) collective-permute-start(f32[1024,128]{1,0:T(8,128)} %shard_map.92), channel_id=1, source_target_pairs={{0,1},{1,0},{2,3},{3,2},{4,5},{5,4},{6,7},{7,6},{8,9},{9,8},{10,11... | collective-permute-start | bytes 1572872 | tf_op jit(solution)/shard_map/ppermute | solution.py:23
  7.4 27.1 %copy-start.4 = (s32[4]{0:T(128)S(1)}, s32[4]{0:T(128)}, u32[]{:S(2)}) copy-start(s32[4]{0:T(128)} %length_ref.1) | copy-start | bytes 52
  11.5 1.0 %copy-start.1 = (f32[1024,128]{1,0:T(8,128)S(1)}, f32[1024,128]{1,0:T(8,128)}, u32[]{:S(2)}) copy-start(f32[1024,128]{1,0:T(8,128)} %shard_map.91.a_ref) | copy-start | bytes 1572868
  13.4 12.9 %all-to-all-start = ((f32[4,256,128]{2,1,0:T(8,128)}), f32[4,256,128]{2,1,0:T(8,128)S(1)}, u32[]{:S(2)}, u32[]{:S(2)}) async-start(f32[4,256,128]{2,1,0:T(8,128)} %shard_map.93), calls=%async_computation | async-start | bytes 1048576 | tf_op jit(solution)/shard_map/all_to_all | solution.py:191
  16.9 29.4 %collective-permute-start.2 = (f32[2,256,256]{2,1,0:T(8,128)S(1)}, f32[2,256,256]{2,1,0:T(8,128)S(1)}, u32[]{:S(2)}, u32[]{:S(2)}) collective-permute-start(f32[2,256,256]{2,1,0:T(8,128)S(1)} %copy-done.2), channel_id=1, source_target_pairs={{0,64},{1,65},{2,66},{3,67},{4,68},{5,69},{6,70},{7,71},{8,72},{9,... | collective-permute-start | bytes 1572872 | tf_op jit(solution)/shard_map/ppermute | solution.py:23
  17.1 31.6 %collective-permute-start.3 = (f32[2,256,256]{2,1,0:T(8,128)S(1)}, f32[2,256,256]{2,1,0:T(8,128)S(1)}, u32[]{:S(2)}, u32[]{:S(2)}) collective-permute-start(f32[2,256,256]{2,1,0:T(8,128)S(1)} %copy-done.2), channel_id=1, source_target_pairs={{0,128},{1,129},{2,130},{3,131},{4,132},{5,133},{6,134},{7,135},{8... | collective-permute-start | bytes 1572872 | tf_op jit(solution)/shard_map/ppermute | solution.py:23
  19.6 29.2 %collective-permute-start.4 = (f32[2,256,256]{2,1,0:T(8,128)S(1)}, f32[2,256,256]{2,1,0:T(8,128)S(1)}, u32[]{:S(2)}, u32[]{:S(2)}) collective-permute-start(f32[2,256,256]{2,1,0:T(8,128)S(1)} %copy-done.2), channel_id=1, source_target_pairs={{0,192},{1,193},{2,194},{3,195},{4,196},{5,197},{6,198},{7,199},{8... | collective-permute-start | bytes 1572872 | tf_op jit(solution)/shard_map/ppermute | solution.py:23
  20.9 35.7 %collective-permute-start.10 = (bf16[2,256,256]{2,1,0:T(8,128)(2,1)S(1)}, bf16[2,256,256]{2,1,0:T(8,128)(2,1)}, u32[]{:S(2)}, u32[]{:S(2)}) collective-permute-start(bf16[2,256,256]{2,1,0:T(8,128)(2,1)S(1)} %copy-done.3), channel_id=1, source_target_pairs={{0,192},{1,193},{2,194},{3,195},{4,196},{5,197},{6,198},{7,199},{8... | collective-permute-start | bytes 786440 | tf_op jit(solution)/shard_map/ppermute | solution.py:23
  26.4 8.2 %collective-permute-start.1 = (f32[256,128]{1,0:T(8,128)S(1)}, f32[256,128]{1,0:T(8,128)S(1)}, u32[]{:S(2)}, u32[]{:S(2)}) collective-permute-start(f32[256,128]{1,0:T(8,128)S(1)} %shard_map.94.a_ref), channel_id=1, source_target_pairs={{0,8},{1,9},{2,10},{3,11},{4,12},{5,13},{6,14},{7,15},{8,0},{9,1},... | collective-permute-start | bytes 393224 | tf_op jit(solution)/shard_map/ppermute | solution.py:23
  36.1 17.2 %all-to-all-start.1 = ((f32[32,8,128]{2,1,0:T(8,128)}), f32[32,8,128]{2,1,0:T(8,128)S(1)}, u32[]{:S(2)}, u32[]{:S(2)}) async-start(f32[32,8,128]{2,1,0:T(8,128)} %shard_map.95), calls=%async_computation.1 | async-start | bytes 262144 | tf_op jit(solution)/shard_map/all_to_all | solution.py:207
  45.0 13.7 %collective-permute-start.8 = (bf16[2,256,256]{2,1,0:T(8,128)(2,1)S(1)}, bf16[2,256,256]{2,1,0:T(8,128)(2,1)S(1)}, u32[]{:S(2)}, u32[]{:S(2)}) collective-permute-start(bf16[2,256,256]{2,1,0:T(8,128)(2,1)S(1)} %copy-done.3), channel_id=1, source_target_pairs={{0,64},{1,65},{2,66},{3,67},{4,68},{5,69},{6,70},{7,71},{8,72},{9,... | collective-permute-start | bytes 786440 | tf_op jit(solution)/shard_map/ppermute | solution.py:23
  46.3 14.4 %collective-permute-start.9 = (bf16[2,256,256]{2,1,0:T(8,128)(2,1)S(1)}, bf16[2,256,256]{2,1,0:T(8,128)(2,1)}, u32[]{:S(2)}, u32[]{:S(2)}) collective-permute-start(bf16[2,256,256]{2,1,0:T(8,128)(2,1)S(1)} %copy-done.3), channel_id=1, source_target_pairs={{0,128},{1,129},{2,130},{3,131},{4,132},{5,133},{6,134},{7,135},{8... | collective-permute-start | bytes 786440 | tf_op jit(solution)/shard_map/ppermute | solution.py:23
  55.1 5.6 %collective-permute-start.5 = (f32[32,256]{1,0:T(8,128)S(1)}, f32[32,256]{1,0:T(8,128)S(1)}, u32[]{:S(2)}, u32[]{:S(2)}) collective-permute-start(f32[32,256]{1,0:T(8,128)S(1)} %shard_map.96.refs_0_), channel_id=1, source_target_pairs={{0,16},{1,17},{2,18},{3,19},{4,20},{5,21},{6,22},{7,23},{8,24},{9,... | collective-permute-start | bytes 98312 | tf_op jit(solution)/shard_map/ppermute | solution.py:23
  55.3 5.3 %collective-permute-start.6 = (f32[32,256]{1,0:T(8,128)S(1)}, f32[32,256]{1,0:T(8,128)S(1)}, u32[]{:S(2)}, u32[]{:S(2)}) collective-permute-start(f32[32,256]{1,0:T(8,128)S(1)} %shard_map.96.refs_0_), channel_id=1, source_target_pairs={{0,32},{1,33},{2,34},{3,35},{4,36},{5,37},{6,38},{7,39},{8,40},{9,... | collective-permute-start | bytes 98312 | tf_op jit(solution)/shard_map/ppermute | solution.py:23
  56.6 4.7 %collective-permute-start.7 = (f32[32,256]{1,0:T(8,128)S(1)}, f32[32,256]{1,0:T(8,128)S(1)}, u32[]{:S(2)}, u32[]{:S(2)}) collective-permute-start(f32[32,256]{1,0:T(8,128)S(1)} %shard_map.96.refs_0_), channel_id=1, source_target_pairs={{0,48},{1,49},{2,50},{3,51},{4,52},{5,53},{6,54},{7,55},{8,56},{9,... | collective-permute-start | bytes 98312 | tf_op jit(solution)/shard_map/ppermute | solution.py:23
  81.5 4.9 %collective-permute-start.11 = (f32[4,256]{1,0:T(4,128)S(1)}, f32[4,256]{1,0:T(4,128)S(1)}, u32[]{:S(2)}, u32[]{:S(2)}) collective-permute-start(f32[4,256]{1,0:T(4,128)S(1)} %shard_map.98), channel_id=1, source_target_pairs={{0,0},{1,16},{2,32},{3,48},{4,4},{5,20},{6,36},{7,52},{8,8},{9,24}... | collective-permute-start | bytes 12296 | tf_op jit(solution)/shard_map/ppermute | solution.py:23

commit v3 on v2

--- a/solution.py
+++ b/solution.py
@@ -36,7 +36,7 @@
 
 
 def to_x(value, k):
-    return send(value, lambda d, m: (d ^ (4 * k), m))
+    return send(value, lambda d, m: ((d + 4 * k) % 16, m))
 
 
 def where():
@@ -92,9 +92,11 @@
         in_specs=specs or [VMEM] * len(args),
         out_specs=[VMEM] * len(out),
         out_shape=[jax.ShapeDtypeStruct(s, jnp.float32) for s in out],
-        scratch_shapes=[pltpu.VMEM(s, jnp.float32) for s in scratch],
+        scratch_shapes=[
+            pltpu.VMEM(s, jnp.float32) if isinstance(s, tuple) else s for s in scratch
+        ],
         cost_estimate=cost(us),
-        compiler_params=pltpu.CompilerParams(vmem_limit_bytes=32 * 2**20),
+        compiler_params=pltpu.CompilerParams(vmem_limit_bytes=12 * 2**20),
     )(*args)
 
 
@@ -106,31 +108,46 @@
 
 
 def total_kernel(parts_ref, out):
+    at = 16 * lax.rem(lax.axis_index("y"), 2) + 8 * lax.axis_index("c")
+    out[...] = jnp.sum(parts_ref[pl.ds(at, 8)], axis=0)
+
+
+def half_kernel(parts_ref, out):
     out[...] = jnp.sum(parts_ref[...], axis=0)
 
 
-def gram_kernel(length_ref, a_ref, b_ref, w_ref, out, held):
+def gram_kernel(length_ref, a_ref, b_ref, w_ref, *refs):
+    out, held = refs[-2:]
     x, y = lax.axis_index("x"), lax.axis_index("y")
     total = a_ref[...] + b_ref[...]
     slots = lax.broadcasted_iota(jnp.int32, w_ref.shape, 1)
     weights = jnp.where(slots < length_ref[y], w_ref[...], 0.0)
-    held[...] = jnp.dot(
-        total[:, :64].T * weights,
-        total[:, 64:],
-        precision=lax.Precision.HIGHEST,
-        preferred_element_type=jnp.float32,
-    )
+    inputs = (total[:, :64].T * weights).reshape(32, 2, -1)
+    for odd in range(2):
+        held[:, 64 * odd : 64 * (odd + 1)] = jnp.dot(
+            inputs[:, odd],
+            total[:, 64:],
+            precision=lax.Precision.HIGHEST,
+            preferred_element_type=jnp.float32,
+        )
     for zl in range(4):
-        piece = []
-        for k in range(4):
-            at = (x ^ k) * 16 + zl * 4
-            even = held[pl.ds(at, 2, stride=2)]
-            odd = held[pl.ds(at + 1, 2, stride=2)]
-            piece.append(jnp.concatenate([even, odd], axis=1))
-        piece = jnp.concatenate(piece, axis=0)
+        piece = jnp.concatenate(
+            [held[pl.ds(lax.rem(x + k, 4) * 8 + zl * 2, 2)] for k in (0, 3, 1, 2)], axis=0
+        )
         for core in range(2):
             for y in range(4):
                 out[16 * core + 4 * zl + y] = piece
+
+
+def two_terms(value):
+    high = value.astype(jnp.bfloat16)
+    return high, (value - high.astype(jnp.float32)).astype(jnp.bfloat16)
+
+
+def times(left, right):
+    return lax.dot_general(
+        left, right, (((1,), (1,)), ((), ())), preferred_element_type=jnp.float32
+    )
 
 
 def image_kernel(rows_ref, *refs):
@@ -140,37 +157,40 @@
         total = 0.0
         for k in range(4):
             rows = [rows_ref[at, 2 * k + half, :] for half in range(2)]
-            total = total + lax.dot_general(
-                jnp.concatenate(rows, axis=1),
-                hess[k][layer],
-                (((1,), (1,)), ((), ())),
-                precision=lax.Precision.HIGHEST,
-                preferred_element_type=jnp.float32,
-            )
+            high, low = two_terms(jnp.concatenate(rows, axis=1))
+            right, rest = two_terms(hess[k][layer])
+            both = times(jnp.concatenate([high, low], axis=0), right)
+            total = total + (both[:16] + (both[16:] + times(high, rest)))
         out[at] = total
 
 
 def score_kernel(*refs):
-    images, queries, out = refs[:4], refs[4:8], refs[8]
-    x = lax.axis_index("x")
+    images, queries = refs[:4], refs[4:8]
+    keep, give, held = refs[8:]
+    x, z = lax.axis_index("x"), lax.axis_index("z")
     image = images[0][...] + images[1][...] + images[2][...] + images[3][...]
-    high = image.astype(jnp.bfloat16)
-    rest = image - high.astype(jnp.float32)
-    mid = rest.astype(jnp.bfloat16)
-    low = (rest - mid.astype(jnp.float32)).astype(jnp.bfloat16)
-    for k in range(4):
+    high, low = two_terms(image)
+    for k, step in enumerate((0, 3, 1, 2)):
         part = 0.0
         for layer in range(2):
             at = slice(16 * layer, 16 * (layer + 1))
-            part = part + lax.dot_general(
-                jnp.concatenate([high[at], mid[at], low[at]], axis=0),
-                queries[k][layer],
-                (((1,), (1,)), ((), ())),
-                preferred_element_type=jnp.float32,
+            part = part + times(
+                jnp.concatenate([high[at], low[at]], axis=0), queries[k][layer]
             )
-        part = part[:16] + part[16:32] + part[32:]
+        part = part[:16] + part[16:]
+        block = lax.rem(x + step, 4)
         for zl in range(4):
-            out[4 * (x ^ k) + zl] = part[4 * zl : 4 * zl + 4]
+            held[(block >> 1) ^ z, 4 * (block & 1) + zl] = part[4 * zl : 4 * zl + 4]
+    keep[...] = held[0]
+    give[...] = held[1]
+
+
+def place_kernel(a_ref, b_ref, out):
+    here = lax.axis_index("zl")
+    out[...] = jnp.zeros_like(out)
+    for y in range(2):
+        for zl in range(4):
+            out[8 * zl + 4 * y + here] = a_ref[4 * y + zl] + b_ref[4 * y + zl]
 
 
 def per_device(
@@ -183,8 +203,10 @@
 
     other = project((1 - c)[None], acts, out_grads, proj_in, proj_out)
     theirs = to_core(other)
-    hess = [hess_inv] + [to_x(hess_inv, k) for k in others]
-    query = [queries] + [to_x(queries, k) for k in others]
+    hess = [hess_inv, to_x(hess_inv, 1), to_x(hess_inv, -1)]
+    query = [queries, to_x(queries, 1), to_x(queries, -1)]
+    hess.append(to_x(hess[1], 1))
+    query.append(to_x(query[2], -1))
     mine = project(c[None], acts, out_grads, proj_in, proj_out)
 
     (blocks,) = call(split_kernel, [(4, 256, 128)], mine, theirs)
@@ -193,7 +215,7 @@
     ids = lax.dynamic_index_in_dim(token_ids, y, 0, keepdims=False)
     weights = token_weight.at[ids].get(mode="promise_in_bounds")[None]
 
-    (half,) = call(total_kernel, [(256, 128)], blocks)
+    (half,) = call(half_kernel, [(256, 128)], blocks)
     (grams,) = call(
         gram_kernel,
         [(32, 8, 128)],
@@ -201,16 +223,19 @@
         half,
         to_z(half),
         weights,
-        scratch=[(64, 64)],
+        scratch=[(32, 128)],
         specs=[SMEM] + [VMEM] * 3,
     )
     grams = lax.all_to_all(grams, ("c", "zl", "y"), 0, 0, tiled=True)
     (image,) = call(image_kernel, [(32, 256)], grams, *hess)
     images = [image] + [to_zl(image, k) for k in others]
-    (parts,) = call(score_kernel, [(16, 4, 256)], *images, *query)
-    parts = lax.all_to_all(parts, MP, 0, 0, tiled=True)
+    keep, give = call(
+        score_kernel, [(8, 4, 256)] * 2, *images, *query, scratch=[(2, 8, 4, 256)]
+    )
+    (parts,) = call(place_kernel, [(32, 4, 256)], keep, to_z(give))
+    parts = lax.all_to_all(parts, ("zl", "y", "c"), 0, 0, tiled=True)
     (scores,) = call(total_kernel, [(4, 256)], parts)
-    return send(scores, lambda d, m: (d // 4 * 4 + m % 4, m // 4 * 4 + d % 4))
+    return scores
 
 
 def solution(mesh):

time: 88.3 us -> 86.8 us (0.983); the launches traced: 87 us -> 86.5 us
  blocking collectives: 18.7 us -> 16.3 us
  starting transfers between devices: 37.4 us -> 39 us
  waiting for transfers between devices: 12.9 us -> 14.1 us
    ppermute x12, waiting for transfers between devices: 4.19 us -> 7.38 us  [send(): return lax.ppermute(value, AXES, pairs)]
    all_to_all x1, waiting for transfers between devices: 4.11 us -> 1.21 us  [per_device(): blocks = lax.all_to_all(blocks, 'y', 0, 0, tiled=True)]
    all_to_all x1, blocking collectives: 18.7 us -> 16.3 us  [per_device(): parts = lax.all_to_all(parts, ('zl', 'y', 'c'), 0, 0, tiled=True)]
    ppermute x12, starting transfers between devices: 25.1 us -> 26.2 us  [send(): return lax.ppermute(value, AXES, pairs)]
    all_to_all x1, waiting for transfers between devices: 4.57 us -> 5.56 us  [per_device(): grams = lax.all_to_all(grams, ('c', 'zl', 'y'), 0, 0, tiled=True)]
    pallas_call x6 -> x7, Pallas kernels: 5.68 us -> 5.27 us  [call(): pl.pallas_call(kernel, in_specs=specs or [VMEM] * len(args), out_specs=[V...]
  transfers between devices with their start and end apart: 14 -> 14, of which waited for: 5 -> 6; matrix products, arithmetic and copies ran while one was open for 3% -> 3% of each run, Pallas kernels for 9% -> 8%
where the time goes in v3:
time: 86.8 us; the launch traced here: 86.5 us
  starting transfers between devices  39 us (45%)
  blocking collectives  16.3 us (19%)
  waiting for transfers between devices  14.1 us (16%)
  Pallas kernels  13.5 us (16%)
  local copies, waits for them, and re-layouts  2.78 us (3%)
    ppermute x12, starting transfers between devices, send(): return lax.ppermute(value, AXES, pairs)  26.2 us
    all_to_all x1, blocking collectives, per_device(): parts = lax.all_to_all(parts, ('zl', 'y', 'c'), 0, 0, tiled=True)  16.3 us
    all_to_all x1, starting transfers between devices, per_device(): grams = lax.all_to_all(grams, ('c', 'zl', 'y'), 0, 0, tiled=True)  9.13 us
    pallas_call x2, Pallas kernels, project(): pl.pallas_call(project_kernel, grid_spec=pltpu.PrefetchScalarGridSpec(num...  8.25 us
    ppermute x12, waiting for transfers between devices, send(): return lax.ppermute(value, AXES, pairs)  7.38 us
    all_to_all x1, waiting for transfers between devices, per_device(): grams = lax.all_to_all(grams, ('c', 'zl', 'y'), 0, 0, tiled=True)  5.56 us
    pallas_call x7, Pallas kernels, call(): pl.pallas_call(kernel, in_specs=specs or [VMEM] * len(args), out_specs=[V...  5.27 us
    all_to_all x1, starting transfers between devices, per_device(): blocks = lax.all_to_all(blocks, 'y', 0, 0, tiled=True)  3.65 us
  transfers between devices with their start and end apart: 14, of which 6 were waited for; matrix products, arithmetic and copies ran while one was open for 3% of the time, Pallas kernels for 8%

profile of v3, /device:TPU:1, one launch (start us, length us, event | category | flops | bytes accessed | tf_op | source)
XLA Modules:
  0.0 86.5 jit_solution(11656306458671891471)
XLA Ops:
  0.0 4.2 %shard_map.92 = f32[1024,128]{1,0:T(8,128)} custom-call(s32[1]{0:T(128)} %bitcast.3.layer_ref, bf16[2,1024,512]{2,1,0:T(8,128)(2,1)} %acts_ref.3, bf16[2,1024,1792]{2,1,0:T(8,128)(2,1)} %grads_ref.3, bf16[2,64,512]{2,1,0:T(8,128)(2,1)} %bitcast.11, bf16[2,64,1792]{2,1,0:T(8,128)(2,1)} %bitcast.9), custom_call_target="tpu_custom_call" | custom-call | flops 1207959552 | bytes 4718592 | tf_op jit(solution)/shard_map/pallas_call | solution.py:62
  4.2 3.2 %collective-permute-start = (f32[1024,128]{1,0:T(8,128)}, f32[1024,128]{1,0:T(8,128)S(1)}, u32[]{:S(2)}, u32[]{:S(2)}) collective-permute-start(f32[1024,128]{1,0:T(8,128)} %shard_map.92), channel_id=1, source_target_pairs={{0,1},{1,0},{2,3},{3,2},{4,5},{5,4},{6,7},{7,6},{8,9},{9,8},{10,11... | collective-permute-start | bytes 1572872 | tf_op jit(solution)/shard_map/ppermute | solution.py:23
  7.4 4.1 %shard_map.91.a_ref = f32[1024,128]{1,0:T(8,128)} custom-call(s32[1]{0:T(128)} %bitcast.layer_ref, bf16[2,1024,512]{2,1,0:T(8,128)(2,1)} %acts_ref.3, bf16[2,1024,1792]{2,1,0:T(8,128)(2,1)} %grads_ref.3, bf16[2,64,512]{2,1,0:T(8,128)(2,1)} %bitcast.12, bf16[2,64,1792]{2,1,0:T(8,128)(2,1)} %bitcast.10), custom_call_target="tpu_custom_call" | custom-call | flops 1207959552 | bytes 4718592 | tf_op jit(solution)/shard_map/pallas_call | solution.py:62
  11.5 0.0 collective-permute-done.b_ref
  11.5 1.0 %copy-done.1 = f32[1024,128]{1,0:T(8,128)S(1)} copy-done((f32[1024,128]{1,0:T(8,128)S(1)}, f32[1024,128]{1,0:T(8,128)}, u32[]{:S(2)}) %copy-start.1) | copy-done | bytes 524312
  12.6 0.9 shard_map.93
  13.4 3.6 %all-to-all-start = ((f32[4,256,128]{2,1,0:T(8,128)}), f32[4,256,128]{2,1,0:T(8,128)S(1)}, u32[]{:S(2)}, u32[]{:S(2)}) async-start(f32[4,256,128]{2,1,0:T(8,128)} %shard_map.93), calls=%async_computation | async-start | bytes 1048576 | tf_op jit(solution)/shard_map/all_to_all | solution.py:213
  17.1 2.6 %collective-permute-start.3 = (f32[2,256,256]{2,1,0:T(8,128)S(1)}, f32[2,256,256]{2,1,0:T(8,128)S(1)}, u32[]{:S(2)}, u32[]{:S(2)}) collective-permute-start(f32[2,256,256]{2,1,0:T(8,128)S(1)} %copy-done.2), channel_id=1, source_target_pairs={{0,192},{1,193},{2,194},{3,195},{4,196},{5,197},{6,198},{7,199},{8... | collective-permute-start | bytes 1572872 | tf_op jit(solution)/shard_map/ppermute | solution.py:23
  19.6 2.5 %collective-permute-done.2.refs_1_ = f32[2,256,256]{2,1,0:T(8,128)S(1)} collective-permute-done((f32[2,256,256]{2,1,0:T(8,128)S(1)}, f32[2,256,256]{2,1,0:T(8,128)S(1)}, u32[]{:S(2)}, u32[]{:S(2)}) %collective-permute-start.2) | collective-permute-done | bytes 524320 | tf_op jit(solution)/shard_map/ppermute | solution.py:23
  22.1 0.0 collective-permute-start.4
  22.1 2.7 %collective-permute-start.9 = (bf16[2,256,256]{2,1,0:T(8,128)(2,1)S(1)}, bf16[2,256,256]{2,1,0:T(8,128)(2,1)}, u32[]{:S(2)}, u32[]{:S(2)}) collective-permute-start(bf16[2,256,256]{2,1,0:T(8,128)(2,1)S(1)} %copy-done.3), channel_id=1, source_target_pairs={{0,192},{1,193},{2,194},{3,195},{4,196},{5,197},{6,198},{7,199},{8... | collective-permute-start | bytes 786440 | tf_op jit(solution)/shard_map/ppermute | solution.py:23
  24.8 1.2 %all-to-all-done.parts_ref = f32[4,256,128]{2,1,0:T(8,128)S(1)} async-done(((f32[4,256,128]{2,1,0:T(8,128)}), f32[4,256,128]{2,1,0:T(8,128)S(1)}, u32[]{:S(2)}, u32[]{:S(2)}) %all-to-all-start) | async-done | bytes 524320 | tf_op jit(solution)/shard_map/all_to_all | solution.py:213
  26.0 7.0 %collective-permute-start.1 = (f32[256,128]{1,0:T(8,128)S(1)}, f32[256,128]{1,0:T(8,128)S(1)}, u32[]{:S(2)}, u32[]{:S(2)}) collective-permute-start(f32[256,128]{1,0:T(8,128)S(1)} %shard_map.94.a_ref), channel_id=1, source_target_pairs={{0,8},{1,9},{2,10},{3,11},{4,12},{5,13},{6,14},{7,15},{8,0},{9,1},... | collective-permute-start | bytes 393224 | tf_op jit(solution)/shard_map/ppermute | solution.py:23
  33.0 0.7 compare_select_fusion
  33.7 1.7 %gather_fusion = f32[256]{0:T(256)S(1)} fusion(f32[128256]{0:T(1024)S(1)} %copy-done, s32[1024]{0:T(1024)S(1)} %pad_clamp_fusion), kind=kCustom, calls=%fused_computation | custom fusion | bytes 3072 | tf_op jit(solution)/shard_map/gather | solution.py:216
  35.5 0.0 collective-permute-done.1.b_ref
  35.5 1.6 %shard_map.95 = f32[32,8,128]{2,1,0:T(8,128)} custom-call(s32[4]{0:T(128)S(1)} %copy-done.4, f32[256,128]{1,0:T(8,128)S(1)} %shard_map.94.a_ref, f32[256,128]{1,0:T(8,128)S(1)} %collective-permute-done.1.b_ref, f32[1,256]{1,0:T(1,128)S(1)} %bitcast.8), custom_call_target="tpu_custom_call" | custom-call | bytes 3690000 | tf_op jit(solution)/shard_map/pallas_call | solution.py:90
  37.1 9.1 %all-to-all-start.1 = ((f32[32,8,128]{2,1,0:T(8,128)}), f32[32,8,128]{2,1,0:T(8,128)S(1)}, u32[]{:S(2)}, u32[]{:S(2)}) async-start(f32[32,8,128]{2,1,0:T(8,128)} %shard_map.95), calls=%async_computation.1 | async-start | bytes 262144 | tf_op jit(solution)/shard_map/all_to_all | solution.py:229
  46.3 1.3 %collective-permute-start.8 = (bf16[2,256,256]{2,1,0:T(8,128)(2,1)S(1)}, bf16[2,256,256]{2,1,0:T(8,128)(2,1)S(1)}, u32[]{:S(2)}, u32[]{:S(2)}) collective-permute-start(bf16[2,256,256]{2,1,0:T(8,128)(2,1)S(1)} %copy-done.3), channel_id=1, source_target_pairs={{0,64},{1,65},{2,66},{3,67},{4,68},{5,69},{6,70},{7,71},{8,72},{9,... | collective-permute-start | bytes 786440 | tf_op jit(solution)/shard_map/ppermute | solution.py:23
  47.5 1.5 %collective-permute-start.10 = (bf16[2,256,256]{2,1,0:T(8,128)(2,1)}, bf16[2,256,256]{2,1,0:T(8,128)(2,1)}, u32[]{:S(2)}, u32[]{:S(2)}) collective-permute-start(bf16[2,256,256]{2,1,0:T(8,128)(2,1)} %collective-permute-done.9.refs_6_), channel_id=1, source_target_pairs={{0,192},{1,193},{2,194},{3,195},{4,196},{5,197},{6,198},{7,199},{8... | collective-permute-start | bytes 786440 | tf_op jit(solution)/shard_map/ppermute | solution.py:23
  49.0 5.6 %all-to-all-done.1.rows_ref = f32[32,8,128]{2,1,0:T(8,128)S(1)} async-done(((f32[32,8,128]{2,1,0:T(8,128)}), f32[32,8,128]{2,1,0:T(8,128)S(1)}, u32[]{:S(2)}, u32[]{:S(2)}) %all-to-all-start.1) | async-done | bytes 131104 | tf_op jit(solution)/shard_map/all_to_all | solution.py:229
  54.6 0.7 shard_map.96.refs_0_
  55.3 0.2 collective-permute-start.5
  55.5 1.3 %collective-permute-start.6 = (f32[32,256]{1,0:T(8,128)S(1)}, f32[32,256]{1,0:T(8,128)S(1)}, u32[]{:S(2)}, u32[]{:S(2)}) collective-permute-start(f32[32,256]{1,0:T(8,128)S(1)} %shard_map.96.refs_0_), channel_id=1, source_target_pairs={{0,32},{1,33},{2,34},{3,35},{4,36},{5,37},{6,38},{7,39},{8,40},{9,... | collective-permute-start | bytes 98312 | tf_op jit(solution)/shard_map/ppermute | solution.py:23
  56.8 2.1 %collective-permute-start.7 = (f32[32,256]{1,0:T(8,128)S(1)}, f32[32,256]{1,0:T(8,128)S(1)}, u32[]{:S(2)}, u32[]{:S(2)}) collective-permute-start(f32[32,256]{1,0:T(8,128)S(1)} %shard_map.96.refs_0_), channel_id=1, source_target_pairs={{0,48},{1,49},{2,50},{3,51},{4,52},{5,53},{6,54},{7,55},{8,56},{9,... | collective-permute-start | bytes 98312 | tf_op jit(solution)/shard_map/ppermute | solution.py:23
  58.8 0.3 collective-permute-done.6.refs_2_
  59.2 2.2 %collective-permute-done.7.refs_3_ = f32[32,256]{1,0:T(8,128)S(1)} collective-permute-done((f32[32,256]{1,0:T(8,128)S(1)}, f32[32,256]{1,0:T(8,128)S(1)}, u32[]{:S(2)}, u32[]{:S(2)}) %collective-permute-start.7) | collective-permute-done | bytes 32800 | tf_op jit(solution)/shard_map/ppermute | solution.py:23
  61.4 1.4 %shard_map.97 = (f32[8,4,256]{2,1,0:T(4,128)S(1)}, f32[8,4,256]{2,1,0:T(4,128)S(1)}) custom-call(f32[32,256]{1,0:T(8,128)S(1)} %shard_map.96.refs_0_, f32[32,256]{1,0:T(8,128)S(1)} %collective-permute-done.5.refs_1_, f32[32,256]{1,0:T(8,128)S(1)} %collective-permute-done.6.refs_2_, f32[32,256]{1,0:T(8,128)S(1)} %collective-permute-done.7.refs_3_, ...), custom_call_target="tpu_custom_call" | custom-call | bytes 3690000 | tf_op jit(solution)/shard_map/pallas_call | solution.py:90
  62.8 4.4 %collective-permute-start.11 = (f32[8,4,256]{2,1,0:T(4,128)S(1)}, f32[8,4,256]{2,1,0:T(4,128)S(1)}, u32[]{:S(2)}, u32[]{:S(2)}) collective-permute-start(f32[8,4,256]{2,1,0:T(4,128)S(1)} %get-tuple-element.8), channel_id=1, source_target_pairs={{0,8},{1,9},{2,10},{3,11},{4,12},{5,13},{6,14},{7,15},{8,0},{9,1},... | collective-permute-start | bytes 98312 | tf_op jit(solution)/shard_map/ppermute | solution.py:23
  67.2 2.4 %collective-permute-done.11.b_ref = f32[8,4,256]{2,1,0:T(4,128)S(1)} collective-permute-done((f32[8,4,256]{2,1,0:T(4,128)S(1)}, f32[8,4,256]{2,1,0:T(4,128)S(1)}, u32[]{:S(2)}, u32[]{:S(2)}) %collective-permute-start.11) | collective-permute-done | bytes 32800 | tf_op jit(solution)/shard_map/ppermute | solution.py:23
  69.6 16.3 %all_to_all.15.parts_ref = f32[32,4,256]{2,1,0:T(4,128)S(1)} all-to-all(f32[32,4,256]{2,1,0:T(4,128)S(1)} %shard_map.98), channel_id=1, replica_groups=mesh['x'=4,'zl'=4,'z'=2,'y'=4,'c'=2] {'zl','y','c'}, dimensions={0} | all-to-all | bytes 262144 | tf_op jit(solution)/shard_map/all_to_all | solution.py:236
  85.9 0.6 shard_map.99
  (19 shorter events, 0.1 us)
Async XLA Ops:
  0.0 33.7 %copy-start = (f32[128256]{0:T(1024)S(1)}, f32[128256]{0:T(1024)}, u32[]{:S(2)}) copy-start(f32[128256]{0:T(1024)} %param.13) | copy-start | bytes 1539076
  0.0 7.4 %copy-start.2 = (f32[2,256,256]{2,1,0:T(8,128)S(1)}, f32[2,256,256]{2,1,0:T(8,128)}, u32[]{:S(2)}) copy-start(f32[2,256,256]{2,1,0:T(8,128)} %refs_0_.1) | copy-start | bytes 1572868
  4.2 18.0 %copy-start.3 = (bf16[2,256,256]{2,1,0:T(8,128)(2,1)S(1)}, bf16[2,256,256]{2,1,0:T(8,128)(2,1)}, u32[]{:S(2)}) copy-start(bf16[2,256,256]{2,1,0:T(8,128)(2,1)} %refs_4_.1) | copy-start | bytes 786436
  4.2 7.4 %collective-permute-start = (f32[1024,128]{1,0:T(8,128)}, f32[1024,128]{1,0:T(8,128)S(1)}, u32[]{:S(2)}, u32[]{:S(2)}) collective-permute-start(f32[1024,128]{1,0:T(8,128)} %shard_map.92), channel_id=1, source_target_pairs={{0,1},{1,0},{2,3},{3,2},{4,5},{5,4},{6,7},{7,6},{8,9},{9,8},{10,11... | collective-permute-start | bytes 1572872 | tf_op jit(solution)/shard_map/ppermute | solution.py:23
  7.4 14.7 %collective-permute-start.2 = (f32[2,256,256]{2,1,0:T(8,128)S(1)}, f32[2,256,256]{2,1,0:T(8,128)S(1)}, u32[]{:S(2)}, u32[]{:S(2)}) collective-permute-start(f32[2,256,256]{2,1,0:T(8,128)S(1)} %copy-done.2), channel_id=1, source_target_pairs={{0,64},{1,65},{2,66},{3,67},{4,68},{5,69},{6,70},{7,71},{8,72},{9,... | collective-permute-start | bytes 1572872 | tf_op jit(solution)/shard_map/ppermute | solution.py:23
  7.4 28.1 %copy-start.4 = (s32[4]{0:T(128)S(1)}, s32[4]{0:T(128)}, u32[]{:S(2)}) copy-start(s32[4]{0:T(128)} %length_ref.1) | copy-start | bytes 52
  11.5 1.0 %copy-start.1 = (f32[1024,128]{1,0:T(8,128)S(1)}, f32[1024,128]{1,0:T(8,128)}, u32[]{:S(2)}) copy-start(f32[1024,128]{1,0:T(8,128)} %shard_map.91.a_ref) | copy-start | bytes 1572868
  13.4 12.6 %all-to-all-start = ((f32[4,256,128]{2,1,0:T(8,128)}), f32[4,256,128]{2,1,0:T(8,128)S(1)}, u32[]{:S(2)}, u32[]{:S(2)}) async-start(f32[4,256,128]{2,1,0:T(8,128)} %shard_map.93), calls=%async_computation | async-start | bytes 1048576 | tf_op jit(solution)/shard_map/all_to_all | solution.py:213
  17.1 32.0 %collective-permute-start.3 = (f32[2,256,256]{2,1,0:T(8,128)S(1)}, f32[2,256,256]{2,1,0:T(8,128)S(1)}, u32[]{:S(2)}, u32[]{:S(2)}) collective-permute-start(f32[2,256,256]{2,1,0:T(8,128)S(1)} %copy-done.2), channel_id=1, source_target_pairs={{0,192},{1,193},{2,194},{3,195},{4,196},{5,197},{6,198},{7,199},{8... | collective-permute-start | bytes 1572872 | tf_op jit(solution)/shard_map/ppermute | solution.py:23
  22.1 26.9 %collective-permute-start.4 = (f32[2,256,256]{2,1,0:T(8,128)S(1)}, f32[2,256,256]{2,1,0:T(8,128)S(1)}, u32[]{:S(2)}, u32[]{:S(2)}) collective-permute-start(f32[2,256,256]{2,1,0:T(8,128)S(1)} %collective-permute-done.2.refs_1_), channel_id=1, source_target_pairs={{0,64},{1,65},{2,66},{3,67},{4,68},{5,69},{6,70},{7,71},{8,72},{9,... | collective-permute-start | bytes 1572872 | tf_op jit(solution)/shard_map/ppermute | solution.py:23
  22.1 25.4 %collective-permute-start.9 = (bf16[2,256,256]{2,1,0:T(8,128)(2,1)S(1)}, bf16[2,256,256]{2,1,0:T(8,128)(2,1)}, u32[]{:S(2)}, u32[]{:S(2)}) collective-permute-start(bf16[2,256,256]{2,1,0:T(8,128)(2,1)S(1)} %copy-done.3), channel_id=1, source_target_pairs={{0,192},{1,193},{2,194},{3,195},{4,196},{5,197},{6,198},{7,199},{8... | collective-permute-start | bytes 786440 | tf_op jit(solution)/shard_map/ppermute | solution.py:23
  26.0 9.5 %collective-permute-start.1 = (f32[256,128]{1,0:T(8,128)S(1)}, f32[256,128]{1,0:T(8,128)S(1)}, u32[]{:S(2)}, u32[]{:S(2)}) collective-permute-start(f32[256,128]{1,0:T(8,128)S(1)} %shard_map.94.a_ref), channel_id=1, source_target_pairs={{0,8},{1,9},{2,10},{3,11},{4,12},{5,13},{6,14},{7,15},{8,0},{9,1},... | collective-permute-start | bytes 393224 | tf_op jit(solution)/shard_map/ppermute | solution.py:23
  37.1 17.5 %all-to-all-start.1 = ((f32[32,8,128]{2,1,0:T(8,128)}), f32[32,8,128]{2,1,0:T(8,128)S(1)}, u32[]{:S(2)}, u32[]{:S(2)}) async-start(f32[32,8,128]{2,1,0:T(8,128)} %shard_map.95), calls=%async_computation.1 | async-start | bytes 262144 | tf_op jit(solution)/shard_map/all_to_all | solution.py:229
  46.3 12.6 %collective-permute-start.8 = (bf16[2,256,256]{2,1,0:T(8,128)(2,1)S(1)}, bf16[2,256,256]{2,1,0:T(8,128)(2,1)S(1)}, u32[]{:S(2)}, u32[]{:S(2)}) collective-permute-start(bf16[2,256,256]{2,1,0:T(8,128)(2,1)S(1)} %copy-done.3), channel_id=1, source_target_pairs={{0,64},{1,65},{2,66},{3,67},{4,68},{5,69},{6,70},{7,71},{8,72},{9,... | collective-permute-start | bytes 786440 | tf_op jit(solution)/shard_map/ppermute | solution.py:23
  47.5 11.3 %collective-permute-start.10 = (bf16[2,256,256]{2,1,0:T(8,128)(2,1)}, bf16[2,256,256]{2,1,0:T(8,128)(2,1)}, u32[]{:S(2)}, u32[]{:S(2)}) collective-permute-start(bf16[2,256,256]{2,1,0:T(8,128)(2,1)} %collective-permute-done.9.refs_6_), channel_id=1, source_target_pairs={{0,192},{1,193},{2,194},{3,195},{4,196},{5,197},{6,198},{7,199},{8... | collective-permute-start | bytes 786440 | tf_op jit(solution)/shard_map/ppermute | solution.py:23
  55.3 3.6 %collective-permute-start.5 = (f32[32,256]{1,0:T(8,128)S(1)}, f32[32,256]{1,0:T(8,128)S(1)}, u32[]{:S(2)}, u32[]{:S(2)}) collective-permute-start(f32[32,256]{1,0:T(8,128)S(1)} %shard_map.96.refs_0_), channel_id=1, source_target_pairs={{0,16},{1,17},{2,18},{3,19},{4,20},{5,21},{6,22},{7,23},{8,24},{9,... | collective-permute-start | bytes 98312 | tf_op jit(solution)/shard_map/ppermute | solution.py:23
  55.5 3.7 %collective-permute-start.6 = (f32[32,256]{1,0:T(8,128)S(1)}, f32[32,256]{1,0:T(8,128)S(1)}, u32[]{:S(2)}, u32[]{:S(2)}) collective-permute-start(f32[32,256]{1,0:T(8,128)S(1)} %shard_map.96.refs_0_), channel_id=1, source_target_pairs={{0,32},{1,33},{2,34},{3,35},{4,36},{5,37},{6,38},{7,39},{8,40},{9,... | collective-permute-start | bytes 98312 | tf_op jit(solution)/shard_map/ppermute | solution.py:23
  56.8 4.6 %collective-permute-start.7 = (f32[32,256]{1,0:T(8,128)S(1)}, f32[32,256]{1,0:T(8,128)S(1)}, u32[]{:S(2)}, u32[]{:S(2)}) collective-permute-start(f32[32,256]{1,0:T(8,128)S(1)} %shard_map.96.refs_0_), channel_id=1, source_target_pairs={{0,48},{1,49},{2,50},{3,51},{4,52},{5,53},{6,54},{7,55},{8,56},{9,... | collective-permute-start | bytes 98312 | tf_op jit(solution)/shard_map/ppermute | solution.py:23
  62.8 6.8 %collective-permute-start.11 = (f32[8,4,256]{2,1,0:T(4,128)S(1)}, f32[8,4,256]{2,1,0:T(4,128)S(1)}, u32[]{:S(2)}, u32[]{:S(2)}) collective-permute-start(f32[8,4,256]{2,1,0:T(4,128)S(1)} %get-tuple-element.8), channel_id=1, source_target_pairs={{0,8},{1,9},{2,10},{3,11},{4,12},{5,13},{6,14},{7,15},{8,0},{9,1},... | collective-permute-start | bytes 98312 | tf_op jit(solution)/shard_map/ppermute | solution.py:23

commit v4 on v3

--- a/solution.py
+++ b/solution.py
@@ -165,9 +165,8 @@
 
 
 def score_kernel(*refs):
-    images, queries = refs[:4], refs[4:8]
-    keep, give, held = refs[8:]
-    x, z = lax.axis_index("x"), lax.axis_index("z")
+    images, queries, out = refs[:4], refs[4:8], refs[8]
+    x = lax.axis_index("x")
     image = images[0][...] + images[1][...] + images[2][...] + images[3][...]
     high, low = two_terms(image)
     for k, step in enumerate((0, 3, 1, 2)):
@@ -178,19 +177,16 @@
                 jnp.concatenate([high[at], low[at]], axis=0), queries[k][layer]
             )
         part = part[:16] + part[16:]
-        block = lax.rem(x + step, 4)
         for zl in range(4):
-            held[(block >> 1) ^ z, 4 * (block & 1) + zl] = part[4 * zl : 4 * zl + 4]
-    keep[...] = held[0]
-    give[...] = held[1]
+            out[4 * lax.rem(x + step, 4) + zl] = part[4 * zl : 4 * zl + 4]
 
 
 def place_kernel(a_ref, b_ref, out):
-    here = lax.axis_index("zl")
+    here = lax.axis_index("zl") >> 1
     out[...] = jnp.zeros_like(out)
-    for y in range(2):
+    for block in range(4):
         for zl in range(4):
-            out[8 * zl + 4 * y + here] = a_ref[4 * y + zl] + b_ref[4 * y + zl]
+            out[8 * zl + 2 * block + here] = a_ref[4 * block + zl] + b_ref[4 * block + zl]
 
 
 def per_device(
@@ -229,11 +225,9 @@
     grams = lax.all_to_all(grams, ("c", "zl", "y"), 0, 0, tiled=True)
     (image,) = call(image_kernel, [(32, 256)], grams, *hess)
     images = [image] + [to_zl(image, k) for k in others]
-    keep, give = call(
-        score_kernel, [(8, 4, 256)] * 2, *images, *query, scratch=[(2, 8, 4, 256)]
-    )
-    (parts,) = call(place_kernel, [(32, 4, 256)], keep, to_z(give))
-    parts = lax.all_to_all(parts, ("zl", "y", "c"), 0, 0, tiled=True)
+    (parts,) = call(score_kernel, [(16, 4, 256)], *images, *query)
+    (parts,) = call(place_kernel, [(32, 4, 256)], parts, to_core(parts))
+    parts = lax.all_to_all(parts, ("zl", "z", "y"), 0, 0, tiled=True)
     (scores,) = call(total_kernel, [(4, 256)], parts)
     return scores
 

time: 86.8 us -> 83.4 us (0.961)
  starting transfers between devices: 39 us -> 36.7 us
  waiting for transfers between devices: 14.1 us -> 12.7 us
    ppermute x12, starting transfers between devices: 26.2 us -> 23.9 us  [send(): return lax.ppermute(value, AXES, pairs)]
    ppermute x12, waiting for transfers between devices: 7.38 us -> 5.93 us  [send(): return lax.ppermute(value, AXES, pairs)]
  transfers between devices with their start and end apart: 14 -> 14, of which waited for: 6 -> 6; matrix products, arithmetic and copies ran while one was open for 3% -> 3% of each run, Pallas kernels for 8% -> 9%
where the time goes in v4:
time: 83.4 us; the launch traced here: 82.5 us
  starting transfers between devices  36.7 us (44%)
  blocking collectives  16.1 us (19%)
  Pallas kernels  13.5 us (16%)
  waiting for transfers between devices  12.7 us (15%)
  local copies, waits for them, and re-layouts  2.78 us (3%)
    ppermute x12, starting transfers between devices, send(): return lax.ppermute(value, AXES, pairs)  23.9 us
    all_to_all x1, blocking collectives, per_device(): parts = lax.all_to_all(parts, ('zl', 'z', 'y'), 0, 0, tiled=True)  16.1 us
    all_to_all x1, starting transfers between devices, per_device(): grams = lax.all_to_all(grams, ('c', 'zl', 'y'), 0, 0, tiled=True)  9.13 us
    pallas_call x2, Pallas kernels, project(): pl.pallas_call(project_kernel, grid_spec=pltpu.PrefetchScalarGridSpec(num...  8.26 us
    ppermute x12, waiting for transfers between devices, send(): return lax.ppermute(value, AXES, pairs)  5.93 us
    all_to_all x1, waiting for transfers between devices, per_device(): grams = lax.all_to_all(grams, ('c', 'zl', 'y'), 0, 0, tiled=True)  5.56 us
    pallas_call x7, Pallas kernels, call(): pl.pallas_call(kernel, in_specs=specs or [VMEM] * len(args), out_specs=[V...  5.24 us
    all_to_all x1, starting transfers between devices, per_device(): blocks = lax.all_to_all(blocks, 'y', 0, 0, tiled=True)  3.65 us
  transfers between devices with their start and end apart: 14, of which 6 were waited for; matrix products, arithmetic and copies ran while one was open for 3% of the time, Pallas kernels for 9%

profile of v4, /device:TPU:1, one launch (start us, length us, event | category | flops | bytes accessed | tf_op | source)
XLA Modules:
  0.0 82.5 jit_solution(13687708254963107380)
XLA Ops:
  0.0 4.2 %shard_map.92 = f32[1024,128]{1,0:T(8,128)} custom-call(s32[1]{0:T(128)} %bitcast.3.layer_ref, bf16[2,1024,512]{2,1,0:T(8,128)(2,1)} %acts_ref.3, bf16[2,1024,1792]{2,1,0:T(8,128)(2,1)} %grads_ref.3, bf16[2,64,512]{2,1,0:T(8,128)(2,1)} %bitcast.11, bf16[2,64,1792]{2,1,0:T(8,128)(2,1)} %bitcast.9), custom_call_target="tpu_custom_call" | custom-call | flops 1207959552 | bytes 4718592 | tf_op jit(solution)/shard_map/pallas_call | solution.py:62
  4.2 3.2 %collective-permute-start = (f32[1024,128]{1,0:T(8,128)}, f32[1024,128]{1,0:T(8,128)S(1)}, u32[]{:S(2)}, u32[]{:S(2)}) collective-permute-start(f32[1024,128]{1,0:T(8,128)} %shard_map.92), channel_id=1, source_target_pairs={{0,1},{1,0},{2,3},{3,2},{4,5},{5,4},{6,7},{7,6},{8,9},{9,8},{10,11... | collective-permute-start | bytes 1572872 | tf_op jit(solution)/shard_map/ppermute | solution.py:23
  7.4 0.0 collective-permute-start.2
  7.4 4.1 %shard_map.91.a_ref = f32[1024,128]{1,0:T(8,128)} custom-call(s32[1]{0:T(128)} %bitcast.layer_ref, bf16[2,1024,512]{2,1,0:T(8,128)(2,1)} %acts_ref.3, bf16[2,1024,1792]{2,1,0:T(8,128)(2,1)} %grads_ref.3, bf16[2,64,512]{2,1,0:T(8,128)(2,1)} %bitcast.12, bf16[2,64,1792]{2,1,0:T(8,128)(2,1)} %bitcast.10), custom_call_target="tpu_custom_call" | custom-call | flops 1207959552 | bytes 4718592 | tf_op jit(solution)/shard_map/pallas_call | solution.py:62
  11.5 0.0 collective-permute-done.b_ref
  11.5 1.0 %copy-done.1 = f32[1024,128]{1,0:T(8,128)S(1)} copy-done((f32[1024,128]{1,0:T(8,128)S(1)}, f32[1024,128]{1,0:T(8,128)}, u32[]{:S(2)}) %copy-start.1) | copy-done | bytes 524312
  12.6 0.8 %shard_map.93 = f32[4,256,128]{2,1,0:T(8,128)} custom-call(f32[1024,128]{1,0:T(8,128)S(1)} %copy-done.1, f32[1024,128]{1,0:T(8,128)S(1)} %collective-permute-done.b_ref), custom_call_target="tpu_custom_call" | custom-call | bytes 3690000 | tf_op jit(solution)/shard_map/pallas_call | solution.py:90
  13.4 3.6 %all-to-all-start = ((f32[4,256,128]{2,1,0:T(8,128)}), f32[4,256,128]{2,1,0:T(8,128)S(1)}, u32[]{:S(2)}, u32[]{:S(2)}) async-start(f32[4,256,128]{2,1,0:T(8,128)} %shard_map.93), calls=%async_computation | async-start | bytes 1048576 | tf_op jit(solution)/shard_map/all_to_all | solution.py:209
  17.1 2.6 %collective-permute-start.3 = (f32[2,256,256]{2,1,0:T(8,128)S(1)}, f32[2,256,256]{2,1,0:T(8,128)S(1)}, u32[]{:S(2)}, u32[]{:S(2)}) collective-permute-start(f32[2,256,256]{2,1,0:T(8,128)S(1)} %copy-done.2), channel_id=1, source_target_pairs={{0,192},{1,193},{2,194},{3,195},{4,196},{5,197},{6,198},{7,199},{8... | collective-permute-start | bytes 1572872 | tf_op jit(solution)/shard_map/ppermute | solution.py:23
  19.6 2.5 %collective-permute-done.2.refs_1_ = f32[2,256,256]{2,1,0:T(8,128)S(1)} collective-permute-done((f32[2,256,256]{2,1,0:T(8,128)S(1)}, f32[2,256,256]{2,1,0:T(8,128)S(1)}, u32[]{:S(2)}, u32[]{:S(2)}) %collective-permute-start.2) | collective-permute-done | bytes 524320 | tf_op jit(solution)/shard_map/ppermute | solution.py:23
  22.1 2.7 %collective-permute-start.9 = (bf16[2,256,256]{2,1,0:T(8,128)(2,1)S(1)}, bf16[2,256,256]{2,1,0:T(8,128)(2,1)}, u32[]{:S(2)}, u32[]{:S(2)}) collective-permute-start(bf16[2,256,256]{2,1,0:T(8,128)(2,1)S(1)} %copy-done.3), channel_id=1, source_target_pairs={{0,192},{1,193},{2,194},{3,195},{4,196},{5,197},{6,198},{7,199},{8... | collective-permute-start | bytes 786440 | tf_op jit(solution)/shard_map/ppermute | solution.py:23
  24.8 1.2 %all-to-all-done.parts_ref = f32[4,256,128]{2,1,0:T(8,128)S(1)} async-done(((f32[4,256,128]{2,1,0:T(8,128)}), f32[4,256,128]{2,1,0:T(8,128)S(1)}, u32[]{:S(2)}, u32[]{:S(2)}) %all-to-all-start) | async-done | bytes 524320 | tf_op jit(solution)/shard_map/all_to_all | solution.py:209
  26.0 7.0 %collective-permute-start.1 = (f32[256,128]{1,0:T(8,128)S(1)}, f32[256,128]{1,0:T(8,128)S(1)}, u32[]{:S(2)}, u32[]{:S(2)}) collective-permute-start(f32[256,128]{1,0:T(8,128)S(1)} %shard_map.94.a_ref), channel_id=1, source_target_pairs={{0,8},{1,9},{2,10},{3,11},{4,12},{5,13},{6,14},{7,15},{8,0},{9,1},... | collective-permute-start | bytes 393224 | tf_op jit(solution)/shard_map/ppermute | solution.py:23
  33.0 0.7 compare_select_fusion
  33.7 1.7 %gather_fusion = f32[256]{0:T(256)S(1)} fusion(f32[128256]{0:T(1024)S(1)} %copy-done, s32[1024]{0:T(1024)S(1)} %pad_clamp_fusion), kind=kCustom, calls=%fused_computation | custom fusion | bytes 3072 | tf_op jit(solution)/shard_map/gather | solution.py:212
  35.4 0.0 collective-permute-done.1.b_ref
  35.5 1.6 %shard_map.95 = f32[32,8,128]{2,1,0:T(8,128)} custom-call(s32[4]{0:T(128)S(1)} %copy-done.4, f32[256,128]{1,0:T(8,128)S(1)} %shard_map.94.a_ref, f32[256,128]{1,0:T(8,128)S(1)} %collective-permute-done.1.b_ref, f32[1,256]{1,0:T(1,128)S(1)} %bitcast.8), custom_call_target="tpu_custom_call" | custom-call | bytes 3690000 | tf_op jit(solution)/shard_map/pallas_call | solution.py:90
  37.1 9.1 %all-to-all-start.1 = ((f32[32,8,128]{2,1,0:T(8,128)}), f32[32,8,128]{2,1,0:T(8,128)S(1)}, u32[]{:S(2)}, u32[]{:S(2)}) async-start(f32[32,8,128]{2,1,0:T(8,128)} %shard_map.95), calls=%async_computation.1 | async-start | bytes 262144 | tf_op jit(solution)/shard_map/all_to_all | solution.py:225
  46.2 1.3 %collective-permute-start.8 = (bf16[2,256,256]{2,1,0:T(8,128)(2,1)S(1)}, bf16[2,256,256]{2,1,0:T(8,128)(2,1)S(1)}, u32[]{:S(2)}, u32[]{:S(2)}) collective-permute-start(bf16[2,256,256]{2,1,0:T(8,128)(2,1)S(1)} %copy-done.3), channel_id=1, source_target_pairs={{0,64},{1,65},{2,66},{3,67},{4,68},{5,69},{6,70},{7,71},{8,72},{9,... | collective-permute-start | bytes 786440 | tf_op jit(solution)/shard_map/ppermute | solution.py:23
  47.5 1.5 %collective-permute-start.10 = (bf16[2,256,256]{2,1,0:T(8,128)(2,1)}, bf16[2,256,256]{2,1,0:T(8,128)(2,1)}, u32[]{:S(2)}, u32[]{:S(2)}) collective-permute-start(bf16[2,256,256]{2,1,0:T(8,128)(2,1)} %collective-permute-done.9.refs_6_), channel_id=1, source_target_pairs={{0,192},{1,193},{2,194},{3,195},{4,196},{5,197},{6,198},{7,199},{8... | collective-permute-start | bytes 786440 | tf_op jit(solution)/shard_map/ppermute | solution.py:23
  49.0 5.6 %all-to-all-done.1.rows_ref = f32[32,8,128]{2,1,0:T(8,128)S(1)} async-done(((f32[32,8,128]{2,1,0:T(8,128)}), f32[32,8,128]{2,1,0:T(8,128)S(1)}, u32[]{:S(2)}, u32[]{:S(2)}) %all-to-all-start.1) | async-done | bytes 131104 | tf_op jit(solution)/shard_map/all_to_all | solution.py:225
  54.6 0.7 shard_map.96.refs_0_
  55.3 0.2 collective-permute-start.5
  55.5 1.3 %collective-permute-start.6 = (f32[32,256]{1,0:T(8,128)S(1)}, f32[32,256]{1,0:T(8,128)S(1)}, u32[]{:S(2)}, u32[]{:S(2)}) collective-permute-start(f32[32,256]{1,0:T(8,128)S(1)} %shard_map.96.refs_0_), channel_id=1, source_target_pairs={{0,32},{1,33},{2,34},{3,35},{4,36},{5,37},{6,38},{7,39},{8,40},{9,... | collective-permute-start | bytes 98312 | tf_op jit(solution)/shard_map/ppermute | solution.py:23
  56.8 2.1 %collective-permute-start.7 = (f32[32,256]{1,0:T(8,128)S(1)}, f32[32,256]{1,0:T(8,128)S(1)}, u32[]{:S(2)}, u32[]{:S(2)}) collective-permute-start(f32[32,256]{1,0:T(8,128)S(1)} %shard_map.96.refs_0_), channel_id=1, source_target_pairs={{0,48},{1,49},{2,50},{3,51},{4,52},{5,53},{6,54},{7,55},{8,56},{9,... | collective-permute-start | bytes 98312 | tf_op jit(solution)/shard_map/ppermute | solution.py:23
  58.8 0.3 collective-permute-done.6.refs_2_
  59.2 2.2 %collective-permute-done.7.refs_3_ = f32[32,256]{1,0:T(8,128)S(1)} collective-permute-done((f32[32,256]{1,0:T(8,128)S(1)}, f32[32,256]{1,0:T(8,128)S(1)}, u32[]{:S(2)}, u32[]{:S(2)}) %collective-permute-start.7) | collective-permute-done | bytes 32800 | tf_op jit(solution)/shard_map/ppermute | solution.py:23
  61.3 1.4 %shard_map.97.a_ref = f32[16,4,256]{2,1,0:T(4,128)S(1)} custom-call(f32[32,256]{1,0:T(8,128)S(1)} %shard_map.96.refs_0_, f32[32,256]{1,0:T(8,128)S(1)} %collective-permute-done.5.refs_1_, f32[32,256]{1,0:T(8,128)S(1)} %collective-permute-done.6.refs_2_, f32[32,256]{1,0:T(8,128)S(1)} %collective-permute-done.7.refs_3_, bf16[2,256,256]{2,1,0:T(8,128)(2,1)S(1)} %copy-done.3, ...), custom_call_target="tpu_custom_call" | custom-call | bytes 3690000 | tf_op jit(solution)/shard_map/pallas_call | solution.py:90
  62.8 2.1 %collective-permute-start.11 = (f32[16,4,256]{2,1,0:T(4,128)S(1)}, f32[16,4,256]{2,1,0:T(4,128)S(1)}, u32[]{:S(2)}, u32[]{:S(2)}) collective-permute-start(f32[16,4,256]{2,1,0:T(4,128)S(1)} %shard_map.97.a_ref), channel_id=1, source_target_pairs={{0,1},{1,0},{2,3},{3,2},{4,5},{5,4},{6,7},{7,6},{8,9},{9,8},{10,11... | collective-permute-start | bytes 196616 | tf_op jit(solution)/shard_map/ppermute | solution.py:23
  64.9 0.9 %collective-permute-done.11.b_ref = f32[16,4,256]{2,1,0:T(4,128)S(1)} collective-permute-done((f32[16,4,256]{2,1,0:T(4,128)S(1)}, f32[16,4,256]{2,1,0:T(4,128)S(1)}, u32[]{:S(2)}, u32[]{:S(2)}) %collective-permute-start.11) | collective-permute-done | bytes 65568 | tf_op jit(solution)/shard_map/ppermute | solution.py:23
  65.8 16.1 %all_to_all.15.parts_ref = f32[32,4,256]{2,1,0:T(4,128)S(1)} all-to-all(f32[32,4,256]{2,1,0:T(4,128)S(1)} %shard_map.98), channel_id=1, replica_groups=mesh['x'=4,'zl'=4,'z'=2,'y'=4,'c'=2] {'zl','z','y'}, dimensions={0} | all-to-all | bytes 262144 | tf_op jit(solution)/shard_map/all_to_all | solution.py:230
  81.9 0.6 shard_map.99
  (19 shorter events, 0.1 us)
Async XLA Ops:
  0.0 33.7 %copy-start = (f32[128256]{0:T(1024)S(1)}, f32[128256]{0:T(1024)}, u32[]{:S(2)}) copy-start(f32[128256]{0:T(1024)} %param.13) | copy-start | bytes 1539076
  0.0 7.4 %copy-start.2 = (f32[2,256,256]{2,1,0:T(8,128)S(1)}, f32[2,256,256]{2,1,0:T(8,128)}, u32[]{:S(2)}) copy-start(f32[2,256,256]{2,1,0:T(8,128)} %refs_0_.1) | copy-start | bytes 1572868
  4.2 18.0 %copy-start.3 = (bf16[2,256,256]{2,1,0:T(8,128)(2,1)S(1)}, bf16[2,256,256]{2,1,0:T(8,128)(2,1)}, u32[]{:S(2)}) copy-start(bf16[2,256,256]{2,1,0:T(8,128)(2,1)} %refs_4_.1) | copy-start | bytes 786436
  4.2 7.4 %collective-permute-start = (f32[1024,128]{1,0:T(8,128)}, f32[1024,128]{1,0:T(8,128)S(1)}, u32[]{:S(2)}, u32[]{:S(2)}) collective-permute-start(f32[1024,128]{1,0:T(8,128)} %shard_map.92), channel_id=1, source_target_pairs={{0,1},{1,0},{2,3},{3,2},{4,5},{5,4},{6,7},{7,6},{8,9},{9,8},{10,11... | collective-permute-start | bytes 1572872 | tf_op jit(solution)/shard_map/ppermute | solution.py:23
  7.4 14.7 %collective-permute-start.2 = (f32[2,256,256]{2,1,0:T(8,128)S(1)}, f32[2,256,256]{2,1,0:T(8,128)S(1)}, u32[]{:S(2)}, u32[]{:S(2)}) collective-permute-start(f32[2,256,256]{2,1,0:T(8,128)S(1)} %copy-done.2), channel_id=1, source_target_pairs={{0,64},{1,65},{2,66},{3,67},{4,68},{5,69},{6,70},{7,71},{8,72},{9,... | collective-permute-start | bytes 1572872 | tf_op jit(solution)/shard_map/ppermute | solution.py:23
  7.4 28.1 %copy-start.4 = (s32[4]{0:T(128)S(1)}, s32[4]{0:T(128)}, u32[]{:S(2)}) copy-start(s32[4]{0:T(128)} %length_ref.1) | copy-start | bytes 52
  11.5 1.0 %copy-start.1 = (f32[1024,128]{1,0:T(8,128)S(1)}, f32[1024,128]{1,0:T(8,128)}, u32[]{:S(2)}) copy-start(f32[1024,128]{1,0:T(8,128)} %shard_map.91.a_ref) | copy-start | bytes 1572868
  13.4 12.6 %all-to-all-start = ((f32[4,256,128]{2,1,0:T(8,128)}), f32[4,256,128]{2,1,0:T(8,128)S(1)}, u32[]{:S(2)}, u32[]{:S(2)}) async-start(f32[4,256,128]{2,1,0:T(8,128)} %shard_map.93), calls=%async_computation | async-start | bytes 1048576 | tf_op jit(solution)/shard_map/all_to_all | solution.py:209
  17.1 31.9 %collective-permute-start.3 = (f32[2,256,256]{2,1,0:T(8,128)S(1)}, f32[2,256,256]{2,1,0:T(8,128)S(1)}, u32[]{:S(2)}, u32[]{:S(2)}) collective-permute-start(f32[2,256,256]{2,1,0:T(8,128)S(1)} %copy-done.2), channel_id=1, source_target_pairs={{0,192},{1,193},{2,194},{3,195},{4,196},{5,197},{6,198},{7,199},{8... | collective-permute-start | bytes 1572872 | tf_op jit(solution)/shard_map/ppermute | solution.py:23
  22.1 26.9 %collective-permute-start.4 = (f32[2,256,256]{2,1,0:T(8,128)S(1)}, f32[2,256,256]{2,1,0:T(8,128)S(1)}, u32[]{:S(2)}, u32[]{:S(2)}) collective-permute-start(f32[2,256,256]{2,1,0:T(8,128)S(1)} %collective-permute-done.2.refs_1_), channel_id=1, source_target_pairs={{0,64},{1,65},{2,66},{3,67},{4,68},{5,69},{6,70},{7,71},{8,72},{9,... | collective-permute-start | bytes 1572872 | tf_op jit(solution)/shard_map/ppermute | solution.py:23
  22.1 25.4 %collective-permute-start.9 = (bf16[2,256,256]{2,1,0:T(8,128)(2,1)S(1)}, bf16[2,256,256]{2,1,0:T(8,128)(2,1)}, u32[]{:S(2)}, u32[]{:S(2)}) collective-permute-start(bf16[2,256,256]{2,1,0:T(8,128)(2,1)S(1)} %copy-done.3), channel_id=1, source_target_pairs={{0,192},{1,193},{2,194},{3,195},{4,196},{5,197},{6,198},{7,199},{8... | collective-permute-start | bytes 786440 | tf_op jit(solution)/shard_map/ppermute | solution.py:23
  26.0 9.4 %collective-permute-start.1 = (f32[256,128]{1,0:T(8,128)S(1)}, f32[256,128]{1,0:T(8,128)S(1)}, u32[]{:S(2)}, u32[]{:S(2)}) collective-permute-start(f32[256,128]{1,0:T(8,128)S(1)} %shard_map.94.a_ref), channel_id=1, source_target_pairs={{0,8},{1,9},{2,10},{3,11},{4,12},{5,13},{6,14},{7,15},{8,0},{9,1},... | collective-permute-start | bytes 393224 | tf_op jit(solution)/shard_map/ppermute | solution.py:23
  37.1 17.5 %all-to-all-start.1 = ((f32[32,8,128]{2,1,0:T(8,128)}), f32[32,8,128]{2,1,0:T(8,128)S(1)}, u32[]{:S(2)}, u32[]{:S(2)}) async-start(f32[32,8,128]{2,1,0:T(8,128)} %shard_map.95), calls=%async_computation.1 | async-start | bytes 262144 | tf_op jit(solution)/shard_map/all_to_all | solution.py:225
  46.2 12.6 %collective-permute-start.8 = (bf16[2,256,256]{2,1,0:T(8,128)(2,1)S(1)}, bf16[2,256,256]{2,1,0:T(8,128)(2,1)S(1)}, u32[]{:S(2)}, u32[]{:S(2)}) collective-permute-start(bf16[2,256,256]{2,1,0:T(8,128)(2,1)S(1)} %copy-done.3), channel_id=1, source_target_pairs={{0,64},{1,65},{2,66},{3,67},{4,68},{5,69},{6,70},{7,71},{8,72},{9,... | collective-permute-start | bytes 786440 | tf_op jit(solution)/shard_map/ppermute | solution.py:23
  47.5 11.3 %collective-permute-start.10 = (bf16[2,256,256]{2,1,0:T(8,128)(2,1)}, bf16[2,256,256]{2,1,0:T(8,128)(2,1)}, u32[]{:S(2)}, u32[]{:S(2)}) collective-permute-start(bf16[2,256,256]{2,1,0:T(8,128)(2,1)} %collective-permute-done.9.refs_6_), channel_id=1, source_target_pairs={{0,192},{1,193},{2,194},{3,195},{4,196},{5,197},{6,198},{7,199},{8... | collective-permute-start | bytes 786440 | tf_op jit(solution)/shard_map/ppermute | solution.py:23
  55.3 3.6 %collective-permute-start.5 = (f32[32,256]{1,0:T(8,128)S(1)}, f32[32,256]{1,0:T(8,128)S(1)}, u32[]{:S(2)}, u32[]{:S(2)}) collective-permute-start(f32[32,256]{1,0:T(8,128)S(1)} %shard_map.96.refs_0_), channel_id=1, source_target_pairs={{0,16},{1,17},{2,18},{3,19},{4,20},{5,21},{6,22},{7,23},{8,24},{9,... | collective-permute-start | bytes 98312 | tf_op jit(solution)/shard_map/ppermute | solution.py:23
  55.5 3.7 %collective-permute-start.6 = (f32[32,256]{1,0:T(8,128)S(1)}, f32[32,256]{1,0:T(8,128)S(1)}, u32[]{:S(2)}, u32[]{:S(2)}) collective-permute-start(f32[32,256]{1,0:T(8,128)S(1)} %shard_map.96.refs_0_), channel_id=1, source_target_pairs={{0,32},{1,33},{2,34},{3,35},{4,36},{5,37},{6,38},{7,39},{8,40},{9,... | collective-permute-start | bytes 98312 | tf_op jit(solution)/shard_map/ppermute | solution.py:23
  56.8 4.6 %collective-permute-start.7 = (f32[32,256]{1,0:T(8,128)S(1)}, f32[32,256]{1,0:T(8,128)S(1)}, u32[]{:S(2)}, u32[]{:S(2)}) collective-permute-start(f32[32,256]{1,0:T(8,128)S(1)} %shard_map.96.refs_0_), channel_id=1, source_target_pairs={{0,48},{1,49},{2,50},{3,51},{4,52},{5,53},{6,54},{7,55},{8,56},{9,... | collective-permute-start | bytes 98312 | tf_op jit(solution)/shard_map/ppermute | solution.py:23
  62.8 3.0 %collective-permute-start.11 = (f32[16,4,256]{2,1,0:T(4,128)S(1)}, f32[16,4,256]{2,1,0:T(4,128)S(1)}, u32[]{:S(2)}, u32[]{:S(2)}) collective-permute-start(f32[16,4,256]{2,1,0:T(4,128)S(1)} %shard_map.97.a_ref), channel_id=1, source_target_pairs={{0,1},{1,0},{2,3},{3,2},{4,5},{5,4},{6,7},{7,6},{8,9},{9,8},{10,11... | collective-permute-start | bytes 196616 | tf_op jit(solution)/shard_map/ppermute | solution.py:23

commit v5 on v4

--- a/solution.py
+++ b/solution.py
@@ -54,7 +54,7 @@
     res_ref[...] = jnp.concatenate([x, g], axis=1)
 
 
-def project(layer, acts, out_grads, proj_in, proj_out):
+def project(layer, acts, out_grads, proj_in, proj_out, limit):
     tokens, width = acts.shape[1:]
     hidden = out_grads.shape[2]
     rank = proj_in.shape[1]
@@ -73,7 +73,7 @@
             out_specs=pl.BlockSpec((block, 2 * rank), lambda t, l: (t, 0)),
         ),
         out_shape=jax.ShapeDtypeStruct((tokens, 2 * rank), jnp.float32),
-        compiler_params=pltpu.CompilerParams(vmem_limit_bytes=56 * 2**20),
+        compiler_params=pltpu.CompilerParams(vmem_limit_bytes=limit * 2**20),
         cost_estimate=pl.CostEstimate(
             flops=2 * tokens * (width + hidden) * 256,
             bytes_accessed=tokens * (width + hidden) * 2,
@@ -108,8 +108,11 @@
 
 
 def total_kernel(parts_ref, out):
-    at = 16 * lax.rem(lax.axis_index("y"), 2) + 8 * lax.axis_index("c")
-    out[...] = jnp.sum(parts_ref[pl.ds(at, 8)], axis=0)
+    at = 2 * lax.rem(lax.axis_index("y"), 2) + lax.axis_index("c")
+    total = parts_ref[at]
+    for k in range(1, 8):
+        total = total + parts_ref[at + 4 * k]
+    out[...] = total
 
 
 def half_kernel(parts_ref, out):
@@ -123,12 +126,15 @@
     slots = lax.broadcasted_iota(jnp.int32, w_ref.shape, 1)
     weights = jnp.where(slots < length_ref[y], w_ref[...], 0.0)
     inputs = (total[:, :64].T * weights).reshape(32, 2, -1)
+    right, rest = two_terms(total[:, 64:])
     for odd in range(2):
-        held[:, 64 * odd : 64 * (odd + 1)] = jnp.dot(
-            inputs[:, odd],
-            total[:, 64:],
-            precision=lax.Precision.HIGHEST,
-            preferred_element_type=jnp.float32,
+        high, low = two_terms(inputs[:, odd])
+
+        def dot(left, other):
+            return jnp.dot(left, other, preferred_element_type=jnp.float32)
+
+        held[:, 64 * odd : 64 * (odd + 1)] = dot(high, right) + (
+            dot(low, right) + dot(high, rest)
         )
     for zl in range(4):
         piece = jnp.concatenate(
@@ -186,7 +192,7 @@
     out[...] = jnp.zeros_like(out)
     for block in range(4):
         for zl in range(4):
-            out[8 * zl + 2 * block + here] = a_ref[4 * block + zl] + b_ref[4 * block + zl]
+            out[16 * (block & 1) + 8 * here + 4 * (block >> 1) + zl] = a_ref[4 * block + zl] + b_ref[4 * block + zl]
 
 
 def per_device(
@@ -197,13 +203,13 @@
     proj_out = jnp.swapaxes(proj_out, 1, 2)
     others = (1, 2, 3)
 
-    other = project((1 - c)[None], acts, out_grads, proj_in, proj_out)
+    other = project((1 - c)[None], acts, out_grads, proj_in, proj_out, 57)
     theirs = to_core(other)
     hess = [hess_inv, to_x(hess_inv, 1), to_x(hess_inv, -1)]
     query = [queries, to_x(queries, 1), to_x(queries, -1)]
     hess.append(to_x(hess[1], 1))
     query.append(to_x(query[2], -1))
-    mine = project(c[None], acts, out_grads, proj_in, proj_out)
+    mine = project(c[None], acts, out_grads, proj_in, proj_out, 51)
 
     (blocks,) = call(split_kernel, [(4, 256, 128)], mine, theirs)
     blocks = lax.all_to_all(blocks, "y", 0, 0, tiled=True)
@@ -227,7 +233,7 @@
     images = [image] + [to_zl(image, k) for k in others]
     (parts,) = call(score_kernel, [(16, 4, 256)], *images, *query)
     (parts,) = call(place_kernel, [(32, 4, 256)], parts, to_core(parts))
-    parts = lax.all_to_all(parts, ("zl", "z", "y"), 0, 0, tiled=True)
+    parts = lax.all_to_all(parts, ("y", "z", "zl"), 0, 0, tiled=True)
     (scores,) = call(total_kernel, [(4, 256)], parts)
     return scores
 

time: 83.4 us -> 81.6 us (0.978)
  local copies, waits for them, and re-layouts: 2.78 us -> 1.74 us
    ppermute x12, waiting for transfers between devices: 5.93 us -> 7.63 us  [send(): return lax.ppermute(value, AXES, pairs)]
    all_to_all x1, waiting for transfers between devices: 1.2 us -> 0.01 us  [per_device(): blocks = lax.all_to_all(blocks, 'y', 0, 0, tiled=True)]
    unnamed x10, local copies, waits for them, and re-layouts: 1.05 us -> 0.02 us
  transfers between devices with their start and end apart: 14 -> 14, of which waited for: 6 -> 5; matrix products, arithmetic and copies ran while one was open for 3% -> 3% of each run, Pallas kernels for 9% -> 8%
where the time goes in v5:
time: 81.6 us; the launch traced here: 81.3 us
  starting transfers between devices  36.9 us (45%)
  blocking collectives  15.8 us (19%)
  waiting for transfers between devices  13.2 us (16%)
  Pallas kernels  12.9 us (16%)
  local copies, waits for them, and re-layouts  1.74 us (2%)
    ppermute x12, starting transfers between devices, send(): return lax.ppermute(value, AXES, pairs)  23.4 us
    all_to_all x1, blocking collectives, per_device(): parts = lax.all_to_all(parts, ('y', 'z', 'zl'), 0, 0, tiled=True)  15.8 us
    all_to_all x1, starting transfers between devices, per_device(): grams = lax.all_to_all(grams, ('c', 'zl', 'y'), 0, 0, tiled=True)  9.8 us
    ppermute x12, waiting for transfers between devices, send(): return lax.ppermute(value, AXES, pairs)  7.63 us
    pallas_call x2, Pallas kernels, project(): pl.pallas_call(project_kernel, grid_spec=pltpu.PrefetchScalarGridSpec(num...  7.6 us
    all_to_all x1, waiting for transfers between devices, per_device(): grams = lax.all_to_all(grams, ('c', 'zl', 'y'), 0, 0, tiled=True)  5.56 us
    pallas_call x7, Pallas kernels, call(): pl.pallas_call(kernel, in_specs=specs or [VMEM] * len(args), out_specs=[V...  5.3 us
    all_to_all x1, starting transfers between devices, per_device(): blocks = lax.all_to_all(blocks, 'y', 0, 0, tiled=True)  3.65 us
  transfers between devices with their start and end apart: 14, of which 5 were waited for; matrix products, arithmetic and copies ran while one was open for 3% of the time, Pallas kernels for 8%

profile of v5, /device:TPU:1, one launch (start us, length us, event | category | flops | bytes accessed | tf_op | source)
XLA Modules:
  0.0 81.3 jit_solution(4090241193043224148)
XLA Ops:
  0.0 4.2 %shard_map.92 = f32[1024,128]{1,0:T(8,128)} custom-call(s32[1]{0:T(128)} %bitcast.3.layer_ref, bf16[2,1024,512]{2,1,0:T(8,128)(2,1)} %acts_ref.3, bf16[2,1024,1792]{2,1,0:T(8,128)(2,1)} %grads_ref.3, bf16[2,64,512]{2,1,0:T(8,128)(2,1)} %bitcast.10, bf16[2,64,1792]{2,1,0:T(8,128)(2,1)} %bitcast.8), custom_call_target="tpu_custom_call" | custom-call | flops 1207959552 | bytes 4718592 | tf_op jit(solution)/shard_map/pallas_call | solution.py:62
  4.2 3.2 %collective-permute-start = (f32[1024,128]{1,0:T(8,128)}, f32[1024,128]{1,0:T(8,128)S(1)}, u32[]{:S(2)}, u32[]{:S(2)}) collective-permute-start(f32[1024,128]{1,0:T(8,128)} %shard_map.92), channel_id=1, source_target_pairs={{0,1},{1,0},{2,3},{3,2},{4,5},{5,4},{6,7},{7,6},{8,9},{9,8},{10,11... | collective-permute-start | bytes 1572872 | tf_op jit(solution)/shard_map/ppermute | solution.py:23
  7.5 0.0 copy-start.4
  7.5 3.4 %shard_map.91.a_ref = f32[1024,128]{1,0:T(8,128)S(1)} custom-call(s32[1]{0:T(128)} %bitcast.layer_ref, bf16[2,1024,512]{2,1,0:T(8,128)(2,1)} %acts_ref.3, bf16[2,1024,1792]{2,1,0:T(8,128)(2,1)} %grads_ref.3, bf16[2,64,512]{2,1,0:T(8,128)(2,1)S(1)} %bitcast.11, bf16[2,64,1792]{2,1,0:T(8,128)(2,1)S(1)} %bitcast.9), custom_call_target="tpu_custom_call" | custom-call | flops 1207959552 | bytes 4718592 | tf_op jit(solution)/shard_map/pallas_call | solution.py:62
  10.9 0.0 collective-permute-done.b_ref
  10.9 0.8 %shard_map.93 = f32[4,256,128]{2,1,0:T(8,128)} custom-call(f32[1024,128]{1,0:T(8,128)S(1)} %shard_map.91.a_ref, f32[1024,128]{1,0:T(8,128)S(1)} %collective-permute-done.b_ref), custom_call_target="tpu_custom_call" | custom-call | bytes 3690000 | tf_op jit(solution)/shard_map/pallas_call | solution.py:90
  11.8 3.6 %all-to-all-start = ((f32[4,256,128]{2,1,0:T(8,128)}), f32[4,256,128]{2,1,0:T(8,128)S(1)}, u32[]{:S(2)}, u32[]{:S(2)}) async-start(f32[4,256,128]{2,1,0:T(8,128)} %shard_map.93), calls=%async_computation | async-start | bytes 1048576 | tf_op jit(solution)/shard_map/all_to_all | solution.py:215
  15.4 2.6 %collective-permute-start.3 = (f32[2,256,256]{2,1,0:T(8,128)S(1)}, f32[2,256,256]{2,1,0:T(8,128)S(1)}, u32[]{:S(2)}, u32[]{:S(2)}) collective-permute-start(f32[2,256,256]{2,1,0:T(8,128)S(1)} %copy-done.3), channel_id=1, source_target_pairs={{0,192},{1,193},{2,194},{3,195},{4,196},{5,197},{6,198},{7,199},{8... | collective-permute-start | bytes 1572872 | tf_op jit(solution)/shard_map/ppermute | solution.py:23
  18.0 4.2 %collective-permute-done.2.refs_1_ = f32[2,256,256]{2,1,0:T(8,128)S(1)} collective-permute-done((f32[2,256,256]{2,1,0:T(8,128)S(1)}, f32[2,256,256]{2,1,0:T(8,128)S(1)}, u32[]{:S(2)}, u32[]{:S(2)}) %collective-permute-start.2) | collective-permute-done | bytes 524320 | tf_op jit(solution)/shard_map/ppermute | solution.py:23
  22.2 2.7 %collective-permute-start.9 = (bf16[2,256,256]{2,1,0:T(8,128)(2,1)}, bf16[2,256,256]{2,1,0:T(8,128)(2,1)}, u32[]{:S(2)}, u32[]{:S(2)}) collective-permute-start(bf16[2,256,256]{2,1,0:T(8,128)(2,1)} %refs_4_.1), channel_id=1, source_target_pairs={{0,192},{1,193},{2,194},{3,195},{4,196},{5,197},{6,198},{7,199},{8... | collective-permute-start | bytes 786440 | tf_op jit(solution)/shard_map/ppermute | solution.py:23
  24.8 0.0 all-to-all-done.parts_ref
  24.9 6.5 %collective-permute-start.1 = (f32[256,128]{1,0:T(8,128)S(1)}, f32[256,128]{1,0:T(8,128)S(1)}, u32[]{:S(2)}, u32[]{:S(2)}) collective-permute-start(f32[256,128]{1,0:T(8,128)S(1)} %shard_map.94.a_ref), channel_id=1, source_target_pairs={{0,8},{1,9},{2,10},{3,11},{4,12},{5,13},{6,14},{7,15},{8,0},{9,1},... | collective-permute-start | bytes 393224 | tf_op jit(solution)/shard_map/ppermute | solution.py:23
  31.4 0.7 compare_select_fusion
  32.1 1.7 %gather_fusion = f32[256]{0:T(256)S(1)} fusion(f32[128256]{0:T(1024)S(1)} %copy-done, s32[1024]{0:T(1024)S(1)} %pad_clamp_fusion), kind=kCustom, calls=%fused_computation | custom fusion | bytes 3072 | tf_op jit(solution)/shard_map/gather | solution.py:218
  33.8 0.0 collective-permute-done.1.b_ref
  33.8 1.7 %shard_map.95 = f32[32,8,128]{2,1,0:T(8,128)} custom-call(s32[4]{0:T(128)S(1)} %copy-done.4, f32[256,128]{1,0:T(8,128)S(1)} %shard_map.94.a_ref, f32[256,128]{1,0:T(8,128)S(1)} %collective-permute-done.1.b_ref, f32[1,256]{1,0:T(1,128)S(1)} %bitcast.12), custom_call_target="tpu_custom_call" | custom-call | bytes 3690000 | tf_op jit(solution)/shard_map/pallas_call | solution.py:90
  35.5 9.8 %all-to-all-start.1 = ((f32[32,8,128]{2,1,0:T(8,128)}), f32[32,8,128]{2,1,0:T(8,128)S(1)}, u32[]{:S(2)}, u32[]{:S(2)}) async-start(f32[32,8,128]{2,1,0:T(8,128)} %shard_map.95), calls=%async_computation.1 | async-start | bytes 262144 | tf_op jit(solution)/shard_map/all_to_all | solution.py:231
  45.3 0.6 collective-permute-start.8
  45.9 0.0 collective-permute-done.9.refs_6_
  45.9 2.1 %collective-permute-start.10 = (bf16[2,256,256]{2,1,0:T(8,128)(2,1)}, bf16[2,256,256]{2,1,0:T(8,128)(2,1)S(1)}, u32[]{:S(2)}, u32[]{:S(2)}) collective-permute-start(bf16[2,256,256]{2,1,0:T(8,128)(2,1)} %collective-permute-done.9.refs_6_), channel_id=1, source_target_pairs={{0,192},{1,193},{2,194},{3,195},{4,196},{5,197},{6,198},{7,199},{8... | collective-permute-start | bytes 786440 | tf_op jit(solution)/shard_map/ppermute | solution.py:23
  48.1 5.6 %all-to-all-done.1.rows_ref = f32[32,8,128]{2,1,0:T(8,128)S(1)} async-done(((f32[32,8,128]{2,1,0:T(8,128)}), f32[32,8,128]{2,1,0:T(8,128)S(1)}, u32[]{:S(2)}, u32[]{:S(2)}) %all-to-all-start.1) | async-done | bytes 131104 | tf_op jit(solution)/shard_map/all_to_all | solution.py:231
  53.7 0.7 shard_map.96.refs_0_
  54.4 0.2 collective-permute-start.5
  54.6 1.3 %collective-permute-start.6 = (f32[32,256]{1,0:T(8,128)S(1)}, f32[32,256]{1,0:T(8,128)S(1)}, u32[]{:S(2)}, u32[]{:S(2)}) collective-permute-start(f32[32,256]{1,0:T(8,128)S(1)} %shard_map.96.refs_0_), channel_id=1, source_target_pairs={{0,32},{1,33},{2,34},{3,35},{4,36},{5,37},{6,38},{7,39},{8,40},{9,... | collective-permute-start | bytes 98312 | tf_op jit(solution)/shard_map/ppermute | solution.py:23
  55.9 2.1 %collective-permute-start.7 = (f32[32,256]{1,0:T(8,128)S(1)}, f32[32,256]{1,0:T(8,128)S(1)}, u32[]{:S(2)}, u32[]{:S(2)}) collective-permute-start(f32[32,256]{1,0:T(8,128)S(1)} %shard_map.96.refs_0_), channel_id=1, source_target_pairs={{0,48},{1,49},{2,50},{3,51},{4,52},{5,53},{6,54},{7,55},{8,56},{9,... | collective-permute-start | bytes 98312 | tf_op jit(solution)/shard_map/ppermute | solution.py:23
  57.9 0.3 collective-permute-done.6.refs_2_
  58.3 2.2 %collective-permute-done.7.refs_3_ = f32[32,256]{1,0:T(8,128)S(1)} collective-permute-done((f32[32,256]{1,0:T(8,128)S(1)}, f32[32,256]{1,0:T(8,128)S(1)}, u32[]{:S(2)}, u32[]{:S(2)}) %collective-permute-start.7) | collective-permute-done | bytes 32800 | tf_op jit(solution)/shard_map/ppermute | solution.py:23
  60.4 1.4 %shard_map.97.a_ref = f32[16,4,256]{2,1,0:T(4,128)S(1)} custom-call(f32[32,256]{1,0:T(8,128)S(1)} %shard_map.96.refs_0_, f32[32,256]{1,0:T(8,128)S(1)} %collective-permute-done.5.refs_1_, f32[32,256]{1,0:T(8,128)S(1)} %collective-permute-done.6.refs_2_, f32[32,256]{1,0:T(8,128)S(1)} %collective-permute-done.7.refs_3_, bf16[2,256,256]{2,1,0:T(8,128)(2,1)} %refs_4_.1, ...), custom_call_target="tpu_custom_call" | custom-call | bytes 3690000 | tf_op jit(solution)/shard_map/pallas_call | solution.py:90
  61.9 2.1 %collective-permute-start.11 = (f32[16,4,256]{2,1,0:T(4,128)S(1)}, f32[16,4,256]{2,1,0:T(4,128)S(1)}, u32[]{:S(2)}, u32[]{:S(2)}) collective-permute-start(f32[16,4,256]{2,1,0:T(4,128)S(1)} %shard_map.97.a_ref), channel_id=1, source_target_pairs={{0,1},{1,0},{2,3},{3,2},{4,5},{5,4},{6,7},{7,6},{8,9},{9,8},{10,11... | collective-permute-start | bytes 196616 | tf_op jit(solution)/shard_map/ppermute | solution.py:23
  64.0 0.9 %collective-permute-done.11.b_ref = f32[16,4,256]{2,1,0:T(4,128)S(1)} collective-permute-done((f32[16,4,256]{2,1,0:T(4,128)S(1)}, f32[16,4,256]{2,1,0:T(4,128)S(1)}, u32[]{:S(2)}, u32[]{:S(2)}) %collective-permute-start.11) | collective-permute-done | bytes 65568 | tf_op jit(solution)/shard_map/ppermute | solution.py:23
  64.9 15.8 %all_to_all.15.parts_ref = f32[32,4,256]{2,1,0:T(4,128)S(1)} all-to-all(f32[32,4,256]{2,1,0:T(4,128)S(1)} %shard_map.98), channel_id=1, replica_groups=mesh['x'=4,'zl'=4,'z'=2,'y'=4,'c'=2] {'y','z','zl'}, dimensions={0} | all-to-all | bytes 262144 | tf_op jit(solution)/shard_map/all_to_all | solution.py:236
  80.7 0.6 shard_map.99
  (19 shorter events, 0.1 us)
Async XLA Ops:
  0.0 32.1 %copy-start = (f32[128256]{0:T(1024)S(1)}, f32[128256]{0:T(1024)}, u32[]{:S(2)}) copy-start(f32[128256]{0:T(1024)} %param.13) | copy-start | bytes 1539076
  0.0 7.5 %copy-start.2 = (bf16[2,512,64]{1,2,0:T(8,128)(2,1)S(1)}, bf16[2,512,64]{1,2,0:T(8,128)(2,1)}, u32[]{:S(2)}) copy-start(bf16[2,512,64]{1,2,0:T(8,128)(2,1)} %param.14) | copy-start | bytes 393220
  0.0 7.5 %copy-start.1 = (bf16[2,1792,64]{1,2,0:T(8,128)(2,1)S(1)}, bf16[2,1792,64]{1,2,0:T(8,128)(2,1)}, u32[]{:S(2)}) copy-start(bf16[2,1792,64]{1,2,0:T(8,128)(2,1)} %param.15) | copy-start | bytes 1376260
  0.0 7.5 %copy-start.3 = (f32[2,256,256]{2,1,0:T(8,128)S(1)}, f32[2,256,256]{2,1,0:T(8,128)}, u32[]{:S(2)}) copy-start(f32[2,256,256]{2,1,0:T(8,128)} %refs_0_.1) | copy-start | bytes 1572868
  4.2 6.7 %collective-permute-start = (f32[1024,128]{1,0:T(8,128)}, f32[1024,128]{1,0:T(8,128)S(1)}, u32[]{:S(2)}, u32[]{:S(2)}) collective-permute-start(f32[1024,128]{1,0:T(8,128)} %shard_map.92), channel_id=1, source_target_pairs={{0,1},{1,0},{2,3},{3,2},{4,5},{5,4},{6,7},{7,6},{8,9},{9,8},{10,11... | collective-permute-start | bytes 1572872 | tf_op jit(solution)/shard_map/ppermute | solution.py:23
  7.5 14.7 %collective-permute-start.2 = (f32[2,256,256]{2,1,0:T(8,128)S(1)}, f32[2,256,256]{2,1,0:T(8,128)S(1)}, u32[]{:S(2)}, u32[]{:S(2)}) collective-permute-start(f32[2,256,256]{2,1,0:T(8,128)S(1)} %copy-done.3), channel_id=1, source_target_pairs={{0,64},{1,65},{2,66},{3,67},{4,68},{5,69},{6,70},{7,71},{8,72},{9,... | collective-permute-start | bytes 1572872 | tf_op jit(solution)/shard_map/ppermute | solution.py:23
  7.5 26.4 %copy-start.4 = (s32[4]{0:T(128)S(1)}, s32[4]{0:T(128)}, u32[]{:S(2)}) copy-start(s32[4]{0:T(128)} %length_ref.1) | copy-start | bytes 52
  11.8 13.1 %all-to-all-start = ((f32[4,256,128]{2,1,0:T(8,128)}), f32[4,256,128]{2,1,0:T(8,128)S(1)}, u32[]{:S(2)}, u32[]{:S(2)}) async-start(f32[4,256,128]{2,1,0:T(8,128)} %shard_map.93), calls=%async_computation | async-start | bytes 1048576 | tf_op jit(solution)/shard_map/all_to_all | solution.py:215
  15.4 32.7 %collective-permute-start.3 = (f32[2,256,256]{2,1,0:T(8,128)S(1)}, f32[2,256,256]{2,1,0:T(8,128)S(1)}, u32[]{:S(2)}, u32[]{:S(2)}) collective-permute-start(f32[2,256,256]{2,1,0:T(8,128)S(1)} %copy-done.3), channel_id=1, source_target_pairs={{0,192},{1,193},{2,194},{3,195},{4,196},{5,197},{6,198},{7,199},{8... | collective-permute-start | bytes 1572872 | tf_op jit(solution)/shard_map/ppermute | solution.py:23
  22.2 25.9 %collective-permute-start.4 = (f32[2,256,256]{2,1,0:T(8,128)S(1)}, f32[2,256,256]{2,1,0:T(8,128)S(1)}, u32[]{:S(2)}, u32[]{:S(2)}) collective-permute-start(f32[2,256,256]{2,1,0:T(8,128)S(1)} %collective-permute-done.2.refs_1_), channel_id=1, source_target_pairs={{0,64},{1,65},{2,66},{3,67},{4,68},{5,69},{6,70},{7,71},{8,72},{9,... | collective-permute-start | bytes 1572872 | tf_op jit(solution)/shard_map/ppermute | solution.py:23
  22.2 23.8 %collective-permute-start.9 = (bf16[2,256,256]{2,1,0:T(8,128)(2,1)}, bf16[2,256,256]{2,1,0:T(8,128)(2,1)}, u32[]{:S(2)}, u32[]{:S(2)}) collective-permute-start(bf16[2,256,256]{2,1,0:T(8,128)(2,1)} %refs_4_.1), channel_id=1, source_target_pairs={{0,192},{1,193},{2,194},{3,195},{4,196},{5,197},{6,198},{7,199},{8... | collective-permute-start | bytes 786440 | tf_op jit(solution)/shard_map/ppermute | solution.py:23
  24.9 9.0 %collective-permute-start.1 = (f32[256,128]{1,0:T(8,128)S(1)}, f32[256,128]{1,0:T(8,128)S(1)}, u32[]{:S(2)}, u32[]{:S(2)}) collective-permute-start(f32[256,128]{1,0:T(8,128)S(1)} %shard_map.94.a_ref), channel_id=1, source_target_pairs={{0,8},{1,9},{2,10},{3,11},{4,12},{5,13},{6,14},{7,15},{8,0},{9,1},... | collective-permute-start | bytes 393224 | tf_op jit(solution)/shard_map/ppermute | solution.py:23
  35.5 18.1 %all-to-all-start.1 = ((f32[32,8,128]{2,1,0:T(8,128)}), f32[32,8,128]{2,1,0:T(8,128)S(1)}, u32[]{:S(2)}, u32[]{:S(2)}) async-start(f32[32,8,128]{2,1,0:T(8,128)} %shard_map.95), calls=%async_computation.1 | async-start | bytes 262144 | tf_op jit(solution)/shard_map/all_to_all | solution.py:231
  45.3 12.6 %collective-permute-start.8 = (bf16[2,256,256]{2,1,0:T(8,128)(2,1)}, bf16[2,256,256]{2,1,0:T(8,128)(2,1)S(1)}, u32[]{:S(2)}, u32[]{:S(2)}) collective-permute-start(bf16[2,256,256]{2,1,0:T(8,128)(2,1)} %refs_4_.1), channel_id=1, source_target_pairs={{0,64},{1,65},{2,66},{3,67},{4,68},{5,69},{6,70},{7,71},{8,72},{9,... | collective-permute-start | bytes 786440 | tf_op jit(solution)/shard_map/ppermute | solution.py:23
  45.9 12.0 %collective-permute-start.10 = (bf16[2,256,256]{2,1,0:T(8,128)(2,1)}, bf16[2,256,256]{2,1,0:T(8,128)(2,1)S(1)}, u32[]{:S(2)}, u32[]{:S(2)}) collective-permute-start(bf16[2,256,256]{2,1,0:T(8,128)(2,1)} %collective-permute-done.9.refs_6_), channel_id=1, source_target_pairs={{0,192},{1,193},{2,194},{3,195},{4,196},{5,197},{6,198},{7,199},{8... | collective-permute-start | bytes 786440 | tf_op jit(solution)/shard_map/ppermute | solution.py:23
  54.4 3.6 %collective-permute-start.5 = (f32[32,256]{1,0:T(8,128)S(1)}, f32[32,256]{1,0:T(8,128)S(1)}, u32[]{:S(2)}, u32[]{:S(2)}) collective-permute-start(f32[32,256]{1,0:T(8,128)S(1)} %shard_map.96.refs_0_), channel_id=1, source_target_pairs={{0,16},{1,17},{2,18},{3,19},{4,20},{5,21},{6,22},{7,23},{8,24},{9,... | collective-permute-start | bytes 98312 | tf_op jit(solution)/shard_map/ppermute | solution.py:23
  54.6 3.7 %collective-permute-start.6 = (f32[32,256]{1,0:T(8,128)S(1)}, f32[32,256]{1,0:T(8,128)S(1)}, u32[]{:S(2)}, u32[]{:S(2)}) collective-permute-start(f32[32,256]{1,0:T(8,128)S(1)} %shard_map.96.refs_0_), channel_id=1, source_target_pairs={{0,32},{1,33},{2,34},{3,35},{4,36},{5,37},{6,38},{7,39},{8,40},{9,... | collective-permute-start | bytes 98312 | tf_op jit(solution)/shard_map/ppermute | solution.py:23
  55.9 4.6 %collective-permute-start.7 = (f32[32,256]{1,0:T(8,128)S(1)}, f32[32,256]{1,0:T(8,128)S(1)}, u32[]{:S(2)}, u32[]{:S(2)}) collective-permute-start(f32[32,256]{1,0:T(8,128)S(1)} %shard_map.96.refs_0_), channel_id=1, source_target_pairs={{0,48},{1,49},{2,50},{3,51},{4,52},{5,53},{6,54},{7,55},{8,56},{9,... | collective-permute-start | bytes 98312 | tf_op jit(solution)/shard_map/ppermute | solution.py:23
  61.9 3.0 %collective-permute-start.11 = (f32[16,4,256]{2,1,0:T(4,128)S(1)}, f32[16,4,256]{2,1,0:T(4,128)S(1)}, u32[]{:S(2)}, u32[]{:S(2)}) collective-permute-start(f32[16,4,256]{2,1,0:T(4,128)S(1)} %shard_map.97.a_ref), channel_id=1, source_target_pairs={{0,1},{1,0},{2,3},{3,2},{4,5},{5,4},{6,7},{7,6},{8,9},{9,8},{10,11... | collective-permute-start | bytes 196616 | tf_op jit(solution)/shard_map/ppermute | solution.py:23

commit v6 on v5

--- a/solution.py
+++ b/solution.py
@@ -207,9 +207,9 @@
     theirs = to_core(other)
     hess = [hess_inv, to_x(hess_inv, 1), to_x(hess_inv, -1)]
     query = [queries, to_x(queries, 1), to_x(queries, -1)]
-    hess.append(to_x(hess[1], 1))
-    query.append(to_x(query[2], -1))
-    mine = project(c[None], acts, out_grads, proj_in, proj_out, 51)
+    hess.append(to_x(hess_inv, 2))
+    query.append(to_x(queries, 2))
+    mine = project(c[None], acts, out_grads, proj_in, proj_out, 48)
 
     (blocks,) = call(split_kernel, [(4, 256, 128)], mine, theirs)
     blocks = lax.all_to_all(blocks, "y", 0, 0, tiled=True)

time: 81.6 us -> 81.3 us (level)
  starting transfers between devices: 36.9 us -> 35 us
  local copies, waits for them, and re-layouts: 1.74 us -> 2.79 us
    ppermute x12, waiting for transfers between devices: 7.63 us -> 3.45 us  [send(): return lax.ppermute(value, AXES, pairs)]
    all_to_all x1, waiting for transfers between devices: 0.01 us -> 3.82 us  [per_device(): blocks = lax.all_to_all(blocks, 'y', 0, 0, tiled=True)]
    unnamed x10 -> x14, local copies, waits for them, and re-layouts: 0.02 us -> 1.06 us
    all_to_all x1, starting transfers between devices: 9.8 us -> 8.85 us  [per_device(): grams = lax.all_to_all(grams, ('c', 'zl', 'y'), 0, 0, tiled=True)]
  transfers between devices with their start and end apart: 14 -> 14, of which waited for: 5 -> 5; matrix products, arithmetic and copies ran while one was open for 3% -> 3% of each run, Pallas kernels for 8% -> 7%
where the time goes in v6:
time: 81.3 us; the launch traced here: 80.4 us
  starting transfers between devices  35 us (43%)
  blocking collectives  15.9 us (20%)
  Pallas kernels  13 us (16%)
  waiting for transfers between devices  12.8 us (16%)
  local copies, waits for them, and re-layouts  2.79 us (3%)
    ppermute x12, starting transfers between devices, send(): return lax.ppermute(value, AXES, pairs)  22.7 us
    all_to_all x1, blocking collectives, per_device(): parts = lax.all_to_all(parts, ('y', 'z', 'zl'), 0, 0, tiled=True)  15.9 us
    all_to_all x1, starting transfers between devices, per_device(): grams = lax.all_to_all(grams, ('c', 'zl', 'y'), 0, 0, tiled=True)  8.85 us
    pallas_call x2, Pallas kernels, project(): pl.pallas_call(project_kernel, grid_spec=pltpu.PrefetchScalarGridSpec(num...  7.75 us
    all_to_all x1, waiting for transfers between devices, per_device(): grams = lax.all_to_all(grams, ('c', 'zl', 'y'), 0, 0, tiled=True)  5.56 us
    pallas_call x7, Pallas kernels, call(): pl.pallas_call(kernel, in_specs=specs or [VMEM] * len(args), out_specs=[V...  5.26 us
    all_to_all x1, waiting for transfers between devices, per_device(): blocks = lax.all_to_all(blocks, 'y', 0, 0, tiled=True)  3.82 us
    all_to_all x1, starting transfers between devices, per_device(): blocks = lax.all_to_all(blocks, 'y', 0, 0, tiled=True)  3.47 us
  transfers between devices with their start and end apart: 14, of which 5 were waited for; matrix products, arithmetic and copies ran while one was open for 3% of the time, Pallas kernels for 7%

profile of v6, /device:TPU:1, one launch (start us, length us, event | category | flops | bytes accessed | tf_op | source)
XLA Modules:
  0.0 80.4 jit_solution(17310443929838170030)
XLA Ops:
  0.0 4.5 %shard_map.92 = f32[1024,128]{1,0:T(8,128)} custom-call(s32[1]{0:T(128)} %bitcast.3.layer_ref, bf16[2,1024,512]{2,1,0:T(8,128)(2,1)} %acts_ref.3, bf16[2,1024,1792]{2,1,0:T(8,128)(2,1)} %grads_ref.3, bf16[2,64,512]{2,1,0:T(8,128)(2,1)} %bitcast.10, bf16[2,64,1792]{2,1,0:T(8,128)(2,1)} %bitcast.8), custom_call_target="tpu_custom_call" | custom-call | flops 1207959552 | bytes 4718592 | tf_op jit(solution)/shard_map/pallas_call | solution.py:62
  4.6 2.9 %collective-permute-start = (f32[1024,128]{1,0:T(8,128)}, f32[1024,128]{1,0:T(8,128)S(1)}, u32[]{:S(2)}, u32[]{:S(2)}) collective-permute-start(f32[1024,128]{1,0:T(8,128)} %shard_map.92), channel_id=1, source_target_pairs={{0,1},{1,0},{2,3},{3,2},{4,5},{5,4},{6,7},{7,6},{8,9},{9,8},{10,11... | collective-permute-start | bytes 1572872 | tf_op jit(solution)/shard_map/ppermute | solution.py:23
  7.5 3.2 %shard_map.91.a_ref = f32[1024,128]{1,0:T(8,128)S(1)} custom-call(s32[1]{0:T(128)} %bitcast.layer_ref, bf16[2,1024,512]{2,1,0:T(8,128)(2,1)S(1)} %copy-done.1, bf16[2,1024,1792]{2,1,0:T(8,128)(2,1)} %grads_ref.3, bf16[2,64,512]{2,1,0:T(8,128)(2,1)S(1)} %bitcast.11, bf16[2,64,1792]{2,1,0:T(8,128)(2,1)S(1)} %bitcast.9), custom_call_target="tpu_custom_call" | custom-call | flops 1207959552 | bytes 4718592 | tf_op jit(solution)/shard_map/pallas_call | solution.py:62
  10.7 0.0 collective-permute-done.b_ref
  10.7 0.9 %shard_map.93 = f32[4,256,128]{2,1,0:T(8,128)} custom-call(f32[1024,128]{1,0:T(8,128)S(1)} %shard_map.91.a_ref, f32[1024,128]{1,0:T(8,128)S(1)} %collective-permute-done.b_ref), custom_call_target="tpu_custom_call" | custom-call | bytes 3690000 | tf_op jit(solution)/shard_map/pallas_call | solution.py:90
  11.6 3.5 %all-to-all-start = ((f32[4,256,128]{2,1,0:T(8,128)}), f32[4,256,128]{2,1,0:T(8,128)S(1)}, u32[]{:S(2)}, u32[]{:S(2)}) async-start(f32[4,256,128]{2,1,0:T(8,128)} %shard_map.93), calls=%async_computation | async-start | bytes 1048576 | tf_op jit(solution)/shard_map/all_to_all | solution.py:215
  15.1 0.2 collective-permute-start.2
  15.3 2.6 %collective-permute-start.3 = (f32[2,256,256]{2,1,0:T(8,128)}, f32[2,256,256]{2,1,0:T(8,128)S(1)}, u32[]{:S(2)}, u32[]{:S(2)}) collective-permute-start(f32[2,256,256]{2,1,0:T(8,128)} %refs_0_.1), channel_id=1, source_target_pairs={{0,192},{1,193},{2,194},{3,195},{4,196},{5,197},{6,198},{7,199},{8... | collective-permute-start | bytes 1572872 | tf_op jit(solution)/shard_map/ppermute | solution.py:23
  17.9 0.4 collective-permute-start.4
  18.3 2.5 %collective-permute-start.10 = (bf16[2,256,256]{2,1,0:T(8,128)(2,1)S(1)}, bf16[2,256,256]{2,1,0:T(8,128)(2,1)S(1)}, u32[]{:S(2)}, u32[]{:S(2)}) collective-permute-start(bf16[2,256,256]{2,1,0:T(8,128)(2,1)S(1)} %copy-done.5), channel_id=1, source_target_pairs={{0,128},{1,129},{2,130},{3,131},{4,132},{5,133},{6,134},{7,135},{8... | collective-permute-start | bytes 786440 | tf_op jit(solution)/shard_map/ppermute | solution.py:23
  20.8 3.8 %all-to-all-done.parts_ref = f32[4,256,128]{2,1,0:T(8,128)S(1)} async-done(((f32[4,256,128]{2,1,0:T(8,128)}), f32[4,256,128]{2,1,0:T(8,128)S(1)}, u32[]{:S(2)}, u32[]{:S(2)}) %all-to-all-start) | async-done | bytes 524320 | tf_op jit(solution)/shard_map/all_to_all | solution.py:215
  24.7 5.6 %collective-permute-start.1 = (f32[256,128]{1,0:T(8,128)S(1)}, f32[256,128]{1,0:T(8,128)S(1)}, u32[]{:S(2)}, u32[]{:S(2)}) collective-permute-start(f32[256,128]{1,0:T(8,128)S(1)} %shard_map.94.a_ref), channel_id=1, source_target_pairs={{0,8},{1,9},{2,10},{3,11},{4,12},{5,13},{6,14},{7,15},{8,0},{9,1},... | collective-permute-start | bytes 393224 | tf_op jit(solution)/shard_map/ppermute | solution.py:23
  30.3 0.7 compare_select_fusion
  31.0 1.7 %gather_fusion = f32[256]{0:T(256)S(1)} fusion(f32[128256]{0:T(1024)S(1)} %copy-done, s32[1024]{0:T(1024)S(1)} %pad_clamp_fusion), kind=kCustom, calls=%fused_computation | custom fusion | bytes 3072 | tf_op jit(solution)/shard_map/gather | solution.py:218
  32.7 0.0 collective-permute-done.1.b_ref
  32.7 1.7 %shard_map.95 = f32[32,8,128]{2,1,0:T(8,128)} custom-call(s32[4]{0:T(128)S(1)} %copy-done.6, f32[256,128]{1,0:T(8,128)S(1)} %shard_map.94.a_ref, f32[256,128]{1,0:T(8,128)S(1)} %collective-permute-done.1.b_ref, f32[1,256]{1,0:T(1,128)S(1)} %bitcast.12), custom_call_target="tpu_custom_call" | custom-call | bytes 3690000 | tf_op jit(solution)/shard_map/pallas_call | solution.py:90
  34.4 8.9 %all-to-all-start.1 = ((f32[32,8,128]{2,1,0:T(8,128)}), f32[32,8,128]{2,1,0:T(8,128)S(1)}, u32[]{:S(2)}, u32[]{:S(2)}) async-start(f32[32,8,128]{2,1,0:T(8,128)} %shard_map.95), calls=%async_computation.1 | async-start | bytes 262144 | tf_op jit(solution)/shard_map/all_to_all | solution.py:231
  43.3 1.3 %collective-permute-start.8 = (bf16[2,256,256]{2,1,0:T(8,128)(2,1)S(1)}, bf16[2,256,256]{2,1,0:T(8,128)(2,1)S(1)}, u32[]{:S(2)}, u32[]{:S(2)}) collective-permute-start(bf16[2,256,256]{2,1,0:T(8,128)(2,1)S(1)} %copy-done.5), channel_id=1, source_target_pairs={{0,64},{1,65},{2,66},{3,67},{4,68},{5,69},{6,70},{7,71},{8,72},{9,... | collective-permute-start | bytes 786440 | tf_op jit(solution)/shard_map/ppermute | solution.py:23
  44.6 1.5 %collective-permute-start.9 = (bf16[2,256,256]{2,1,0:T(8,128)(2,1)S(1)}, bf16[2,256,256]{2,1,0:T(8,128)(2,1)}, u32[]{:S(2)}, u32[]{:S(2)}) collective-permute-start(bf16[2,256,256]{2,1,0:T(8,128)(2,1)S(1)} %copy-done.5), channel_id=1, source_target_pairs={{0,192},{1,193},{2,194},{3,195},{4,196},{5,197},{6,198},{7,199},{8... | collective-permute-start | bytes 786440 | tf_op jit(solution)/shard_map/ppermute | solution.py:23
  46.1 5.6 %all-to-all-done.1.rows_ref = f32[32,8,128]{2,1,0:T(8,128)S(1)} async-done(((f32[32,8,128]{2,1,0:T(8,128)}), f32[32,8,128]{2,1,0:T(8,128)S(1)}, u32[]{:S(2)}, u32[]{:S(2)}) %all-to-all-start.1) | async-done | bytes 131104 | tf_op jit(solution)/shard_map/all_to_all | solution.py:231
  51.6 1.0 %copy-done.4 = f32[2,256,256]{2,1,0:T(8,128)S(1)} copy-done((f32[2,256,256]{2,1,0:T(8,128)S(1)}, f32[2,256,256]{2,1,0:T(8,128)}, u32[]{:S(2)}) %copy-start.4) | copy-done | bytes 524312
  52.7 0.7 shard_map.96.refs_0_
  53.3 0.2 collective-permute-start.5
  53.6 1.3 %collective-permute-start.6 = (f32[32,256]{1,0:T(8,128)S(1)}, f32[32,256]{1,0:T(8,128)S(1)}, u32[]{:S(2)}, u32[]{:S(2)}) collective-permute-start(f32[32,256]{1,0:T(8,128)S(1)} %shard_map.96.refs_0_), channel_id=1, source_target_pairs={{0,32},{1,33},{2,34},{3,35},{4,36},{5,37},{6,38},{7,39},{8,40},{9,... | collective-permute-start | bytes 98312 | tf_op jit(solution)/shard_map/ppermute | solution.py:23
  54.9 2.1 %collective-permute-start.7 = (f32[32,256]{1,0:T(8,128)S(1)}, f32[32,256]{1,0:T(8,128)S(1)}, u32[]{:S(2)}, u32[]{:S(2)}) collective-permute-start(f32[32,256]{1,0:T(8,128)S(1)} %shard_map.96.refs_0_), channel_id=1, source_target_pairs={{0,48},{1,49},{2,50},{3,51},{4,52},{5,53},{6,54},{7,55},{8,56},{9,... | collective-permute-start | bytes 98312 | tf_op jit(solution)/shard_map/ppermute | solution.py:23
  56.9 0.3 collective-permute-done.6.refs_2_
  57.3 2.2 %collective-permute-done.7.refs_3_ = f32[32,256]{1,0:T(8,128)S(1)} collective-permute-done((f32[32,256]{1,0:T(8,128)S(1)}, f32[32,256]{1,0:T(8,128)S(1)}, u32[]{:S(2)}, u32[]{:S(2)}) %collective-permute-start.7) | collective-permute-done | bytes 32800 | tf_op jit(solution)/shard_map/ppermute | solution.py:23
  59.4 1.3 %shard_map.97.a_ref = f32[16,4,256]{2,1,0:T(4,128)S(1)} custom-call(f32[32,256]{1,0:T(8,128)S(1)} %shard_map.96.refs_0_, f32[32,256]{1,0:T(8,128)S(1)} %collective-permute-done.5.refs_1_, f32[32,256]{1,0:T(8,128)S(1)} %collective-permute-done.6.refs_2_, f32[32,256]{1,0:T(8,128)S(1)} %collective-permute-done.7.refs_3_, bf16[2,256,256]{2,1,0:T(8,128)(2,1)S(1)} %copy-done.5, ...), custom_call_target="tpu_custom_call" | custom-call | bytes 3690000 | tf_op jit(solution)/shard_map/pallas_call | solution.py:90
  60.8 2.1 %collective-permute-start.11 = (f32[16,4,256]{2,1,0:T(4,128)S(1)}, f32[16,4,256]{2,1,0:T(4,128)S(1)}, u32[]{:S(2)}, u32[]{:S(2)}) collective-permute-start(f32[16,4,256]{2,1,0:T(4,128)S(1)} %shard_map.97.a_ref), channel_id=1, source_target_pairs={{0,1},{1,0},{2,3},{3,2},{4,5},{5,4},{6,7},{7,6},{8,9},{9,8},{10,11... | collective-permute-start | bytes 196616 | tf_op jit(solution)/shard_map/ppermute | solution.py:23
  62.9 0.9 %collective-permute-done.11.b_ref = f32[16,4,256]{2,1,0:T(4,128)S(1)} collective-permute-done((f32[16,4,256]{2,1,0:T(4,128)S(1)}, f32[16,4,256]{2,1,0:T(4,128)S(1)}, u32[]{:S(2)}, u32[]{:S(2)}) %collective-permute-start.11) | collective-permute-done | bytes 65568 | tf_op jit(solution)/shard_map/ppermute | solution.py:23
  63.8 15.9 %all_to_all.15.parts_ref = f32[32,4,256]{2,1,0:T(4,128)S(1)} all-to-all(f32[32,4,256]{2,1,0:T(4,128)S(1)} %shard_map.98), channel_id=1, replica_groups=mesh['x'=4,'zl'=4,'z'=2,'y'=4,'c'=2] {'y','z','zl'}, dimensions={0} | all-to-all | bytes 262144 | tf_op jit(solution)/shard_map/all_to_all | solution.py:236
  79.8 0.6 shard_map.99
  (23 shorter events, 0.1 us)
Async XLA Ops:
  0.0 31.0 %copy-start = (f32[128256]{0:T(1024)S(1)}, f32[128256]{0:T(1024)}, u32[]{:S(2)}) copy-start(f32[128256]{0:T(1024)} %param.13) | copy-start | bytes 1539076
  0.0 7.5 %copy-start.3 = (bf16[2,512,64]{1,2,0:T(8,128)(2,1)S(1)}, bf16[2,512,64]{1,2,0:T(8,128)(2,1)}, u32[]{:S(2)}) copy-start(bf16[2,512,64]{1,2,0:T(8,128)(2,1)} %param.14) | copy-start | bytes 393220
  0.0 7.5 %copy-start.2 = (bf16[2,1792,64]{1,2,0:T(8,128)(2,1)S(1)}, bf16[2,1792,64]{1,2,0:T(8,128)(2,1)}, u32[]{:S(2)}) copy-start(bf16[2,1792,64]{1,2,0:T(8,128)(2,1)} %param.15) | copy-start | bytes 1376260
  0.0 7.5 %copy-start.1 = (bf16[2,1024,512]{2,1,0:T(8,128)(2,1)S(1)}, bf16[2,1024,512]{2,1,0:T(8,128)(2,1)}, u32[]{:S(2)}) copy-start(bf16[2,1024,512]{2,1,0:T(8,128)(2,1)} %acts_ref.3) | copy-start | bytes 6291460
  4.6 13.7 %copy-start.5 = (bf16[2,256,256]{2,1,0:T(8,128)(2,1)S(1)}, bf16[2,256,256]{2,1,0:T(8,128)(2,1)}, u32[]{:S(2)}) copy-start(bf16[2,256,256]{2,1,0:T(8,128)(2,1)} %refs_4_.1) | copy-start | bytes 786436
  4.6 6.2 %collective-permute-start = (f32[1024,128]{1,0:T(8,128)}, f32[1024,128]{1,0:T(8,128)S(1)}, u32[]{:S(2)}, u32[]{:S(2)}) collective-permute-start(f32[1024,128]{1,0:T(8,128)} %shard_map.92), channel_id=1, source_target_pairs={{0,1},{1,0},{2,3},{3,2},{4,5},{5,4},{6,7},{7,6},{8,9},{9,8},{10,11... | collective-permute-start | bytes 1572872 | tf_op jit(solution)/shard_map/ppermute | solution.py:23
  7.5 25.2 %copy-start.6 = (s32[4]{0:T(128)S(1)}, s32[4]{0:T(128)}, u32[]{:S(2)}) copy-start(s32[4]{0:T(128)} %length_ref.1) | copy-start | bytes 52
  11.6 13.0 %all-to-all-start = ((f32[4,256,128]{2,1,0:T(8,128)}), f32[4,256,128]{2,1,0:T(8,128)S(1)}, u32[]{:S(2)}, u32[]{:S(2)}) async-start(f32[4,256,128]{2,1,0:T(8,128)} %shard_map.93), calls=%async_computation | async-start | bytes 1048576 | tf_op jit(solution)/shard_map/all_to_all | solution.py:215
  15.1 29.5 %collective-permute-start.2 = (f32[2,256,256]{2,1,0:T(8,128)}, f32[2,256,256]{2,1,0:T(8,128)S(1)}, u32[]{:S(2)}, u32[]{:S(2)}) collective-permute-start(f32[2,256,256]{2,1,0:T(8,128)} %refs_0_.1), channel_id=1, source_target_pairs={{0,64},{1,65},{2,66},{3,67},{4,68},{5,69},{6,70},{7,71},{8,72},{9,... | collective-permute-start | bytes 1572872 | tf_op jit(solution)/shard_map/ppermute | solution.py:23
  15.3 30.7 %collective-permute-start.3 = (f32[2,256,256]{2,1,0:T(8,128)}, f32[2,256,256]{2,1,0:T(8,128)S(1)}, u32[]{:S(2)}, u32[]{:S(2)}) collective-permute-start(f32[2,256,256]{2,1,0:T(8,128)} %refs_0_.1), channel_id=1, source_target_pairs={{0,192},{1,193},{2,194},{3,195},{4,196},{5,197},{6,198},{7,199},{8... | collective-permute-start | bytes 1572872 | tf_op jit(solution)/shard_map/ppermute | solution.py:23
  17.9 28.2 %collective-permute-start.4 = (f32[2,256,256]{2,1,0:T(8,128)}, f32[2,256,256]{2,1,0:T(8,128)S(1)}, u32[]{:S(2)}, u32[]{:S(2)}) collective-permute-start(f32[2,256,256]{2,1,0:T(8,128)} %refs_0_.1), channel_id=1, source_target_pairs={{0,128},{1,129},{2,130},{3,131},{4,132},{5,133},{6,134},{7,135},{8... | collective-permute-start | bytes 1572872 | tf_op jit(solution)/shard_map/ppermute | solution.py:23
  18.3 36.6 %collective-permute-start.10 = (bf16[2,256,256]{2,1,0:T(8,128)(2,1)S(1)}, bf16[2,256,256]{2,1,0:T(8,128)(2,1)S(1)}, u32[]{:S(2)}, u32[]{:S(2)}) collective-permute-start(bf16[2,256,256]{2,1,0:T(8,128)(2,1)S(1)} %copy-done.5), channel_id=1, source_target_pairs={{0,128},{1,129},{2,130},{3,131},{4,132},{5,133},{6,134},{7,135},{8... | collective-permute-start | bytes 786440 | tf_op jit(solution)/shard_map/ppermute | solution.py:23
  24.7 8.0 %collective-permute-start.1 = (f32[256,128]{1,0:T(8,128)S(1)}, f32[256,128]{1,0:T(8,128)S(1)}, u32[]{:S(2)}, u32[]{:S(2)}) collective-permute-start(f32[256,128]{1,0:T(8,128)S(1)} %shard_map.94.a_ref), channel_id=1, source_target_pairs={{0,8},{1,9},{2,10},{3,11},{4,12},{5,13},{6,14},{7,15},{8,0},{9,1},... | collective-permute-start | bytes 393224 | tf_op jit(solution)/shard_map/ppermute | solution.py:23
  34.4 17.2 %all-to-all-start.1 = ((f32[32,8,128]{2,1,0:T(8,128)}), f32[32,8,128]{2,1,0:T(8,128)S(1)}, u32[]{:S(2)}, u32[]{:S(2)}) async-start(f32[32,8,128]{2,1,0:T(8,128)} %shard_map.95), calls=%async_computation.1 | async-start | bytes 262144 | tf_op jit(solution)/shard_map/all_to_all | solution.py:231
  43.3 13.6 %collective-permute-start.8 = (bf16[2,256,256]{2,1,0:T(8,128)(2,1)S(1)}, bf16[2,256,256]{2,1,0:T(8,128)(2,1)S(1)}, u32[]{:S(2)}, u32[]{:S(2)}) collective-permute-start(bf16[2,256,256]{2,1,0:T(8,128)(2,1)S(1)} %copy-done.5), channel_id=1, source_target_pairs={{0,64},{1,65},{2,66},{3,67},{4,68},{5,69},{6,70},{7,71},{8,72},{9,... | collective-permute-start | bytes 786440 | tf_op jit(solution)/shard_map/ppermute | solution.py:23
  44.6 12.3 %collective-permute-start.9 = (bf16[2,256,256]{2,1,0:T(8,128)(2,1)S(1)}, bf16[2,256,256]{2,1,0:T(8,128)(2,1)}, u32[]{:S(2)}, u32[]{:S(2)}) collective-permute-start(bf16[2,256,256]{2,1,0:T(8,128)(2,1)S(1)} %copy-done.5), channel_id=1, source_target_pairs={{0,192},{1,193},{2,194},{3,195},{4,196},{5,197},{6,198},{7,199},{8... | collective-permute-start | bytes 786440 | tf_op jit(solution)/shard_map/ppermute | solution.py:23
  51.6 1.0 %copy-start.4 = (f32[2,256,256]{2,1,0:T(8,128)S(1)}, f32[2,256,256]{2,1,0:T(8,128)}, u32[]{:S(2)}) copy-start(f32[2,256,256]{2,1,0:T(8,128)} %refs_0_.1) | copy-start | bytes 1572868
  53.3 3.6 %collective-permute-start.5 = (f32[32,256]{1,0:T(8,128)S(1)}, f32[32,256]{1,0:T(8,128)S(1)}, u32[]{:S(2)}, u32[]{:S(2)}) collective-permute-start(f32[32,256]{1,0:T(8,128)S(1)} %shard_map.96.refs_0_), channel_id=1, source_target_pairs={{0,16},{1,17},{2,18},{3,19},{4,20},{5,21},{6,22},{7,23},{8,24},{9,... | collective-permute-start | bytes 98312 | tf_op jit(solution)/shard_map/ppermute | solution.py:23
  53.6 3.7 %collective-permute-start.6 = (f32[32,256]{1,0:T(8,128)S(1)}, f32[32,256]{1,0:T(8,128)S(1)}, u32[]{:S(2)}, u32[]{:S(2)}) collective-permute-start(f32[32,256]{1,0:T(8,128)S(1)} %shard_map.96.refs_0_), channel_id=1, source_target_pairs={{0,32},{1,33},{2,34},{3,35},{4,36},{5,37},{6,38},{7,39},{8,40},{9,... | collective-permute-start | bytes 98312 | tf_op jit(solution)/shard_map/ppermute | solution.py:23
  54.9 4.6 %collective-permute-start.7 = (f32[32,256]{1,0:T(8,128)S(1)}, f32[32,256]{1,0:T(8,128)S(1)}, u32[]{:S(2)}, u32[]{:S(2)}) collective-permute-start(f32[32,256]{1,0:T(8,128)S(1)} %shard_map.96.refs_0_), channel_id=1, source_target_pairs={{0,48},{1,49},{2,50},{3,51},{4,52},{5,53},{6,54},{7,55},{8,56},{9,... | collective-permute-start | bytes 98312 | tf_op jit(solution)/shard_map/ppermute | solution.py:23
  60.8 3.0 %collective-permute-start.11 = (f32[16,4,256]{2,1,0:T(4,128)S(1)}, f32[16,4,256]{2,1,0:T(4,128)S(1)}, u32[]{:S(2)}, u32[]{:S(2)}) collective-permute-start(f32[16,4,256]{2,1,0:T(4,128)S(1)} %shard_map.97.a_ref), channel_id=1, source_target_pairs={{0,1},{1,0},{2,3},{3,2},{4,5},{5,4},{6,7},{7,6},{8,9},{9,8},{10,11... | collective-permute-start | bytes 196616 | tf_op jit(solution)/shard_map/ppermute | solution.py:23
